TPU v7x, 512 devices: a whole 4x4x16 slice. The times are simulated.
512 devices in a mesh: dp: 8 (over y, core), tensor: 64 (over x, z).
Axes of the slice: x: 4, y: 4, z: 16, core: 2. Of those that a mesh axis runs over, the one named last changes fastest.
Arguments:
- tokens: bfloat16 [1024, 8192], P('dp', 'tensor'), may hold values from -6 to 6
- grad_out: bfloat16 [1024, 8192], P('dp', 'tensor'), may hold values from -6 to 6
- up_weight: bfloat16 [64, 128, 4096], P('tensor', 'dp'), may hold values from -0.125 to 0.125
- down_weight: bfloat16 [64, 128, 4096], P('tensor', 'dp'), may hold values from -0.125 to 0.125
- up_local: int32 [64, 128], P('tensor'), may hold values from 0 to 3, as said below
- up_col: int32 [64, 128], P('tensor'), may hold values from 0 to 127, as said below
- down_local: int32 [64, 128], P('tensor'), may hold values from 0 to 3, as said below
- down_col: int32 [64, 128], P('tensor'), may hold values from 0 to 127, as said below
- up_perm: int32 [256], replicated, may hold values from 0 to 255, each once
- down_perm: int32 [256], replicated, may hold values from 0 to 255, each once
Outputs:
- grad_tokens: bfloat16 [1024, 8192], P('dp', 'tensor')
- grad_up: bfloat16 [64, 128, 4096], P('tensor')
- grad_down: bfloat16 [64, 128, 4096], P('tensor')
Inputs may be any that keep to these rules, and one draw needn't show every extreme that they name: `up_local`: for each owner, slots of one hidden block stand together, blocks in rising order, each of its 4 blocks with one slot or more. `up_col`: input blocks of one hidden block are distinct. `down_local`: for each owner, slots of one hidden block stand together, blocks in rising order, each of its 4 blocks with one slot or more. `down_col`: output blocks of one hidden block are distinct.
All inputs are finite; a program needn't handle non-finite values.
Results may differ from a plain program's by a relative error of at most 0.017.
Values may be sent and summed in bfloat16 or wider, within the bound.
No kernel may reach another device: no remote copies, remote signals or barrier semaphores. Data moves between devices by JAX's collectives and lax.ppermute only.
A program may use at most 64 MiB of HBM per device.

v0:
```python
import math

import jax
import jax.numpy as jnp
from jax import lax
from jax.sharding import PartitionSpec as P

BLOCK = 64
HPD = 4


def gelu_parts(value):
    cdf = 0.5 * (1.0 + lax.erf(value * 0.7071067811865476))
    return (value * cdf, cdf + value * jnp.exp(-0.5 * value * value) * 0.3989422804014327)


def project_up(x_trans, mats, cols, local):
    gathered = x_trans[cols]
    prod = jnp.einsum("skt,skn->snt", gathered, mats, preferred_element_type=jnp.float32)
    return jax.ops.segment_sum(prod, local, num_segments=HPD)


def inverse_of(order):
    count = order.shape[0]
    return jnp.zeros((count,), jnp.int32).at[order].set(jnp.arange(count, dtype=jnp.int32))


def to_rows(blocks):
    count = blocks.shape[2]
    return jnp.transpose(blocks, (2, 0, 1)).reshape(count, -1)


def to_blocks(rows_form):
    count = rows_form.shape[0]
    return jnp.transpose(rows_form.reshape(count, -1, BLOCK), (1, 2, 0))


def reorder_columns(spread, order):
    count = spread.shape[0]
    return spread.reshape(count, -1, BLOCK)[:, order].reshape(count, -1)


def input_terms(dpre_slots, up_mats, up_cols, in_blocks):
    count = dpre_slots.shape[2]
    dx_slots = jnp.einsum("snt,skn->skt", dpre_slots, up_mats, preferred_element_type=jnp.float32)
    dx_blocks = jax.ops.segment_sum(dx_slots, up_cols, num_segments=in_blocks)
    return jnp.transpose(dx_blocks, (2, 0, 1)).reshape(count, -1)


def per_device(
    tokens,
    grad_out,
    up_weight,
    down_weight,
    up_local,
    up_col,
    down_local,
    down_col,
    up_perm,
    down_perm,
):
    whole_x, whole_dy = (
        lax.all_gather(tokens, "tensor", axis=1, tiled=True),
        lax.all_gather(grad_out, "tensor", axis=1, tiled=True),
    )
    rows = whole_x.shape[0]
    x_trans = jnp.transpose(whole_x).reshape(-1, BLOCK, rows)
    dy_trans = jnp.transpose(whole_dy).reshape(-1, BLOCK, rows)
    in_blocks = x_trans.shape[0]
    up_loc = up_local[0]
    up_cols = up_col[0]
    down_loc = down_local[0]
    down_cols = down_col[0]
    scale = 1.0 / math.sqrt(rows * lax.axis_size("dp"))
    up_all, down_all = (
        lax.all_gather(up_weight, "dp", axis=1, tiled=True),
        lax.all_gather(down_weight, "dp", axis=1, tiled=True),
    )
    up_mats = up_all[0].reshape(-1, BLOCK, BLOCK)
    pre = project_up(x_trans, up_mats, up_cols, up_loc)
    down_mats = down_all[0].reshape(-1, BLOCK, BLOCK)
    to_down = inverse_of(up_perm)[down_perm]
    to_up = inverse_of(down_perm)[up_perm]
    active, slope = gelu_parts(pre)
    hidden = to_rows(active.astype(jnp.bfloat16))
    spread = lax.all_to_all(hidden, "tensor", split_axis=0, concat_axis=1, tiled=True)
    held_rows = lax.all_to_all(
        reorder_columns(spread, to_down), "tensor", split_axis=1, concat_axis=0, tiled=True
    )
    held = to_blocks(held_rows)
    dy_slots = dy_trans[down_cols]
    dh_slots = jnp.einsum("snt,skn->skt", dy_slots, down_mats, preferred_element_type=jnp.float32)
    dh = jax.ops.segment_sum(dh_slots, down_loc, num_segments=HPD, indices_are_sorted=True).astype(
        jnp.bfloat16
    )
    down_terms = (
        jnp.einsum("skt,snt->skn", held[down_loc], dy_slots, preferred_element_type=jnp.float32)
        * scale
    )
    back = lax.all_to_all(to_rows(dh), "tensor", split_axis=0, concat_axis=1, tiled=True)
    dh_up = to_blocks(
        lax.all_to_all(
            reorder_columns(back, to_up), "tensor", split_axis=1, concat_axis=0, tiled=True
        )
    )
    dpre = (dh_up.astype(jnp.float32) * slope).astype(jnp.bfloat16)
    dpre_slots = dpre[up_loc]
    dx_rows = input_terms(dpre_slots, up_mats, up_cols, in_blocks)
    grad_tokens = lax.psum_scatter(dx_rows, "tensor", scatter_dimension=1, tiled=True).astype(
        jnp.bfloat16
    )
    x_slots = x_trans[up_cols]
    up_terms = (
        jnp.einsum("skt,snt->skn", x_slots, dpre_slots, preferred_element_type=jnp.float32) * scale
    )
    up_total, down_total = (
        lax.psum(up_terms.astype(jnp.bfloat16), "dp").astype(jnp.float32),
        lax.psum(down_terms.astype(jnp.bfloat16), "dp").astype(jnp.float32),
    )
    grad_up = up_total.astype(jnp.bfloat16).reshape(1, -1, BLOCK * BLOCK)
    grad_down = down_total.astype(jnp.bfloat16).reshape(1, -1, BLOCK * BLOCK)
    return (grad_tokens, grad_up, grad_down)


def solution(mesh):
    return jax.shard_map(
        per_device,
        mesh=mesh,
        in_specs=(
            P("dp", "tensor"),
            P("dp", "tensor"),
            P("tensor", "dp", None),
            P("tensor", "dp", None),
            P("tensor", None),
            P("tensor", None),
            P("tensor", None),
            P("tensor", None),
            P(),
            P(),
        ),
        out_specs=(P("dp", "tensor"), P("tensor", None, None), P("tensor", None, None)),
        check_vma=False,
    )
```

profile of v0, /device:TPU:24, one launch (start us, length us, event | category | flops | bytes accessed | tf_op | source)
XLA Modules:
  0.0 1249.8 jit_solution(18217563529272206323)
XLA Ops:
  19.1 25.0 %all-gather.7.cloned.1.call-done = bf16[1,128,4096]{2,1,0:T(8,128)(2,1)} async-done(((bf16[1,16,4096]{2,1,0:T(8,128)(2,1)}), bf16[1,128,4096]{2,1,0:T(8,128)(2,1)}) %all-gather.7.cloned.1.call-update) | async-done | bytes 1048592 | tf_op jit(solution)/shard_map/all_gather | solution.py:77
  45.7 3.8 copy.41
  49.6 140.3 %all-gather.5.cloned.1.call-done = bf16[128,8192]{0,1:T(8,128)(2,1)} async-done(((bf16[128,128]{0,1:T(8,128)(2,1)}), bf16[128,8192]{0,1:T(8,128)(2,1)}) %all-gather.5.cloned.1.call-update) | async-done | bytes 2097168 | tf_op jit(solution)/shard_map/all_gather | solution.py:64
  192.4 4.2 convolution_bitcast_fusion.2
  196.7 13.7 %scatter_fusion = f32[4,64,128]{2,1,0:T(8,128)S(1)} fusion(f32[4,64,128]{2,1,0:T(8,128)S(1)} %broadcast.109.clone.1, s32[128]{0:T(128)S(1)} %bitcast.85, f32[128,64,128]{2,1,0:T(8,128)} %convolution_bitcast_fusion.2), kind=kCustom, calls=%fused_computation.8 | custom fusion | flops 1048576 | bytes 12583424 | tf_op jit(solution)/shard_map/scatter-add | solution.py:93
  211.3 10.2 all-to-all-start
  226.6 3.8 copy.51
  230.4 133.0 %all-gather.9.cloned.1.call-done = bf16[128,8192]{0,1:T(8,128)(2,1)} async-done(((bf16[128,128]{0,1:T(8,128)(2,1)}), bf16[128,8192]{0,1:T(8,128)(2,1)}) %all-gather.9.cloned.1.call-update) | async-done | bytes 2097168 | tf_op jit(solution)/shard_map/all_gather | solution.py:63
  369.3 10.4 all-to-all-start.1
  379.7 5.0 convolution_bitcast_fusion.1
  384.8 13.6 %scatter_fusion.1 = f32[4,64,128]{2,1,0:T(8,128)S(1)} fusion(f32[4,64,128]{2,1,0:T(8,128)S(1)} %broadcast.109.clone, s32[128]{0:T(128)S(1)} %bitcast.86, f32[128,64,128]{2,1,0:T(8,128)} %convolution_bitcast_fusion.1), kind=kCustom, calls=%fused_computation.10 | custom fusion | flops 1048576 | bytes 12583424 | tf_op jit(solution)/shard_map/scatter-add | solution.py:20
  399.9 15.0 %all-to-all-start.2 = ((bf16[64,2,256]{2,1,0:T(2,128)(2,1)}), bf16[64,2,256]{2,1,0:T(2,128)(2,1)S(1)}, u32[]{:S(2)}, u32[]{:S(2)}) async-start(bf16[64,2,256]{2,1,0:T(2,128)(2,1)} %all_to_all.51), calls=%async_computation.3 | async-start | bytes 131072 | tf_op jit(solution)/shard_map/all_to_all | solution.py:86
  417.0 12.5 all-to-all-done.2
  431.6 4.6 all-to-all-start.3
  436.2 4.8 multiply_convert_fusion.1
  441.0 4.0 copy.53
  445.0 5.8 all-to-all-done.3
  453.3 4.2 multiply_convert_fusion
  457.4 4.2 copy.60
  461.9 4.2 convolution_bitcast_fusion
  468.6 20.4 %scatter_fusion.2 = f32[128,64,128]{2,1,0:T(8,128)} fusion(f32[128,64,128]{2,1,0:T(8,128)} %broadcast_in_dim.6, s32[128]{0:T(128)S(1)} %bitcast.87, f32[128,64,128]{2,1,0:T(8,128)} %convolution_bitcast_fusion), kind=kCustom, calls=%fused_computation.11 | custom fusion | flops 1048576 | bytes 12583424 | tf_op jit(solution)/shard_map/scatter-add | solution.py:46
  489.1 5.7 copy.52
  494.7 40.8 %all-reduce.3.cloned.1.call-done = (bf16[1,128,4096]{1,2,0:T(8,128)(2,1)}, bf16[1,128,4096]{1,2,0:T(8,128)(2,1)}) async-done(((bf16[1,128,4096]{1,2,0:T(8,128)(2,1)}, bf16[1,128,4096]{1,2,0:T(8,128)(2,1)}), (bf16[1,128,4096]{1,2,0:T(8,128)(2,1)}, bf16[1,128,4096]{1,2,0:T(8,128)(2,1)})) %all-reduce.3.cloned.1.call-update) | async-done | bytes 2097168 | tf_op jit(solution)/shard_map/psum | solution.py:117
  539.2 702.3 %reduce-scatter.2.cloned.1.call-done = f32[128,128]{1,0:T(8,128)} async-done(((f32[128,8192]{1,0:T(8,128)}), f32[128,128]{1,0:T(8,128)}) %reduce-scatter.2.cloned.1.call-update) | async-done | bytes 65552 | tf_op jit(solution)/shard_map/reduce_scatter | solution.py:109
  (86 shorter events, 43.8 us)
Async XLA Ops:
  7.2 37.0 %all-gather.7.cloned.1.call-start = ((), (), s32[]{:S(2)}) async-start(), calls=%async_computation.6 | async-start | bytes 1179648 | tf_op jit(solution)/shard_map/all_gather | solution.py:77
  7.9 182.0 %all-gather.5.cloned.1.call-start = ((), (), s32[]{:S(2)}) async-start(), calls=%async_computation.5 | async-start | bytes 2129920 | tf_op jit(solution)/shard_map/all_gather | solution.py:64
  9.4 215.5 %all-gather.11.cloned.1.call-start = ((), (), s32[]{:S(2)}) async-start(), calls=%async_computation.8 | async-start | bytes 1179648 | tf_op jit(solution)/shard_map/all_gather | solution.py:76
  10.2 353.2 %all-gather.9.cloned.1.call-start = ((), (), s32[]{:S(2)}) async-start(), calls=%async_computation.7 | async-start | bytes 2129920 | tf_op jit(solution)/shard_map/all_gather | solution.py:63
  192.4 4.3 copy-start.2
  211.3 155.8 %all-to-all-start = ((bf16[64,2,256]{2,1,0:T(2,128)(2,1)}), bf16[64,2,256]{2,1,0:T(2,128)(2,1)S(1)}, u32[]{:S(2)}, u32[]{:S(2)}) async-start(bf16[64,2,256]{2,1,0:T(2,128)(2,1)} %all_to_all.46), calls=%async_computation | async-start | bytes 131072 | tf_op jit(solution)/shard_map/all_to_all | solution.py:100
  369.3 29.1 %all-to-all-start.1 = ((bf16[2,64,256]{2,0,1:T(2,128)(2,1)}), bf16[2,64,256]{2,0,1:T(2,128)(2,1)S(1)}, u32[]{:S(2)}, u32[]{:S(2)}) async-start(bf16[2,64,256]{2,0,1:T(2,128)(2,1)} %copy.46), calls=%async_computation.1 | async-start | bytes 131072 | tf_op jit(solution)/shard_map/all_to_all | solution.py:102
  379.7 5.1 copy-start.3
  399.9 29.6 %all-to-all-start.2 = ((bf16[64,2,256]{2,1,0:T(2,128)(2,1)}), bf16[64,2,256]{2,1,0:T(2,128)(2,1)S(1)}, u32[]{:S(2)}, u32[]{:S(2)}) async-start(bf16[64,2,256]{2,1,0:T(2,128)(2,1)} %all_to_all.51), calls=%async_computation.3 | async-start | bytes 131072 | tf_op jit(solution)/shard_map/all_to_all | solution.py:86
  431.6 19.3 %all-to-all-start.3 = ((bf16[2,64,256]{2,0,1:T(2,128)(2,1)}), bf16[2,64,256]{2,0,1:T(2,128)(2,1)S(1)}, u32[]{:S(2)}, u32[]{:S(2)}) async-start(bf16[2,64,256]{2,0,1:T(2,128)(2,1)} %copy.58), calls=%async_computation.4 | async-start | bytes 131072 | tf_op jit(solution)/shard_map/all_to_all | solution.py:87
  436.2 99.3 %all-reduce.3.cloned.1.call-start = ((), (), s32[]{:S(2)}) async-start(), calls=%async_computation.10 | async-start | bytes 4194304 | tf_op jit(solution)/shard_map/psum | solution.py:117
  457.4 4.5 copy-start
  461.6 779.9 %reduce-scatter.2.cloned.1.call-start = ((), (), s32[]{:S(2)}) async-start(), calls=%async_computation.9 | async-start | bytes 4259840 | tf_op jit(solution)/shard_map/reduce_scatter | solution.py:109
  466.1 2.5 copy-start.4
  535.5 2.4 copy-start.1
Sparse Core Ops, SparseCore 0:
  10.2 33.9 all-gather.6
  47.6 142.1 all-gather.4
  192.0 25.7 all-gather.10
  221.2 142.1 all-gather.8
  461.7 73.7 all-reduce.2
  539.8 701.7 reduce-scatter.1
where the time goes:
time: 1250 us
  waiting for transfers between devices  1060 us (85%)
  local copies, waits for them, and re-layouts  57.7 us (5%)
  other arithmetic  53.4 us (4%)
  starting transfers between devices  40.7 us (3%)
  matrix products  22.4 us (2%)
  between operations  14.5 us (1%)
    reduce_scatter x1, waiting for transfers between devices, per_device(): lax.psum_scatter(dx_rows, 'tensor', scatter_dimension=1, tiled=True)  702 us
    all_gather x1, waiting for transfers between devices, per_device(): lax.all_gather(grad_out, 'tensor', axis=1, tiled=True)  140 us
    all_gather x1, waiting for transfers between devices, per_device(): lax.all_gather(tokens, 'tensor', axis=1, tiled=True)  133 us
    psum x1, waiting for transfers between devices, per_device(): lax.psum(up_terms.astype(jnp.bfloat16), 'dp').astype(jnp.float32)  40.8 us
  transfers between devices with their start and end apart: 10, of which 7 were waited for; matrix products, arithmetic and copies ran while one was open for 9% of the time, Pallas kernels for 0%

commit v1 on v0

v1 whole, which is shorter than its diff:
```python
import jax
import jax.numpy as jnp
import numpy as np
from jax import lax
from jax.experimental import pallas as pl
from jax.experimental.pallas import tpu as pltpu
from jax.sharding import PartitionSpec as P

BLOCK = 64
HPD = 4
NX, NZ, NY = 4, 16, 4
BF = jnp.bfloat16
F32 = jnp.float32
VM = pl.BlockSpec(memory_space=pltpu.VMEM)
SM = pl.BlockSpec(memory_space=pltpu.SMEM)


def from_tensor(value, dx, dz):
    pairs = [
        (((x + dx) % NX) * NZ + (z + dz) % NZ, x * NZ + z) for x in range(NX) for z in range(NZ)
    ]
    return lax.ppermute(value, "tensor", pairs)


def from_y(value, dy):
    pairs = [(((y + dy) % NY) * 2 + c, y * 2 + c) for y in range(NY) for c in range(2)]
    return lax.ppermute(value, "dp", pairs)


def from_core(value):
    return lax.ppermute(value, "dp", [(d ^ 1, d) for d in range(2 * NY)])


def add(*parts):
    total = parts[0].astype(F32)
    for part in parts[1:]:
        total = total + part.astype(F32)
    return total.astype(BF)


Z_ORDER = (0, 5, 11, 1, 6, 12, 15, 4, 10, 2, 7, 13, 14, 3, 9, 8)
Z_SLOT = np.argsort(np.array(Z_ORDER)).astype(np.int32)


def gather_features(tokens, grad_out):
    own = jnp.stack([tokens, grad_out])[:, None]
    plus, minus = from_tensor(own, 0, 5), from_tensor(own, 0, -5)
    three = jnp.concatenate([own, plus, minus], axis=1)
    parts = [three] + [from_tensor(three, 0, dz) for dz in (1, -1, 2, -2)] + [from_tensor(plus, 0, 3)]
    x, dy = (jnp.concatenate([part[i] for part in parts]) for i in range(2))
    x_plus, dy_minus = from_tensor(x, 1, 0), from_tensor(dy, -1, 0)
    dy_plus, x_minus = from_tensor(dy, 1, 0), from_tensor(x, -1, 0)
    x_two, dy_two = from_tensor(x_plus, 1, 0), from_tensor(dy_minus, -1, 0)
    return (x, x_plus, x_two, x_minus, dy, dy_plus, dy_two, dy_minus), (plus, minus)


def block_place(cols):
    me = lax.axis_index("tensor")
    owner = cols // 2
    dx = (owner // NZ - me // NZ) % NX
    dz = (owner - me) % NZ
    slot = jnp.sum(jnp.where(dz[:, None] == jnp.arange(NZ), Z_SLOT[None], 0), axis=1)
    return ((dx * NZ + slot) * 2 + cols % 2).astype(jnp.int32)


def left_half():
    return lax.broadcasted_iota(jnp.int32, (BLOCK, 2 * BLOCK), 1) < BLOCK


def swap_halves(tile):
    return jnp.concatenate([tile[:, BLOCK:], tile[:, :BLOCK]], axis=1)


def spread_kernel(up_at, up_loc, down_at, down_loc, pairs, up_dense, down_dense):
    left = left_half()

    def clear(i, _):
        up_dense[pl.ds(2 * i, 2)] = jnp.zeros((2, 256, 128), BF)
        down_dense[pl.ds(2 * i, 2)] = jnp.zeros((2, 256, 128), BF)
        return 0

    lax.fori_loop(0, 32, clear, 0)

    def place(g, _):
        for p in range(8):
            for which, at_ref, loc_ref, dense in (
                (0, up_at, up_loc, up_dense),
                (1, down_at, down_loc, down_dense),
            ):
                tile = pairs[g, which, p]
                turned = swap_halves(tile)
                for side in range(2):
                    slot = g * 16 + side * 8 + p
                    at, loc = at_ref[slot], loc_ref[slot]
                    half = at % 2
                    view = dense.at[at // 2, pl.ds(pl.multiple_of(loc * BLOCK, BLOCK), BLOCK), :]
                    value = jnp.where(half == side, tile, turned)
                    view[...] = jnp.where(left == (half == 0), value, view[...])
        return 0

    lax.fori_loop(0, 8, place, 0)


def spread_weights(tables, pairs):
    shape = jax.ShapeDtypeStruct((64, 256, 128), BF)
    return pl.pallas_call(
        spread_kernel,
        in_specs=[SM] * 4 + [VM],
        out_specs=[VM, VM],
        out_shape=[shape, shape],
        compiler_params=pltpu.CompilerParams(vmem_limit_bytes=16 << 20),
        cost_estimate=pl.CostEstimate(flops=0, bytes_accessed=12 << 20, transcendentals=0),
        name="spread_weights",
    )(*tables, pairs)


def exchange_order(outward):
    row = lax.broadcasted_iota(jnp.int32, (512, 512), 0 if outward else 1)
    col = lax.broadcasted_iota(jnp.int32, (512, 512), 1 if outward else 0)
    return ((row % 8) * BLOCK + row // 8 == col).astype(F32).astype(BF)


def wide(ref, start, count):
    return jnp.concatenate([ref[start + i] for i in range(count)], axis=1)


def times_dense(features, dense):
    total = None
    for part in range(4):
        for first in (0, 8):
            term = lax.dot_general(
                wide(features[part], first, 8),
                wide(dense, part * 16 + first, 8),
                (((1,), (1,)), ((), ())),
                preferred_element_type=F32,
            )
            total = term if total is None else total + term
    return total


def forward_kernel(*refs):
    xs, dys, (up_dense, down_dense, out, slope) = refs[:4], refs[4:8], refs[8:]
    pre = times_dense(xs, up_dense)
    cdf = 0.5 * (1.0 + lax.erf(pre * 0.7071067811865476))
    slope[...] = cdf + pre * jnp.exp(-0.5 * pre * pre) * 0.3989422804014327
    hidden = (pre * cdf).astype(BF)
    both = jnp.concatenate([hidden, times_dense(dys, down_dense).astype(BF)], axis=1)
    out[...] = lax.dot_general(
        exchange_order(True), both, (((1,), (1,)), ((), ())), preferred_element_type=F32
    ).astype(BF)


def forward(features, up_dense, down_dense):
    return pl.pallas_call(
        forward_kernel,
        in_specs=[VM] * 10,
        out_specs=[VM, VM],
        out_shape=[
            jax.ShapeDtypeStruct((512, 128), BF),
            jax.ShapeDtypeStruct((128, 256), F32),
        ],
        compiler_params=pltpu.CompilerParams(vmem_limit_bytes=28 << 20),
        cost_estimate=pl.CostEstimate(flops=1 << 30, bytes_accessed=12 << 20, transcendentals=1 << 16),
        name="forward",
    )(*features, up_dense, down_dense)


def backward_kernel(me_ref, z_slot, up_at, up_loc, down_at, down_loc, *refs):
    xs, dys, (back, slope, up_w) = refs[:4], refs[4:8], refs[8:11]
    (same, other, near, to_plus, to_minus, later, up_dense, down_dense) = refs[11:]
    left = left_half()
    scale = 1.0 / 32.0
    both = jnp.dot(exchange_order(False), back[...], preferred_element_type=F32)
    hidden_t = both[:256].astype(BF)
    dpre_f32 = both[256:].T * slope[...]
    dpre = dpre_f32.astype(BF)
    dpre_t = dpre_f32.T.astype(BF)

    def terms(target, z, part):
        w = jnp.concatenate([up_w[part * NZ + z_slot[z + j]] for j in range(2)], axis=1)
        value = jnp.dot(dpre, w, preferred_element_type=F32).astype(BF)
        target[z] = value[:, :128]
        target[z + 1] = value[:, 128:]

    for z in range(0, NZ, 2):
        low = z < NZ // 2
        terms(to_plus, z, 2 if low else 1)
        terms(to_minus, z, 3 if low else 2)
        terms(later, z, 1 if low else 3)
        terms(near, z, 0)

    for part in range(4):

        def step(i, _, part=part):
            at = part * 16 + 2 * i
            for lhs, source, dense in ((dpre_t, xs, up_dense), (hidden_t, dys, down_dense)):
                value = jnp.dot(lhs, wide(source[part], 2 * i, 2), preferred_element_type=F32)
                value = (value * scale).astype(BF)
                dense[at] = value[:, :128]
                dense[at + 1] = value[:, 128:]
            return 0

        lax.fori_loop(0, 8, step, 0, unroll=2)
    me = me_ref[0]
    for dc, target in ((0, same), (1, other)):

        def pick(dy, _, dc=dc, target=target):
            first = ((((me // 2 + dy) % NY) * 2) + (me % 2 + dc) % 2) * 16
            for p in range(8):
                for which, at_ref, loc_ref, dense in (
                    (0, up_at, up_loc, up_dense),
                    (1, down_at, down_loc, down_dense),
                ):
                    sides = []
                    for side in range(2):
                        slot = first + side * 8 + p
                        at, loc = at_ref[slot], loc_ref[slot]
                        tile = dense[at // 2, pl.ds(pl.multiple_of(loc * BLOCK, BLOCK), BLOCK), :]
                        sides.append(jnp.where(at % 2 == side, tile, swap_halves(tile)))
                    target[dy, which, p] = jnp.where(left, sides[0], sides[1])
            return 0

        lax.fori_loop(0, 4, pick, 0)


def backward(me, z_slot, tables, features, back, slope, up_w):
    shape = jax.ShapeDtypeStruct((4, 2, 8, BLOCK, 128), BF)
    chunk = jax.ShapeDtypeStruct((NZ, 128, 128), BF)
    return pl.pallas_call(
        backward_kernel,
        in_specs=[SM] * 6 + [VM] * 11,
        out_specs=[VM] * 6,
        out_shape=[shape, shape, chunk, chunk, chunk, chunk],
        scratch_shapes=[pltpu.VMEM((64, 256, 128), BF), pltpu.VMEM((64, 256, 128), BF)],
        compiler_params=pltpu.CompilerParams(vmem_limit_bytes=32 << 20),
        cost_estimate=pl.CostEstimate(flops=3 << 29, bytes_accessed=14 << 20, transcendentals=0),
        name="backward",
    )(me, z_slot, *tables, *features, back, slope, up_w)


def pack(up, down):
    up = jnp.swapaxes(up.reshape(2, 8, BLOCK, BLOCK), 2, 3)
    slots = jnp.stack([up, down.reshape(2, 8, BLOCK, BLOCK)])
    return jnp.concatenate([slots[:, 0], slots[:, 1]], axis=3)


def unpack(pairs, turned=False):
    axis = 1 if turned else 2
    slots = jnp.concatenate(jnp.split(pairs, 2, axis=axis))
    return slots.reshape(16, BLOCK * BLOCK)


Y_GROUPS = [[y * 2 + c for y in range(NY)] for c in range(2)]
Z_GROUPS = [[x * NZ + z for z in range(NZ)] for x in range(NX)]


def exchange(rows):
    return lax.all_to_all(rows.reshape(64, 8, 128), "tensor", 0, 0, tiled=True).reshape(512, 128)


def reduce_all(same, other, near, to_plus, to_minus, later):
    half = NZ // 2
    order = lax.optimization_barrier
    got_plus, got_minus = from_tensor(to_plus, -1, 0), from_tensor(to_minus, 1, 0)
    total = add(same, from_core(other))
    y_plus, y_minus = jnp.stack([total[2, 0], total[1, 1]]), jnp.stack([total[2, 1], total[3, 0]])
    got_plus, got_minus, _, _ = order((got_plus, got_minus, y_plus, y_minus))
    on_plus, on_minus = add(later[:half], got_plus[:half]), add(later[half:], got_minus[half:])
    y_plus, y_minus = from_y(y_plus, -1), from_y(y_minus, 1)
    low, high = from_tensor(on_plus, -1, 0), from_tensor(on_minus, 1, 0)
    y_plus, y_minus, _, _ = order((y_plus, y_minus, on_plus, on_minus))
    on_down, on_up = add(total[3, 1], y_minus[0]), add(total[1, 0], y_plus[0])
    low, high, _, _ = order((low, high, on_down, on_up))
    on_down, on_up = order((from_y(on_down, 1), from_y(on_up, -1)))
    down = unpack(add(total[0, 1], y_plus[1], on_down))
    up = unpack(jnp.swapaxes(add(total[0, 0], on_up, y_minus[1]), 1, 2), True)
    low = add(near[:half], low, got_minus[:half])
    high = add(near[half:], got_plus[half:], high)
    column, own = order((jnp.concatenate([low, high]), jnp.stack([up, down])))
    mine = lax.all_gather(own, "dp", axis=0, axis_index_groups=Y_GROUPS)
    parts = lax.all_to_all(column, "tensor", 0, 0, tiled=True, axis_index_groups=Z_GROUPS)
    theirs = from_core(mine)
    even = lax.axis_index("dp") % 2 == 0
    up, down = (
        jnp.stack(
            [
                jnp.where(even, mine[:, i], theirs[:, i]),
                jnp.where(even, theirs[:, i], mine[:, i]),
            ],
            axis=1,
        ).reshape(1, 128, -1)
        for i in range(2)
    )
    return jnp.sum(parts.astype(F32), axis=0).astype(BF), up, down


def per_device(
    tokens,
    grad_out,
    up_weight,
    down_weight,
    up_local,
    up_col,
    down_local,
    down_col,
    up_perm,
    down_perm,
):
    features, first = gather_features(tokens, grad_out)
    up_own, down_own, *_ = lax.optimization_barrier((up_weight[0], down_weight[0], *first))
    pairs = lax.all_gather(pack(up_own, down_own), "dp", axis=0)
    tables = (block_place(up_col[0]), up_local[0], block_place(down_col[0]), down_local[0])
    up4, down4 = up_perm.reshape(-1, HPD), down_perm.reshape(-1, HPD)
    wanted = jnp.stack([down4, up4 + 256], axis=1).reshape(-1)
    present = jnp.stack([up4, down4 + 256], axis=1).reshape(-1)
    route = (wanted[:, None] == present[None, :]).astype(BF)
    z_from_me = (jnp.arange(NZ) - lax.axis_index("tensor")) % NZ
    z_slot = jnp.sum(jnp.where(z_from_me[:, None] == jnp.arange(NZ), Z_SLOT[None], 0), axis=1)

    up_dense, down_dense = spread_weights(tables, pairs)
    sent, slope = forward(features, up_dense, down_dense)
    routed = jnp.dot(route, exchange(sent), preferred_element_type=F32).astype(BF)
    back = exchange(routed)
    me = lax.axis_index("dp").astype(jnp.int32)
    terms = backward(
        me.reshape(1), z_slot.astype(jnp.int32), tables, features, back, slope, up_dense
    )
    return reduce_all(*terms)


def solution(mesh):
    return jax.shard_map(
        per_device,
        mesh=mesh,
        in_specs=(
            P("dp", "tensor"),
            P("dp", "tensor"),
            P("tensor", "dp", None),
            P("tensor", "dp", None),
            P("tensor", None),
            P("tensor", None),
            P("tensor", None),
            P("tensor", None),
            P(),
            P(),
        ),
        out_specs=(P("dp", "tensor"), P("tensor", None, None), P("tensor", None, None)),
        check_vma=False,
    )
```

time: 1250 us -> 255 us (0.20)
  waiting for transfers between devices: 1060 us -> 90.6 us
  starting transfers between devices: 40.7 us -> 107 us
  local copies, waits for them, and re-layouts: 57.7 us -> 8.95 us
  other arithmetic: 53.4 us -> 8.27 us
  matrix products: 22.4 us -> 1.92 us
  Pallas kernels: 0 us -> 19.2 us
    reduce_scatter x1 -> x0, waiting for transfers between devices: 702 us -> none  [per_device(): lax.psum_scatter(dx_rows, 'tensor', scatter_dimension=1, tiled=True)]
    all_gather x4 -> x2, waiting for transfers between devices: 298 us -> 19.3 us  [the longest x1 19.3 us: reduce_all(): mine = lax.all_gather(own, 'dp', axis=0, axis_index_groups=Y_GROUPS)]
    ppermute x0 -> x23, starting transfers between devices: none -> 85.8 us  [the longest x17 67.8 us: from_tensor(): return lax.ppermute(value, 'tensor', pairs)]
    scatter-add x3 -> x0, other arithmetic: 47.7 us -> none  [the longest x1 20.4 us: input_terms(): dx_blocks = jax.ops.segment_sum(dx_slots, up_cols, num_segments=in_blocks)]
    psum x1 -> x0, waiting for transfers between devices: 40.8 us -> none  [per_device(): lax.psum(up_terms.astype(jnp.bfloat16), 'dp').astype(jnp.float32)]
    ppermute x0 -> x23, waiting for transfers between devices: none -> 36.1 us  [the longest x17 34.6 us: from_tensor(): return lax.ppermute(value, 'tensor', pairs)]
    dot_general x5 -> x1, matrix products: 22.4 us -> 1.92 us  [per_device(): jnp.dot(route, exchange(sent), preferred_element_type=F32).astype(BF)]
    pallas_call x0 -> x3, Pallas kernels: none -> 19.2 us  [the longest x1 10 us: backward(): pl.pallas_call(backward_kernel, in_specs=[SM] * 6 + [VM] * 11, out_specs=...]
  transfers between devices with their start and end apart: 10 -> 28, of which waited for: 7 -> 15; matrix products, arithmetic and copies ran while one was open for 9% -> 1% of each run, Pallas kernels for 0% -> 2%
where the time goes in v1:
time: 255 us; the launch traced here: 251 us
  starting transfers between devices  107 us (42%)
  waiting for transfers between devices  90.6 us (36%)
  Pallas kernels  19.2 us (8%)
  between operations  14.7 us (6%)
  local copies, waits for them, and re-layouts  8.95 us (4%)
  other arithmetic  8.27 us (3%)
    ppermute x17, starting transfers between devices, from_tensor(): return lax.ppermute(value, 'tensor', pairs)  67.8 us
    ppermute x17, waiting for transfers between devices, from_tensor(): return lax.ppermute(value, 'tensor', pairs)  34.6 us
    all_to_all x2, waiting for transfers between devices, exchange(): lax.all_to_all(rows.reshape(64, 8, 128), 'tensor', 0, 0, tiled=True)  29.9 us
    all_gather x1, waiting for transfers between devices, reduce_all(): mine = lax.all_gather(own, 'dp', axis=0, axis_index_groups=Y_GROUPS)  19.3 us
    all_to_all x2, starting transfers between devices, exchange(): lax.all_to_all(rows.reshape(64, 8, 128), 'tensor', 0, 0, tiled=True)  17.6 us
    ppermute x4, starting transfers between devices, from_y(): return lax.ppermute(value, 'dp', pairs)  14.1 us
    pallas_call x1, Pallas kernels, backward(): pl.pallas_call(backward_kernel, in_specs=[SM] * 6 + [VM] * 11, out_specs=...  10 us
    all_to_all x1, waiting for transfers between devices, reduce_all(): lax.all_to_all(column, 'tensor', 0, 0, tiled=True, axis_index_groups=Z_GR...  5.39 us
  transfers between devices with their start and end apart: 28, of which 15 were waited for; matrix products, arithmetic and copies ran while one was open for 1% of the time, Pallas kernels for 2%

profile of v1, /device:TPU:24, one launch (start us, length us, event | category | flops | bytes accessed | tf_op | source)
XLA Modules:
  0.0 250.8 jit_solution(2547714592549910339)
XLA Ops:
  8.0 14.4 %collective-permute-start = (bf16[2,1,128,128]{3,2,1,0:T(8,128)(2,1)S(1)}, bf16[2,1,128,128]{3,2,1,0:T(8,128)(2,1)S(1)}, u32[]{:S(2)}, u32[]{:S(2)}) collective-permute-start(bf16[2,1,128,128]{3,2,1,0:T(8,128)(2,1)S(1)} %maximum_bitcast_fusion), channel_id=1, source_target_pairs={{5,0},{6,1},{7,2},{8,3},{9,4},{10,5},{11,6},{12,7},{13,8},{14,9},{... | collective-permute-start | bytes 196616 | tf_op jit(solution)/shard_map/ppermute | solution.py:22
  24.3 4.3 %collective-permute-done = bf16[2,1,128,128]{3,2,1,0:T(8,128)(2,1)S(1)} collective-permute-done((bf16[2,1,128,128]{3,2,1,0:T(8,128)(2,1)S(1)}, bf16[2,1,128,128]{3,2,1,0:T(8,128)(2,1)S(1)}, u32[]{:S(2)}, u32[]{:S(2)}) %collective-permute-start) | collective-permute-done | bytes 65568 | tf_op jit(solution)/shard_map/ppermute | solution.py:22
  28.6 10.2 %collective-permute-done.1 = bf16[2,1,128,128]{3,2,1,0:T(8,128)(2,1)S(1)} collective-permute-done((bf16[2,1,128,128]{3,2,1,0:T(8,128)(2,1)S(1)}, bf16[2,1,128,128]{3,2,1,0:T(8,128)(2,1)S(1)}, u32[]{:S(2)}, u32[]{:S(2)}) %collective-permute-start.1) | collective-permute-done | bytes 65568 | tf_op jit(solution)/shard_map/ppermute | solution.py:22
  45.0 3.4 %collective-permute-start.3 = (bf16[2,3,128,128]{3,2,1,0:T(8,128)(2,1)S(1)}, bf16[2,3,128,128]{3,2,1,0:T(8,128)(2,1)S(1)}, u32[]{:S(2)}, u32[]{:S(2)}) collective-permute-start(bf16[2,3,128,128]{3,2,1,0:T(8,128)(2,1)S(1)} %pad_maximum_fusion.10), channel_id=1, source_target_pairs={{15,0},{0,1},{1,2},{2,3},{3,4},{4,5},{5,6},{6,7},{7,8},{8,9},{9,10... | collective-permute-start | bytes 589832 | tf_op jit(solution)/shard_map/ppermute | solution.py:22
  50.8 4.4 %collective-permute-start.5 = (bf16[2,3,128,128]{3,2,1,0:T(8,128)(2,1)S(1)}, bf16[2,3,128,128]{3,2,1,0:T(8,128)(2,1)S(1)}, u32[]{:S(2)}, u32[]{:S(2)}) collective-permute-start(bf16[2,3,128,128]{3,2,1,0:T(8,128)(2,1)S(1)} %pad_maximum_fusion.10), channel_id=1, source_target_pairs={{14,0},{15,1},{0,2},{1,3},{2,4},{3,5},{4,6},{5,7},{6,8},{7,9},{8,1... | collective-permute-start | bytes 589832 | tf_op jit(solution)/shard_map/ppermute | solution.py:22
  58.5 5.5 %collective-permute-done.5 = bf16[2,3,128,128]{3,2,1,0:T(8,128)(2,1)S(1)} collective-permute-done((bf16[2,3,128,128]{3,2,1,0:T(8,128)(2,1)S(1)}, bf16[2,3,128,128]{3,2,1,0:T(8,128)(2,1)S(1)}, u32[]{:S(2)}, u32[]{:S(2)}) %collective-permute-start.5) | collective-permute-done | bytes 196640 | tf_op jit(solution)/shard_map/ppermute | solution.py:22
  67.4 3.7 %collective-permute-start.7 = (bf16[16,128,128]{2,1,0:T(8,128)(2,1)S(1)}, bf16[16,128,128]{2,1,0:T(8,128)(2,1)S(1)}, u32[]{:S(2)}, u32[]{:S(2)}) collective-permute-start(bf16[16,128,128]{2,1,0:T(8,128)(2,1)S(1)} %get-tuple-element.86.refs_0_), channel_id=1, source_target_pairs={{16,0},{17,1},{18,2},{19,3},{20,4},{21,5},{22,6},{23,7},{24,8},{25... | collective-permute-start | bytes 1572872 | tf_op jit(solution)/shard_map/ppermute | solution.py:22
  71.3 3.5 %collective-permute-start.10 = (bf16[16,128,128]{2,1,0:T(8,128)(2,1)S(1)}, bf16[16,128,128]{2,1,0:T(8,128)(2,1)S(1)}, u32[]{:S(2)}, u32[]{:S(2)}) collective-permute-start(bf16[16,128,128]{2,1,0:T(8,128)(2,1)S(1)} %get-tuple-element.85.refs_4_), channel_id=1, source_target_pairs={{16,0},{17,1},{18,2},{19,3},{20,4},{21,5},{22,6},{23,7},{24,8},{25... | collective-permute-start | bytes 1572872 | tf_op jit(solution)/shard_map/ppermute | solution.py:22
  84.2 4.9 %collective-permute-start.8 = (bf16[16,128,128]{2,1,0:T(8,128)(2,1)S(1)}, bf16[16,128,128]{2,1,0:T(8,128)(2,1)}, u32[]{:S(2)}, u32[]{:S(2)}) collective-permute-start(bf16[16,128,128]{2,1,0:T(8,128)(2,1)S(1)} %collective-permute-done.7.refs_1_), channel_id=1, source_target_pairs={{16,0},{17,1},{18,2},{19,3},{20,4},{21,5},{22,6},{23,7},{24,8},{25... | collective-permute-start | bytes 1572872 | tf_op jit(solution)/shard_map/ppermute | solution.py:22
  90.8 4.2 %spread_weights.1 = (bf16[64,256,128]{2,1,0:T(8,128)(2,1)S(1)}, bf16[64,256,128]{2,1,0:T(8,128)(2,1)S(1)}) custom-call(s32[128]{0:T(128)S(1)} %fusion.26.up_at, s32[128]{0:T(128)S(1)} %bitcast.153, s32[128]{0:T(128)S(1)} %fusion.27.down_at, s32[128]{0:T(128)S(1)} %bitcast.155, bf16[8,2,8,64,128]{4,3,2,1,0:T(8,128)(2,1)S(1)} %bitcast.151), custom_call_target="tpu_custom_call" | custom-call | bytes 12582912 | tf_op jit(solution)/shard_map/spread_weights/pallas_call | solution.py:106
  95.4 4.8 %collective-permute-done.12.refs_6_ = bf16[16,128,128]{2,1,0:T(8,128)(2,1)} collective-permute-done((bf16[16,128,128]{2,1,0:T(8,128)(2,1)S(1)}, bf16[16,128,128]{2,1,0:T(8,128)(2,1)}, u32[]{:S(2)}, u32[]{:S(2)}) %collective-permute-start.12) | collective-permute-done | bytes 524320 | tf_op jit(solution)/shard_map/ppermute | solution.py:22
  102.2 4.9 %forward.1 = (bf16[512,128]{1,0:T(8,128)(2,1)}, f32[128,256]{1,0:T(8,128)S(1)}) custom-call(bf16[16,128,128]{2,1,0:T(8,128)(2,1)S(1)} %get-tuple-element.86.refs_0_, bf16[16,128,128]{2,1,0:T(8,128)(2,1)S(1)} %collective-permute-done.7.refs_1_, bf16[16,128,128]{2,1,0:T(8,128)(2,1)} %collective-permute-done.8.refs_2_, ...), custom_call_target="tpu_custom_call" | custom-call | flops 1073741824 | bytes 12582912 | tf_op jit(solution)/shard_map/forward/pallas_call | solution.py:154
  107.1 12.1 %all-to-all-start = ((bf16[64,8,128]{2,1,0:T(8,128)(2,1)}), bf16[64,8,128]{2,1,0:T(8,128)(2,1)}, u32[]{:S(2)}, u32[]{:S(2)}) async-start(bf16[64,8,128]{2,1,0:T(8,128)(2,1)} %bitcast.27), calls=%async_computation | async-start | bytes 262144 | tf_op jit(solution)/shard_map/all_to_all | solution.py:258
  119.8 14.8 %all-to-all-done = bf16[64,8,128]{2,1,0:T(8,128)(2,1)} async-done(((bf16[64,8,128]{2,1,0:T(8,128)(2,1)}), bf16[64,8,128]{2,1,0:T(8,128)(2,1)}, u32[]{:S(2)}, u32[]{:S(2)}) %all-to-all-start) | async-done | bytes 131104 | tf_op jit(solution)/shard_map/all_to_all | solution.py:258
  136.5 5.5 %all-to-all-start.1 = ((bf16[64,8,128]{2,1,0:T(8,128)(2,1)}), bf16[64,8,128]{2,1,0:T(8,128)(2,1)S(1)}, u32[]{:S(2)}, u32[]{:S(2)}) async-start(bf16[64,8,128]{2,1,0:T(8,128)(2,1)} %fusion), calls=%async_computation.1 | async-start | bytes 262144 | tf_op jit(solution)/shard_map/all_to_all | solution.py:258
  142.3 15.0 %all-to-all-done.1 = bf16[64,8,128]{2,1,0:T(8,128)(2,1)S(1)} async-done(((bf16[64,8,128]{2,1,0:T(8,128)(2,1)}), bf16[64,8,128]{2,1,0:T(8,128)(2,1)S(1)}, u32[]{:S(2)}, u32[]{:S(2)}) %all-to-all-start.1) | async-done | bytes 131104 | tf_op jit(solution)/shard_map/all_to_all | solution.py:258
  159.5 10.0 %backward.1 = (bf16[4,2,8,64,128]{4,3,2,1,0:T(8,128)(2,1)S(1)}, bf16[4,2,8,64,128]{4,3,2,1,0:T(8,128)(2,1)S(1)}, bf16[16,128,128]{2,1,0:T(8,128)(2,1)S(1)}, bf16...) custom-call(s32[1]{0:T(128)} %bitcast.me_ref, ...), custom_call_target="tpu_custom_call" | custom-call | flops 1610612736 | bytes 14680064 | tf_op jit(solution)/shard_map/backward/pallas_call | solution.py:229
  174.1 4.4 %collective-permute-start.14 = (bf16[16,128,128]{2,1,0:T(8,128)(2,1)S(1)}, bf16[16,128,128]{2,1,0:T(8,128)(2,1)S(1)}, u32[]{:S(2)}, u32[]{:S(2)}) collective-permute-start(bf16[16,128,128]{2,1,0:T(8,128)(2,1)S(1)} %get-tuple-element.34), channel_id=1, source_target_pairs={{16,0},{17,1},{18,2},{19,3},{20,4},{21,5},{22,6},{23,7},{24,8},{25... | collective-permute-start | bytes 1572872 | tf_op jit(solution)/shard_map/ppermute | solution.py:22
  181.7 4.4 %collective-permute-start.18 = (bf16[2,8,64,128]{3,2,1,0:T(8,128)(2,1)S(1)}, bf16[2,8,64,128]{3,2,1,0:T(8,128)(2,1)S(1)}, u32[]{:S(2)}, u32[]{:S(2)}) collective-permute-start(bf16[2,8,64,128]{3,2,1,0:T(8,128)(2,1)S(1)} %pad_maximum_fusion.5), channel_id=1, source_target_pairs={{384,0},{448,64},{0,128},{64,192},{128,256},{192,320},{256,384},{3... | collective-permute-start | bytes 786440 | tf_op jit(solution)/shard_map/ppermute | solution.py:27
  193.6 4.4 %collective-permute-start.17 = (bf16[8,128,128]{2,1,0:T(8,128)(2,1)S(1)}, bf16[8,128,128]{2,1,0:T(8,128)(2,1)S(1)}, u32[]{:S(2)}, u32[]{:S(2)}) collective-permute-start(bf16[8,128,128]{2,1,0:T(8,128)(2,1)S(1)} %get-tuple-element.67), channel_id=1, source_target_pairs={{16,0},{17,1},{18,2},{19,3},{20,4},{21,5},{22,6},{23,7},{24,8},{25... | collective-permute-start | bytes 786440 | tf_op jit(solution)/shard_map/ppermute | solution.py:22
  200.7 4.4 %collective-permute-start.21 = (bf16[8,64,128]{2,1,0:T(8,128)(2,1)S(1)}, bf16[8,64,128]{2,1,0:T(8,128)(2,1)S(1)}, u32[]{:S(2)}, u32[]{:S(2)}) collective-permute-start(bf16[8,64,128]{2,1,0:T(8,128)(2,1)S(1)} %get-tuple-element.59), channel_id=1, source_target_pairs={{384,0},{448,64},{0,128},{64,192},{128,256},{192,320},{256,384},{3... | collective-permute-start | bytes 393224 | tf_op jit(solution)/shard_map/ppermute | solution.py:27
  209.6 3.6 %all-to-all-start.2 = ((bf16[16,128,128]{2,1,0:T(8,128)(2,1)}), bf16[16,128,128]{2,1,0:T(8,128)(2,1)S(1)}, u32[]{:S(2)}, u32[]{:S(2)}) async-start(bf16[16,128,128]{2,1,0:T(8,128)(2,1)} %pad_maximum_fusion.3), calls=%async_computation.2 | async-start | bytes 1048576 | tf_op jit(solution)/shard_map/all_to_all | solution.py:281
  213.2 19.3 %all-gather.7.cloned.1.call-done = bf16[8,16,4096]{2,1,0:T(8,128)(2,1)} async-done(((bf16[2,16,4096]{2,1,0:T(8,128)(2,1)}), bf16[8,16,4096]{2,1,0:T(8,128)(2,1)}) %all-gather.7.cloned.1.call-update) | async-done | bytes 1048592 | tf_op jit(solution)/shard_map/all_gather | solution.py:280
  234.4 5.4 %all-to-all-done.2 = bf16[16,128,128]{2,1,0:T(8,128)(2,1)S(1)} async-done(((bf16[16,128,128]{2,1,0:T(8,128)(2,1)}), bf16[16,128,128]{2,1,0:T(8,128)(2,1)S(1)}, u32[]{:S(2)}, u32[]{:S(2)}) %all-to-all-start.2) | async-done | bytes 524320 | tf_op jit(solution)/shard_map/all_to_all | solution.py:281
  (109 shorter events, 64.5 us)
Async XLA Ops:
  7.2 82.0 %all-gather.5.cloned.1.call-start = ((), (), s32[]{:S(2)}) async-start(), calls=%async_computation.3 | async-start | bytes 2359296 | tf_op jit(solution)/shard_map/all_gather | solution.py:311
  8.0 20.6 %collective-permute-start = (bf16[2,1,128,128]{3,2,1,0:T(8,128)(2,1)S(1)}, bf16[2,1,128,128]{3,2,1,0:T(8,128)(2,1)S(1)}, u32[]{:S(2)}, u32[]{:S(2)}) collective-permute-start(bf16[2,1,128,128]{3,2,1,0:T(8,128)(2,1)S(1)} %maximum_bitcast_fusion), channel_id=1, source_target_pairs={{5,0},{6,1},{7,2},{8,3},{9,4},{10,5},{11,6},{12,7},{13,8},{14,9},{... | collective-permute-start | bytes 196616 | tf_op jit(solution)/shard_map/ppermute | solution.py:22
  22.4 16.4 %collective-permute-start.1 = (bf16[2,1,128,128]{3,2,1,0:T(8,128)(2,1)S(1)}, bf16[2,1,128,128]{3,2,1,0:T(8,128)(2,1)S(1)}, u32[]{:S(2)}, u32[]{:S(2)}) collective-permute-start(bf16[2,1,128,128]{3,2,1,0:T(8,128)(2,1)S(1)} %maximum_bitcast_fusion), channel_id=1, source_target_pairs={{11,0},{12,1},{13,2},{14,3},{15,4},{0,5},{1,6},{2,7},{3,8},{4,9},{... | collective-permute-start | bytes 196616 | tf_op jit(solution)/shard_map/ppermute | solution.py:22
  42.6 15.7 %collective-permute-start.2 = (bf16[2,3,128,128]{3,2,1,0:T(8,128)(2,1)S(1)}, bf16[2,3,128,128]{3,2,1,0:T(8,128)(2,1)S(1)}, u32[]{:S(2)}, u32[]{:S(2)}) collective-permute-start(bf16[2,3,128,128]{3,2,1,0:T(8,128)(2,1)S(1)} %pad_maximum_fusion.10), channel_id=1, source_target_pairs={{1,0},{2,1},{3,2},{4,3},{5,4},{6,5},{7,6},{8,7},{9,8},{10,9},{11,1... | collective-permute-start | bytes 589832 | tf_op jit(solution)/shard_map/ppermute | solution.py:22
  45.0 13.3 %collective-permute-start.3 = (bf16[2,3,128,128]{3,2,1,0:T(8,128)(2,1)S(1)}, bf16[2,3,128,128]{3,2,1,0:T(8,128)(2,1)S(1)}, u32[]{:S(2)}, u32[]{:S(2)}) collective-permute-start(bf16[2,3,128,128]{3,2,1,0:T(8,128)(2,1)S(1)} %pad_maximum_fusion.10), channel_id=1, source_target_pairs={{15,0},{0,1},{1,2},{2,3},{3,4},{4,5},{5,6},{6,7},{7,8},{8,9},{9,10... | collective-permute-start | bytes 589832 | tf_op jit(solution)/shard_map/ppermute | solution.py:22
  48.5 9.9 %collective-permute-start.4 = (bf16[2,3,128,128]{3,2,1,0:T(8,128)(2,1)S(1)}, bf16[2,3,128,128]{3,2,1,0:T(8,128)(2,1)S(1)}, u32[]{:S(2)}, u32[]{:S(2)}) collective-permute-start(bf16[2,3,128,128]{3,2,1,0:T(8,128)(2,1)S(1)} %pad_maximum_fusion.10), channel_id=1, source_target_pairs={{2,0},{3,1},{4,2},{5,3},{6,4},{7,5},{8,6},{9,7},{10,8},{11,9},{12,... | collective-permute-start | bytes 589832 | tf_op jit(solution)/shard_map/ppermute | solution.py:22
  50.8 13.2 %collective-permute-start.5 = (bf16[2,3,128,128]{3,2,1,0:T(8,128)(2,1)S(1)}, bf16[2,3,128,128]{3,2,1,0:T(8,128)(2,1)S(1)}, u32[]{:S(2)}, u32[]{:S(2)}) collective-permute-start(bf16[2,3,128,128]{3,2,1,0:T(8,128)(2,1)S(1)} %pad_maximum_fusion.10), channel_id=1, source_target_pairs={{14,0},{15,1},{0,2},{1,3},{2,4},{3,5},{4,6},{5,7},{6,8},{7,9},{8,1... | collective-permute-start | bytes 589832 | tf_op jit(solution)/shard_map/ppermute | solution.py:22
  64.0 14.9 %collective-permute-start.11 = (bf16[16,128,128]{2,1,0:T(8,128)(2,1)S(1)}, bf16[16,128,128]{2,1,0:T(8,128)(2,1)S(1)}, u32[]{:S(2)}, u32[]{:S(2)}) collective-permute-start(bf16[16,128,128]{2,1,0:T(8,128)(2,1)S(1)} %get-tuple-element.85.refs_4_), channel_id=1, source_target_pairs={{48,0},{49,1},{50,2},{51,3},{52,4},{53,5},{54,6},{55,7},{56,8},{57... | collective-permute-start | bytes 1572872 | tf_op jit(solution)/shard_map/ppermute | solution.py:22
  67.4 16.8 %collective-permute-start.7 = (bf16[16,128,128]{2,1,0:T(8,128)(2,1)S(1)}, bf16[16,128,128]{2,1,0:T(8,128)(2,1)S(1)}, u32[]{:S(2)}, u32[]{:S(2)}) collective-permute-start(bf16[16,128,128]{2,1,0:T(8,128)(2,1)S(1)} %get-tuple-element.86.refs_0_), channel_id=1, source_target_pairs={{16,0},{17,1},{18,2},{19,3},{20,4},{21,5},{22,6},{23,7},{24,8},{25... | collective-permute-start | bytes 1572872 | tf_op jit(solution)/shard_map/ppermute | solution.py:22
  71.3 24.1 %collective-permute-start.10 = (bf16[16,128,128]{2,1,0:T(8,128)(2,1)S(1)}, bf16[16,128,128]{2,1,0:T(8,128)(2,1)S(1)}, u32[]{:S(2)}, u32[]{:S(2)}) collective-permute-start(bf16[16,128,128]{2,1,0:T(8,128)(2,1)S(1)} %get-tuple-element.85.refs_4_), channel_id=1, source_target_pairs={{16,0},{17,1},{18,2},{19,3},{20,4},{21,5},{22,6},{23,7},{24,8},{25... | collective-permute-start | bytes 1572872 | tf_op jit(solution)/shard_map/ppermute | solution.py:22
  74.7 20.7 %collective-permute-start.9 = (bf16[16,128,128]{2,1,0:T(8,128)(2,1)S(1)}, bf16[16,128,128]{2,1,0:T(8,128)(2,1)S(1)}, u32[]{:S(2)}, u32[]{:S(2)}) collective-permute-start(bf16[16,128,128]{2,1,0:T(8,128)(2,1)S(1)} %get-tuple-element.86.refs_0_), channel_id=1, source_target_pairs={{48,0},{49,1},{50,2},{51,3},{52,4},{53,5},{54,6},{55,7},{56,8},{57... | collective-permute-start | bytes 1572872 | tf_op jit(solution)/shard_map/ppermute | solution.py:22
  79.0 21.3 %collective-permute-start.12 = (bf16[16,128,128]{2,1,0:T(8,128)(2,1)S(1)}, bf16[16,128,128]{2,1,0:T(8,128)(2,1)}, u32[]{:S(2)}, u32[]{:S(2)}) collective-permute-start(bf16[16,128,128]{2,1,0:T(8,128)(2,1)S(1)} %collective-permute-done.11.refs_7_), channel_id=1, source_target_pairs={{48,0},{49,1},{50,2},{51,3},{52,4},{53,5},{54,6},{55,7},{56,8},{57... | collective-permute-start | bytes 1572872 | tf_op jit(solution)/shard_map/ppermute | solution.py:22
  84.2 18.0 %collective-permute-start.8 = (bf16[16,128,128]{2,1,0:T(8,128)(2,1)S(1)}, bf16[16,128,128]{2,1,0:T(8,128)(2,1)}, u32[]{:S(2)}, u32[]{:S(2)}) collective-permute-start(bf16[16,128,128]{2,1,0:T(8,128)(2,1)S(1)} %collective-permute-done.7.refs_1_), channel_id=1, source_target_pairs={{16,0},{17,1},{18,2},{19,3},{20,4},{21,5},{22,6},{23,7},{24,8},{25... | collective-permute-start | bytes 1572872 | tf_op jit(solution)/shard_map/ppermute | solution.py:22
  107.1 27.5 %all-to-all-start = ((bf16[64,8,128]{2,1,0:T(8,128)(2,1)}), bf16[64,8,128]{2,1,0:T(8,128)(2,1)}, u32[]{:S(2)}, u32[]{:S(2)}) async-start(bf16[64,8,128]{2,1,0:T(8,128)(2,1)} %bitcast.27), calls=%async_computation | async-start | bytes 262144 | tf_op jit(solution)/shard_map/all_to_all | solution.py:258
  136.5 20.8 %all-to-all-start.1 = ((bf16[64,8,128]{2,1,0:T(8,128)(2,1)}), bf16[64,8,128]{2,1,0:T(8,128)(2,1)S(1)}, u32[]{:S(2)}, u32[]{:S(2)}) async-start(bf16[64,8,128]{2,1,0:T(8,128)(2,1)} %fusion), calls=%async_computation.1 | async-start | bytes 262144 | tf_op jit(solution)/shard_map/all_to_all | solution.py:258
  142.1 90.4 %all-gather.7.cloned.1.call-start = ((), (), s32[]{:S(2)}) async-start(), calls=%async_computation.4 | async-start | bytes 1310720 | tf_op jit(solution)/shard_map/all_gather | solution.py:280
  169.5 9.0 %collective-permute-start.15 = (bf16[4,2,8,64,128]{4,3,2,1,0:T(8,128)(2,1)S(1)}, bf16[4,2,8,64,128]{4,3,2,1,0:T(8,128)(2,1)S(1)}, u32[]{:S(2)}, u32[]{:S(2)}) collective-permute-start(bf16[4,2,8,64,128]{4,3,2,1,0:T(8,128)(2,1)S(1)} %get-tuple-element.36), channel_id=1, source_target_pairs={{64,0},{0,64},{192,128},{128,192},{320,256},{256,320},{448,384},{3... | collective-permute-start | bytes 3145736 | tf_op jit(solution)/shard_map/ppermute | solution.py:31
  171.5 17.4 %collective-permute-start.13 = (bf16[16,128,128]{2,1,0:T(8,128)(2,1)S(1)}, bf16[16,128,128]{2,1,0:T(8,128)(2,1)S(1)}, u32[]{:S(2)}, u32[]{:S(2)}) collective-permute-start(bf16[16,128,128]{2,1,0:T(8,128)(2,1)S(1)} %get-tuple-element.33), channel_id=1, source_target_pairs={{48,0},{49,1},{50,2},{51,3},{52,4},{53,5},{54,6},{55,7},{56,8},{57... | collective-permute-start | bytes 1572872 | tf_op jit(solution)/shard_map/ppermute | solution.py:22
  174.1 16.0 %collective-permute-start.14 = (bf16[16,128,128]{2,1,0:T(8,128)(2,1)S(1)}, bf16[16,128,128]{2,1,0:T(8,128)(2,1)S(1)}, u32[]{:S(2)}, u32[]{:S(2)}) collective-permute-start(bf16[16,128,128]{2,1,0:T(8,128)(2,1)S(1)} %get-tuple-element.34), channel_id=1, source_target_pairs={{16,0},{17,1},{18,2},{19,3},{20,4},{21,5},{22,6},{23,7},{24,8},{25... | collective-permute-start | bytes 1572872 | tf_op jit(solution)/shard_map/ppermute | solution.py:22
  179.0 18.9 %collective-permute-start.19 = (bf16[2,8,64,128]{3,2,1,0:T(8,128)(2,1)S(1)}, bf16[2,8,64,128]{3,2,1,0:T(8,128)(2,1)S(1)}, u32[]{:S(2)}, u32[]{:S(2)}) collective-permute-start(bf16[2,8,64,128]{3,2,1,0:T(8,128)(2,1)S(1)} %pad_maximum_fusion.6), channel_id=1, source_target_pairs={{128,0},{192,64},{256,128},{320,192},{384,256},{448,320},{0,384},{... | collective-permute-start | bytes 786440 | tf_op jit(solution)/shard_map/ppermute | solution.py:27
  181.7 16.2 %collective-permute-start.18 = (bf16[2,8,64,128]{3,2,1,0:T(8,128)(2,1)S(1)}, bf16[2,8,64,128]{3,2,1,0:T(8,128)(2,1)S(1)}, u32[]{:S(2)}, u32[]{:S(2)}) collective-permute-start(bf16[2,8,64,128]{3,2,1,0:T(8,128)(2,1)S(1)} %pad_maximum_fusion.5), channel_id=1, source_target_pairs={{384,0},{448,64},{0,128},{64,192},{128,256},{192,320},{256,384},{3... | collective-permute-start | bytes 786440 | tf_op jit(solution)/shard_map/ppermute | solution.py:27
  190.2 14.9 %collective-permute-start.16 = (bf16[8,128,128]{2,1,0:T(8,128)(2,1)S(1)}, bf16[8,128,128]{2,1,0:T(8,128)(2,1)S(1)}, u32[]{:S(2)}, u32[]{:S(2)}) collective-permute-start(bf16[8,128,128]{2,1,0:T(8,128)(2,1)S(1)} %get-tuple-element.68), channel_id=1, source_target_pairs={{48,0},{49,1},{50,2},{51,3},{52,4},{53,5},{54,6},{55,7},{56,8},{57... | collective-permute-start | bytes 786440 | tf_op jit(solution)/shard_map/ppermute | solution.py:22
  193.6 11.6 %collective-permute-start.17 = (bf16[8,128,128]{2,1,0:T(8,128)(2,1)S(1)}, bf16[8,128,128]{2,1,0:T(8,128)(2,1)S(1)}, u32[]{:S(2)}, u32[]{:S(2)}) collective-permute-start(bf16[8,128,128]{2,1,0:T(8,128)(2,1)S(1)} %get-tuple-element.67), channel_id=1, source_target_pairs={{16,0},{17,1},{18,2},{19,3},{20,4},{21,5},{22,6},{23,7},{24,8},{25... | collective-permute-start | bytes 786440 | tf_op jit(solution)/shard_map/ppermute | solution.py:22
  209.6 30.2 %all-to-all-start.2 = ((bf16[16,128,128]{2,1,0:T(8,128)(2,1)}), bf16[16,128,128]{2,1,0:T(8,128)(2,1)S(1)}, u32[]{:S(2)}, u32[]{:S(2)}) async-start(bf16[16,128,128]{2,1,0:T(8,128)(2,1)} %pad_maximum_fusion.3), calls=%async_computation.2 | async-start | bytes 1048576 | tf_op jit(solution)/shard_map/all_to_all | solution.py:281
  (14 other events, 297.0 us)
Sparse Core Ops, SparseCore 0:
  42.7 24.1 all-gather.4
  209.7 22.6 all-gather.6

commit v2 on v1

--- a/solution.py
+++ b/solution.py
@@ -20,11 +20,6 @@
         (((x + dx) % NX) * NZ + (z + dz) % NZ, x * NZ + z) for x in range(NX) for z in range(NZ)
     ]
     return lax.ppermute(value, "tensor", pairs)
-
-
-def from_y(value, dy):
-    pairs = [(((y + dy) % NY) * 2 + c, y * 2 + c) for y in range(NY) for c in range(2)]
-    return lax.ppermute(value, "dp", pairs)
 
 
 def from_core(value):
@@ -165,16 +160,8 @@
     )(*features, up_dense, down_dense)
 
 
-def backward_kernel(me_ref, z_slot, up_at, up_loc, down_at, down_loc, *refs):
-    xs, dys, (back, slope, up_w) = refs[:4], refs[4:8], refs[8:11]
-    (same, other, near, to_plus, to_minus, later, up_dense, down_dense) = refs[11:]
-    left = left_half()
-    scale = 1.0 / 32.0
-    both = jnp.dot(exchange_order(False), back[...], preferred_element_type=F32)
-    hidden_t = both[:256].astype(BF)
-    dpre_f32 = both[256:].T * slope[...]
-    dpre = dpre_f32.astype(BF)
-    dpre_t = dpre_f32.T.astype(BF)
+def input_kernel(z_slot, dpre_ref, up_w, near, to_plus, to_minus, later):
+    dpre = dpre_ref[...]
 
     def terms(target, z, part):
         w = jnp.concatenate([up_w[part * NZ + z_slot[z + j]] for j in range(2)], axis=1)
@@ -189,6 +176,30 @@
         terms(later, z, 1 if low else 3)
         terms(near, z, 0)
 
+
+def input_terms(z_slot, dpre, up_w):
+    chunk = jax.ShapeDtypeStruct((NZ, 128, 128), BF)
+    return pl.pallas_call(
+        input_kernel,
+        in_specs=[SM] + [VM] * 2,
+        out_specs=[VM] * 4,
+        out_shape=[chunk] * 4,
+        compiler_params=pltpu.CompilerParams(vmem_limit_bytes=20 << 20),
+        cost_estimate=pl.CostEstimate(flops=1 << 29, bytes_accessed=6 << 20, transcendentals=0),
+        name="input_terms",
+    )(z_slot, dpre, up_w)
+
+
+def weight_kernel(up_at, up_loc, down_at, down_loc, *refs):
+    xs, dys = refs[:4], refs[4:8]
+    back, slope, out, dpre_out, up_dense, down_dense = refs[8:]
+    left = left_half()
+    scale = 1.0 / 32.0
+    both = jnp.dot(exchange_order(False), back[...], preferred_element_type=F32)
+    hidden_t = both[:256].astype(BF)
+    dpre = both[256:].T * slope[...]
+    dpre_out[...] = dpre.astype(BF)
+    dpre_t = dpre.T.astype(BF)
     for part in range(4):
 
         def step(i, _, part=part):
@@ -201,47 +212,67 @@
             return 0
 
         lax.fori_loop(0, 8, step, 0, unroll=2)
-    me = me_ref[0]
-    for dc, target in ((0, same), (1, other)):
-
-        def pick(dy, _, dc=dc, target=target):
-            first = ((((me // 2 + dy) % NY) * 2) + (me % 2 + dc) % 2) * 16
-            for p in range(8):
-                for which, at_ref, loc_ref, dense in (
-                    (0, up_at, up_loc, up_dense),
-                    (1, down_at, down_loc, down_dense),
-                ):
-                    sides = []
-                    for side in range(2):
-                        slot = first + side * 8 + p
-                        at, loc = at_ref[slot], loc_ref[slot]
-                        tile = dense[at // 2, pl.ds(pl.multiple_of(loc * BLOCK, BLOCK), BLOCK), :]
-                        sides.append(jnp.where(at % 2 == side, tile, swap_halves(tile)))
-                    target[dy, which, p] = jnp.where(left, sides[0], sides[1])
-            return 0
-
-        lax.fori_loop(0, 4, pick, 0)
-
-
-def backward(me, z_slot, tables, features, back, slope, up_w):
-    shape = jax.ShapeDtypeStruct((4, 2, 8, BLOCK, 128), BF)
-    chunk = jax.ShapeDtypeStruct((NZ, 128, 128), BF)
-    return pl.pallas_call(
-        backward_kernel,
-        in_specs=[SM] * 6 + [VM] * 11,
-        out_specs=[VM] * 6,
-        out_shape=[shape, shape, chunk, chunk, chunk, chunk],
+
+    def pick(device, _):
+        for p in range(8):
+            for which, at_ref, loc_ref, dense in (
+                (0, up_at, up_loc, up_dense),
+                (1, down_at, down_loc, down_dense),
+            ):
+                sides = []
+                for side in range(2):
+                    slot = device * 16 + side * 8 + p
+                    at, loc = at_ref[slot], loc_ref[slot]
+                    tile = dense[at // 2, pl.ds(pl.multiple_of(loc * BLOCK, BLOCK), BLOCK), :]
+                    sides.append(jnp.where(at % 2 == side, tile, swap_halves(tile)))
+                out[device, which, p] = jnp.where(left, sides[0], sides[1])
+        return 0
+
+    lax.fori_loop(0, 8, pick, 0)
+
+
+def weight_terms(tables, features, back, slope):
+    return pl.pallas_call(
+        weight_kernel,
+        in_specs=[SM] * 4 + [VM] * 10,
+        out_specs=[VM, VM],
+        out_shape=[
+            jax.ShapeDtypeStruct((8, 2, 8, BLOCK, 128), BF),
+            jax.ShapeDtypeStruct((128, 256), BF),
+        ],
         scratch_shapes=[pltpu.VMEM((64, 256, 128), BF), pltpu.VMEM((64, 256, 128), BF)],
-        compiler_params=pltpu.CompilerParams(vmem_limit_bytes=32 << 20),
+        compiler_params=pltpu.CompilerParams(vmem_limit_bytes=24 << 20),
         cost_estimate=pl.CostEstimate(flops=3 << 29, bytes_accessed=14 << 20, transcendentals=0),
-        name="backward",
-    )(me, z_slot, *tables, *features, back, slope, up_w)
+        name="weight_terms",
+    )(*tables, *features, back, slope)
+
+
+def pack_kernel(up, down, out):
+    for which, ref in ((0, up), (1, down)):
+        rows = []
+        for at in range(0, BLOCK * BLOCK, 2 * BLOCK):
+            tile = ref[:, at : at + 2 * BLOCK].astype(F32)
+            for side in (slice(0, BLOCK), slice(BLOCK, 2 * BLOCK)):
+                rows.append(jnp.concatenate([tile[:8, side], tile[8:, side]], axis=1))
+        pairs = jnp.swapaxes(jnp.stack(rows), 0, 1)
+        for p in range(8):
+            pair = pairs[p]
+            if which == 0:
+                pair = pair.T
+                pair = jnp.concatenate([pair[:BLOCK], pair[BLOCK:]], axis=1)
+            out[which, p] = pair.astype(BF)
 
 
 def pack(up, down):
-    up = jnp.swapaxes(up.reshape(2, 8, BLOCK, BLOCK), 2, 3)
-    slots = jnp.stack([up, down.reshape(2, 8, BLOCK, BLOCK)])
-    return jnp.concatenate([slots[:, 0], slots[:, 1]], axis=3)
+    return pl.pallas_call(
+        pack_kernel,
+        in_specs=[VM, VM],
+        out_specs=VM,
+        out_shape=jax.ShapeDtypeStruct((2, 8, BLOCK, 2 * BLOCK), BF),
+        compiler_params=pltpu.CompilerParams(vmem_limit_bytes=8 << 20),
+        cost_estimate=pl.CostEstimate(flops=0, bytes_accessed=1 << 19, transcendentals=0),
+        name="pack",
+    )(up, down)
 
 
 def unpack(pairs, turned=False):
@@ -258,40 +289,47 @@
     return lax.all_to_all(rows.reshape(64, 8, 128), "tensor", 0, 0, tiled=True).reshape(512, 128)
 
 
-def reduce_all(same, other, near, to_plus, to_minus, later):
+def place_kernel(me_ref, mine, theirs, parts, up, down, tokens):
+    tokens[...] = jnp.sum(parts[...].astype(F32), axis=0).astype(BF)
+    core = me_ref[0] % 2
+    for y in range(NY):
+        for c in range(2):
+            rows = pl.ds((y * 2 + c) * 16, 16)
+            up[rows] = jnp.where(core == c, mine[y, 0], theirs[y, 0])
+            down[rows] = jnp.where(core == c, mine[y, 1], theirs[y, 1])
+
+
+def place_slots(me, mine, theirs, parts):
+    shape = jax.ShapeDtypeStruct((128, BLOCK * BLOCK), BF)
+    return pl.pallas_call(
+        place_kernel,
+        in_specs=[SM, VM, VM, VM],
+        out_specs=[VM, VM, VM],
+        out_shape=[shape, shape, jax.ShapeDtypeStruct((128, 128), BF)],
+        compiler_params=pltpu.CompilerParams(vmem_limit_bytes=8 << 20),
+        cost_estimate=pl.CostEstimate(flops=0, bytes_accessed=4 << 20, transcendentals=0),
+        name="place_slots",
+    )(me, mine, theirs, parts)
+
+
+def reduce_all(me, slots, near, to_plus, to_minus, later):
     half = NZ // 2
     order = lax.optimization_barrier
     got_plus, got_minus = from_tensor(to_plus, -1, 0), from_tensor(to_minus, 1, 0)
-    total = add(same, from_core(other))
-    y_plus, y_minus = jnp.stack([total[2, 0], total[1, 1]]), jnp.stack([total[2, 1], total[3, 0]])
-    got_plus, got_minus, _, _ = order((got_plus, got_minus, y_plus, y_minus))
+    slots = lax.all_to_all(slots, "dp", 0, 0, tiled=True)
     on_plus, on_minus = add(later[:half], got_plus[:half]), add(later[half:], got_minus[half:])
-    y_plus, y_minus = from_y(y_plus, -1), from_y(y_minus, 1)
     low, high = from_tensor(on_plus, -1, 0), from_tensor(on_minus, 1, 0)
-    y_plus, y_minus, _, _ = order((y_plus, y_minus, on_plus, on_minus))
-    on_down, on_up = add(total[3, 1], y_minus[0]), add(total[1, 0], y_plus[0])
-    low, high, _, _ = order((low, high, on_down, on_up))
-    on_down, on_up = order((from_y(on_down, 1), from_y(on_up, -1)))
-    down = unpack(add(total[0, 1], y_plus[1], on_down))
-    up = unpack(jnp.swapaxes(add(total[0, 0], on_up, y_minus[1]), 1, 2), True)
     low = add(near[:half], low, got_minus[:half])
     high = add(near[half:], got_plus[half:], high)
-    column, own = order((jnp.concatenate([low, high]), jnp.stack([up, down])))
+    column = jnp.concatenate([low, high])
+    slots, _ = order((slots, column))
+    own = jnp.sum(slots.astype(F32), axis=0).astype(BF)
+    own = jnp.stack([unpack(jnp.swapaxes(own[0], 1, 2), True), unpack(own[1])])
+    column, own = order((column, own))
+    parts = lax.all_to_all(column, "tensor", 0, 0, tiled=True, axis_index_groups=Z_GROUPS)
     mine = lax.all_gather(own, "dp", axis=0, axis_index_groups=Y_GROUPS)
-    parts = lax.all_to_all(column, "tensor", 0, 0, tiled=True, axis_index_groups=Z_GROUPS)
-    theirs = from_core(mine)
-    even = lax.axis_index("dp") % 2 == 0
-    up, down = (
-        jnp.stack(
-            [
-                jnp.where(even, mine[:, i], theirs[:, i]),
-                jnp.where(even, theirs[:, i], mine[:, i]),
-            ],
-            axis=1,
-        ).reshape(1, 128, -1)
-        for i in range(2)
-    )
-    return jnp.sum(parts.astype(F32), axis=0).astype(BF), up, down
+    up, down, grad_tokens = place_slots(me, mine, from_core(mine), parts)
+    return grad_tokens, up[None], down[None]
 
 
 def per_device(
@@ -321,11 +359,9 @@
     sent, slope = forward(features, up_dense, down_dense)
     routed = jnp.dot(route, exchange(sent), preferred_element_type=F32).astype(BF)
     back = exchange(routed)
-    me = lax.axis_index("dp").astype(jnp.int32)
-    terms = backward(
-        me.reshape(1), z_slot.astype(jnp.int32), tables, features, back, slope, up_dense
-    )
-    return reduce_all(*terms)
+    me = lax.axis_index("dp").astype(jnp.int32).reshape(1)
+    slots, dpre = weight_terms(tables, features, back, slope)
+    return reduce_all(me, slots, *input_terms(z_slot.astype(jnp.int32), dpre, up_dense))
 
 
 def solution(mesh):

time: 255 us -> 251 us (0.984)
  blocking collectives: 0 us -> 20.6 us
  starting transfers between devices: 107 us -> 89.8 us
  waiting for transfers between devices: 90.6 us -> 85.7 us
  other arithmetic: 8.27 us -> 3.61 us
  Pallas kernels: 19.2 us -> 23.4 us
    all_to_all x0 -> x1, blocking collectives: none -> 20.6 us  [exchange(): lax.all_to_all(rows.reshape(64, 8, 128), 'tensor', 0, 0, tiled=True)]
    all_to_all x2 -> x1, waiting for transfers between devices: 29.9 us -> 14.4 us  [exchange(): lax.all_to_all(rows.reshape(64, 8, 128), 'tensor', 0, 0, tiled=True)]
    ppermute x4 -> x0, starting transfers between devices: 14.1 us -> none  [from_y(): return lax.ppermute(value, 'dp', pairs)]
    ppermute x17, waiting for transfers between devices: 34.6 us -> 46.6 us  [from_tensor(): return lax.ppermute(value, 'tensor', pairs)]
    all_to_all x2 -> x1, starting transfers between devices: 17.6 us -> 11.8 us  [exchange(): lax.all_to_all(rows.reshape(64, 8, 128), 'tensor', 0, 0, tiled=True)]
    all_to_all x0 -> x1, starting transfers between devices: none -> 4.82 us  [reduce_all(): slots = lax.all_to_all(slots, 'dp', 0, 0, tiled=True)]
    pallas_call x1 -> x4, Pallas kernels: 10 us -> 14.3 us  [the longest x1 10.4 us: weight_terms(): pl.pallas_call(weight_kernel, in_specs=[SM] * 4 + [VM] * 10, out_specs=[V...]
    unnamed x25 -> x33, local copies, waits for them, and re-layouts: 3.95 us -> 6.98 us
  transfers between devices with their start and end apart: 28 -> 23, of which waited for: 15 -> 15; matrix products, arithmetic and copies ran while one was open for 1% -> 1% of each run, Pallas kernels for 2% -> 2%
where the time goes in v2:
time: 251 us; the launch traced here: 248 us
  starting transfers between devices  89.8 us (36%)
  waiting for transfers between devices  85.7 us (34%)
  Pallas kernels  23.4 us (9%)
  blocking collectives  20.6 us (8%)
  between operations  14.6 us (6%)
  local copies, waits for them, and re-layouts  9.12 us (4%)
  other arithmetic  3.61 us (1%)
    ppermute x17, starting transfers between devices, from_tensor(): return lax.ppermute(value, 'tensor', pairs)  67.7 us
    ppermute x17, waiting for transfers between devices, from_tensor(): return lax.ppermute(value, 'tensor', pairs)  46.6 us
    all_to_all x1, blocking collectives, exchange(): lax.all_to_all(rows.reshape(64, 8, 128), 'tensor', 0, 0, tiled=True)  20.6 us
    all_gather x1, waiting for transfers between devices, reduce_all(): mine = lax.all_gather(own, 'dp', axis=0, axis_index_groups=Y_GROUPS)  20.2 us
    all_to_all x1, waiting for transfers between devices, exchange(): lax.all_to_all(rows.reshape(64, 8, 128), 'tensor', 0, 0, tiled=True)  14.4 us
    all_to_all x1, starting transfers between devices, exchange(): lax.all_to_all(rows.reshape(64, 8, 128), 'tensor', 0, 0, tiled=True)  11.8 us
    pallas_call x1, Pallas kernels, weight_terms(): pl.pallas_call(weight_kernel, in_specs=[SM] * 4 + [VM] * 10, out_specs=[V...  10.4 us
    unnamed x33, local copies, waits for them, and re-layouts  6.98 us
  transfers between devices with their start and end apart: 23, of which 15 were waited for; matrix products, arithmetic and copies ran while one was open for 1% of the time, Pallas kernels for 2%

profile of v2, /device:TPU:24, one launch (start us, length us, event | category | flops | bytes accessed | tf_op | source)
XLA Modules:
  0.0 248.0 jit_solution(4209357117726088808)
XLA Ops:
  8.1 14.4 %collective-permute-start = (bf16[2,1,128,128]{3,2,1,0:T(8,128)(2,1)S(1)}, bf16[2,1,128,128]{3,2,1,0:T(8,128)(2,1)S(1)}, u32[]{:S(2)}, u32[]{:S(2)}) collective-permute-start(bf16[2,1,128,128]{3,2,1,0:T(8,128)(2,1)S(1)} %maximum_bitcast_fusion), channel_id=1, source_target_pairs={{5,0},{6,1},{7,2},{8,3},{9,4},{10,5},{11,6},{12,7},{13,8},{14,9},{... | collective-permute-start | bytes 196616 | tf_op jit(solution)/shard_map/ppermute | solution.py:22
  24.4 4.3 %collective-permute-done = bf16[2,1,128,128]{3,2,1,0:T(8,128)(2,1)S(1)} collective-permute-done((bf16[2,1,128,128]{3,2,1,0:T(8,128)(2,1)S(1)}, bf16[2,1,128,128]{3,2,1,0:T(8,128)(2,1)S(1)}, u32[]{:S(2)}, u32[]{:S(2)}) %collective-permute-start) | collective-permute-done | bytes 65568 | tf_op jit(solution)/shard_map/ppermute | solution.py:22
  28.6 10.2 %collective-permute-done.1 = bf16[2,1,128,128]{3,2,1,0:T(8,128)(2,1)S(1)} collective-permute-done((bf16[2,1,128,128]{3,2,1,0:T(8,128)(2,1)S(1)}, bf16[2,1,128,128]{3,2,1,0:T(8,128)(2,1)S(1)}, u32[]{:S(2)}, u32[]{:S(2)}) %collective-permute-start.1) | collective-permute-done | bytes 65568 | tf_op jit(solution)/shard_map/ppermute | solution.py:22
  44.2 3.4 %collective-permute-start.3 = (bf16[2,3,128,128]{3,2,1,0:T(8,128)(2,1)S(1)}, bf16[2,3,128,128]{3,2,1,0:T(8,128)(2,1)S(1)}, u32[]{:S(2)}, u32[]{:S(2)}) collective-permute-start(bf16[2,3,128,128]{3,2,1,0:T(8,128)(2,1)S(1)} %pad_maximum_fusion.4), channel_id=1, source_target_pairs={{15,0},{0,1},{1,2},{2,3},{3,4},{4,5},{5,6},{6,7},{7,8},{8,9},{9,10... | collective-permute-start | bytes 589832 | tf_op jit(solution)/shard_map/ppermute | solution.py:22
  50.0 4.4 %collective-permute-start.5 = (bf16[2,3,128,128]{3,2,1,0:T(8,128)(2,1)S(1)}, bf16[2,3,128,128]{3,2,1,0:T(8,128)(2,1)S(1)}, u32[]{:S(2)}, u32[]{:S(2)}) collective-permute-start(bf16[2,3,128,128]{3,2,1,0:T(8,128)(2,1)S(1)} %pad_maximum_fusion.4), channel_id=1, source_target_pairs={{14,0},{15,1},{0,2},{1,3},{2,4},{3,5},{4,6},{5,7},{6,8},{7,9},{8,1... | collective-permute-start | bytes 589832 | tf_op jit(solution)/shard_map/ppermute | solution.py:22
  57.6 5.5 %collective-permute-done.5 = bf16[2,3,128,128]{3,2,1,0:T(8,128)(2,1)S(1)} collective-permute-done((bf16[2,3,128,128]{3,2,1,0:T(8,128)(2,1)S(1)}, bf16[2,3,128,128]{3,2,1,0:T(8,128)(2,1)S(1)}, u32[]{:S(2)}, u32[]{:S(2)}) %collective-permute-start.5) | collective-permute-done | bytes 196640 | tf_op jit(solution)/shard_map/ppermute | solution.py:22
  66.6 3.7 %collective-permute-start.7 = (bf16[16,128,128]{2,1,0:T(8,128)(2,1)S(1)}, bf16[16,128,128]{2,1,0:T(8,128)(2,1)S(1)}, u32[]{:S(2)}, u32[]{:S(2)}) collective-permute-start(bf16[16,128,128]{2,1,0:T(8,128)(2,1)S(1)} %get-tuple-element.66.refs_0_), channel_id=1, source_target_pairs={{16,0},{17,1},{18,2},{19,3},{20,4},{21,5},{22,6},{23,7},{24,8},{25... | collective-permute-start | bytes 1572872 | tf_op jit(solution)/shard_map/ppermute | solution.py:22
  70.5 3.5 %collective-permute-start.10 = (bf16[16,128,128]{2,1,0:T(8,128)(2,1)S(1)}, bf16[16,128,128]{2,1,0:T(8,128)(2,1)S(1)}, u32[]{:S(2)}, u32[]{:S(2)}) collective-permute-start(bf16[16,128,128]{2,1,0:T(8,128)(2,1)S(1)} %get-tuple-element.65.refs_4_), channel_id=1, source_target_pairs={{16,0},{17,1},{18,2},{19,3},{20,4},{21,5},{22,6},{23,7},{24,8},{25... | collective-permute-start | bytes 1572872 | tf_op jit(solution)/shard_map/ppermute | solution.py:22
  83.4 4.9 %collective-permute-start.8 = (bf16[16,128,128]{2,1,0:T(8,128)(2,1)S(1)}, bf16[16,128,128]{2,1,0:T(8,128)(2,1)}, u32[]{:S(2)}, u32[]{:S(2)}) collective-permute-start(bf16[16,128,128]{2,1,0:T(8,128)(2,1)S(1)} %collective-permute-done.7.refs_1_), channel_id=1, source_target_pairs={{16,0},{17,1},{18,2},{19,3},{20,4},{21,5},{22,6},{23,7},{24,8},{25... | collective-permute-start | bytes 1572872 | tf_op jit(solution)/shard_map/ppermute | solution.py:22
  90.0 4.2 %spread_weights.1 = (bf16[64,256,128]{2,1,0:T(8,128)(2,1)S(1)}, bf16[64,256,128]{2,1,0:T(8,128)(2,1)S(1)}) custom-call(s32[128]{0:T(128)S(1)} %fusion.17.up_at, s32[128]{0:T(128)S(1)} %bitcast.112, s32[128]{0:T(128)S(1)} %fusion.18.down_at, s32[128]{0:T(128)S(1)} %bitcast.114, bf16[8,2,8,64,128]{4,3,2,1,0:T(8,128)(2,1)S(1)} %bitcast.106), custom_call_target="tpu_custom_call" | custom-call | bytes 12582912 | tf_op jit(solution)/shard_map/spread_weights/pallas_call | solution.py:101
  94.6 4.8 %collective-permute-done.12.refs_6_ = bf16[16,128,128]{2,1,0:T(8,128)(2,1)} collective-permute-done((bf16[16,128,128]{2,1,0:T(8,128)(2,1)S(1)}, bf16[16,128,128]{2,1,0:T(8,128)(2,1)}, u32[]{:S(2)}, u32[]{:S(2)}) %collective-permute-start.12) | collective-permute-done | bytes 524320 | tf_op jit(solution)/shard_map/ppermute | solution.py:22
  101.4 4.9 %forward.1 = (bf16[512,128]{1,0:T(8,128)(2,1)}, f32[128,256]{1,0:T(8,128)S(1)}) custom-call(bf16[16,128,128]{2,1,0:T(8,128)(2,1)S(1)} %get-tuple-element.66.refs_0_, bf16[16,128,128]{2,1,0:T(8,128)(2,1)S(1)} %collective-permute-done.7.refs_1_, bf16[16,128,128]{2,1,0:T(8,128)(2,1)} %collective-permute-done.8.refs_2_, ...), custom_call_target="tpu_custom_call" | custom-call | flops 1073741824 | bytes 12582912 | tf_op jit(solution)/shard_map/forward/pallas_call | solution.py:149
  106.3 11.8 %all-to-all-start = ((bf16[64,8,128]{2,1,0:T(8,128)(2,1)}), bf16[64,8,128]{2,1,0:T(8,128)(2,1)S(1)}, u32[]{:S(2)}, u32[]{:S(2)}) async-start(bf16[64,8,128]{2,1,0:T(8,128)(2,1)} %bitcast.23), calls=%async_computation | async-start | bytes 262144 | tf_op jit(solution)/shard_map/all_to_all | solution.py:289
  119.3 14.4 %all-to-all-done = bf16[64,8,128]{2,1,0:T(8,128)(2,1)S(1)} async-done(((bf16[64,8,128]{2,1,0:T(8,128)(2,1)}), bf16[64,8,128]{2,1,0:T(8,128)(2,1)S(1)}, u32[]{:S(2)}, u32[]{:S(2)}) %all-to-all-start) | async-done | bytes 131104 | tf_op jit(solution)/shard_map/all_to_all | solution.py:289
  134.7 20.6 %all_to_all.20 = bf16[64,8,128]{2,1,0:T(8,128)(2,1)S(1)} all-to-all(bf16[64,8,128]{2,1,0:T(8,128)(2,1)S(1)} %fusion), channel_id=1, replica_groups=mesh['dp'=8,'tensor'=64] {'tensor'}, dimensions={0} | all-to-all | bytes 262144 | tf_op jit(solution)/shard_map/all_to_all | solution.py:289
  155.3 10.4 %weight_terms.1 = (bf16[8,2,8,64,128]{4,3,2,1,0:T(8,128)(2,1)}, bf16[128,256]{1,0:T(8,128)(2,1)S(1)}) custom-call(s32[128]{0:T(128)S(1)} %fusion.17.up_at, s32[128]{0:T(128)S(1)} %bitcast.113, s32[128]{0:T(128)S(1)} %fusion.18.down_at, s32[128]{0:T(128)S(1)} %bitcast.115, bf16[16,128,128]{2,1,0:T(8,128)(2,1)S(1)} %get-tuple-element.66.refs_0_, ...), custom_call_target="tpu_custom_call" | custom-call | flops 1610612736 | bytes 14680064 | tf_op jit(solution)/shard_map/weight_terms/pallas_call | solution.py:235
  165.8 4.8 %all-to-all-start.2 = ((bf16[8,2,8,64,128]{4,3,2,1,0:T(8,128)(2,1)}), bf16[8,2,8,64,128]{4,3,2,1,0:T(8,128)(2,1)S(1)}, u32[]{:S(2)}, u32[]{:S(2)}) async-start(bf16[8,2,8,64,128]{4,3,2,1,0:T(8,128)(2,1)} %get-tuple-element.32), calls=%async_computation.2 | async-start | bytes 4194304 | tf_op jit(solution)/shard_map/all_to_all | solution.py:319
  176.9 4.4 %collective-permute-start.15 = (bf16[16,128,128]{2,1,0:T(8,128)(2,1)S(1)}, bf16[16,128,128]{2,1,0:T(8,128)(2,1)S(1)}, u32[]{:S(2)}, u32[]{:S(2)}) collective-permute-start(bf16[16,128,128]{2,1,0:T(8,128)(2,1)S(1)} %get-tuple-element.31), channel_id=1, source_target_pairs={{16,0},{17,1},{18,2},{19,3},{20,4},{21,5},{22,6},{23,7},{24,8},{25... | collective-permute-start | bytes 1572872 | tf_op jit(solution)/shard_map/ppermute | solution.py:22
  181.3 10.0 %collective-permute-done.13 = bf16[16,128,128]{2,1,0:T(8,128)(2,1)S(1)} collective-permute-done((bf16[16,128,128]{2,1,0:T(8,128)(2,1)S(1)}, bf16[16,128,128]{2,1,0:T(8,128)(2,1)S(1)}, u32[]{:S(2)}, u32[]{:S(2)}) %collective-permute-start.13) | collective-permute-done | bytes 524320 | tf_op jit(solution)/shard_map/ppermute | solution.py:22
  196.0 4.2 %collective-permute-start.16 = (bf16[8,128,128]{2,1,0:T(8,128)(2,1)S(1)}, bf16[8,128,128]{2,1,0:T(8,128)(2,1)S(1)}, u32[]{:S(2)}, u32[]{:S(2)}) collective-permute-start(bf16[8,128,128]{2,1,0:T(8,128)(2,1)S(1)} %get-tuple-element.48), channel_id=1, source_target_pairs={{16,0},{17,1},{18,2},{19,3},{20,4},{21,5},{22,6},{23,7},{24,8},{25... | collective-permute-start | bytes 786440 | tf_op jit(solution)/shard_map/ppermute | solution.py:22
  200.2 3.5 %collective-permute-done.14 = bf16[8,128,128]{2,1,0:T(8,128)(2,1)S(1)} collective-permute-done((bf16[8,128,128]{2,1,0:T(8,128)(2,1)S(1)}, bf16[8,128,128]{2,1,0:T(8,128)(2,1)S(1)}, u32[]{:S(2)}, u32[]{:S(2)}) %collective-permute-start.14) | collective-permute-done | bytes 262176 | tf_op jit(solution)/shard_map/ppermute | solution.py:22
  208.3 3.6 %all-to-all-start.3 = ((bf16[16,128,128]{2,1,0:T(8,128)(2,1)}), bf16[16,128,128]{2,1,0:T(8,128)(2,1)S(1)}, u32[]{:S(2)}, u32[]{:S(2)}) async-start(bf16[16,128,128]{2,1,0:T(8,128)(2,1)} %pad_maximum_fusion), calls=%async_computation.3 | async-start | bytes 1048576 | tf_op jit(solution)/shard_map/all_to_all | solution.py:329
  211.9 20.2 %all-gather.7.cloned.1.call-done = bf16[8,16,4096]{2,1,0:T(8,128)(2,1)} async-done(((bf16[2,16,4096]{2,1,0:T(8,128)(2,1)}), bf16[8,16,4096]{2,1,0:T(8,128)(2,1)}) %all-gather.7.cloned.1.call-update) | async-done | bytes 1048592 | tf_op jit(solution)/shard_map/all_gather | solution.py:330
  234.1 4.4 %all-to-all-done.3.parts = bf16[16,128,128]{2,1,0:T(8,128)(2,1)S(1)} async-done(((bf16[16,128,128]{2,1,0:T(8,128)(2,1)}), bf16[16,128,128]{2,1,0:T(8,128)(2,1)S(1)}, u32[]{:S(2)}, u32[]{:S(2)}) %all-to-all-start.3) | async-done | bytes 524320 | tf_op jit(solution)/shard_map/all_to_all | solution.py:329
  (97 shorter events, 52.8 us)
Async XLA Ops:
  7.2 81.2 %copy-start.6 = (s32[1,128]{1,0:T(1,128)S(1)}, s32[1,128]{1,0:T(1,128)}, u32[]{:S(2)}) copy-start(s32[1,128]{1,0:T(1,128)} %param.17) | copy-start | bytes 1540
  7.2 81.2 %all-gather.5.cloned.1.call-start = ((), (), s32[]{:S(2)}) async-start(), calls=%async_computation.4 | async-start | bytes 2359296 | tf_op jit(solution)/shard_map/all_gather | solution.py:349
  8.1 20.6 %collective-permute-start = (bf16[2,1,128,128]{3,2,1,0:T(8,128)(2,1)S(1)}, bf16[2,1,128,128]{3,2,1,0:T(8,128)(2,1)S(1)}, u32[]{:S(2)}, u32[]{:S(2)}) collective-permute-start(bf16[2,1,128,128]{3,2,1,0:T(8,128)(2,1)S(1)} %maximum_bitcast_fusion), channel_id=1, source_target_pairs={{5,0},{6,1},{7,2},{8,3},{9,4},{10,5},{11,6},{12,7},{13,8},{14,9},{... | collective-permute-start | bytes 196616 | tf_op jit(solution)/shard_map/ppermute | solution.py:22
  22.4 16.4 %collective-permute-start.1 = (bf16[2,1,128,128]{3,2,1,0:T(8,128)(2,1)S(1)}, bf16[2,1,128,128]{3,2,1,0:T(8,128)(2,1)S(1)}, u32[]{:S(2)}, u32[]{:S(2)}) collective-permute-start(bf16[2,1,128,128]{3,2,1,0:T(8,128)(2,1)S(1)} %maximum_bitcast_fusion), channel_id=1, source_target_pairs={{11,0},{12,1},{13,2},{14,3},{15,4},{0,5},{1,6},{2,7},{3,8},{4,9},{... | collective-permute-start | bytes 196616 | tf_op jit(solution)/shard_map/ppermute | solution.py:22
  41.8 15.7 %collective-permute-start.2 = (bf16[2,3,128,128]{3,2,1,0:T(8,128)(2,1)S(1)}, bf16[2,3,128,128]{3,2,1,0:T(8,128)(2,1)S(1)}, u32[]{:S(2)}, u32[]{:S(2)}) collective-permute-start(bf16[2,3,128,128]{3,2,1,0:T(8,128)(2,1)S(1)} %pad_maximum_fusion.4), channel_id=1, source_target_pairs={{1,0},{2,1},{3,2},{4,3},{5,4},{6,5},{7,6},{8,7},{9,8},{10,9},{11,1... | collective-permute-start | bytes 589832 | tf_op jit(solution)/shard_map/ppermute | solution.py:22
  44.2 13.3 %collective-permute-start.3 = (bf16[2,3,128,128]{3,2,1,0:T(8,128)(2,1)S(1)}, bf16[2,3,128,128]{3,2,1,0:T(8,128)(2,1)S(1)}, u32[]{:S(2)}, u32[]{:S(2)}) collective-permute-start(bf16[2,3,128,128]{3,2,1,0:T(8,128)(2,1)S(1)} %pad_maximum_fusion.4), channel_id=1, source_target_pairs={{15,0},{0,1},{1,2},{2,3},{3,4},{4,5},{5,6},{6,7},{7,8},{8,9},{9,10... | collective-permute-start | bytes 589832 | tf_op jit(solution)/shard_map/ppermute | solution.py:22
  47.7 9.9 %collective-permute-start.4 = (bf16[2,3,128,128]{3,2,1,0:T(8,128)(2,1)S(1)}, bf16[2,3,128,128]{3,2,1,0:T(8,128)(2,1)S(1)}, u32[]{:S(2)}, u32[]{:S(2)}) collective-permute-start(bf16[2,3,128,128]{3,2,1,0:T(8,128)(2,1)S(1)} %pad_maximum_fusion.4), channel_id=1, source_target_pairs={{2,0},{3,1},{4,2},{5,3},{6,4},{7,5},{8,6},{9,7},{10,8},{11,9},{12,... | collective-permute-start | bytes 589832 | tf_op jit(solution)/shard_map/ppermute | solution.py:22
  50.0 13.2 %collective-permute-start.5 = (bf16[2,3,128,128]{3,2,1,0:T(8,128)(2,1)S(1)}, bf16[2,3,128,128]{3,2,1,0:T(8,128)(2,1)S(1)}, u32[]{:S(2)}, u32[]{:S(2)}) collective-permute-start(bf16[2,3,128,128]{3,2,1,0:T(8,128)(2,1)S(1)} %pad_maximum_fusion.4), channel_id=1, source_target_pairs={{14,0},{15,1},{0,2},{1,3},{2,4},{3,5},{4,6},{5,7},{6,8},{7,9},{8,1... | collective-permute-start | bytes 589832 | tf_op jit(solution)/shard_map/ppermute | solution.py:22
  54.4 8.8 %collective-permute-start.6 = (bf16[2,1,128,128]{3,2,1,0:T(8,128)(2,1)S(1)}, bf16[2,1,128,128]{3,2,1,0:T(8,128)(2,1)S(1)}, u32[]{:S(2)}, u32[]{:S(2)}) collective-permute-start(bf16[2,1,128,128]{3,2,1,0:T(8,128)(2,1)S(1)} %collective-permute-done), channel_id=1, source_target_pairs={{3,0},{4,1},{5,2},{6,3},{7,4},{8,5},{9,6},{10,7},{11,8},{12,9},{13... | collective-permute-start | bytes 196616 | tf_op jit(solution)/shard_map/ppermute | solution.py:22
  63.2 14.9 %collective-permute-start.11 = (bf16[16,128,128]{2,1,0:T(8,128)(2,1)S(1)}, bf16[16,128,128]{2,1,0:T(8,128)(2,1)S(1)}, u32[]{:S(2)}, u32[]{:S(2)}) collective-permute-start(bf16[16,128,128]{2,1,0:T(8,128)(2,1)S(1)} %get-tuple-element.65.refs_4_), channel_id=1, source_target_pairs={{48,0},{49,1},{50,2},{51,3},{52,4},{53,5},{54,6},{55,7},{56,8},{57... | collective-permute-start | bytes 1572872 | tf_op jit(solution)/shard_map/ppermute | solution.py:22
  66.6 16.8 %collective-permute-start.7 = (bf16[16,128,128]{2,1,0:T(8,128)(2,1)S(1)}, bf16[16,128,128]{2,1,0:T(8,128)(2,1)S(1)}, u32[]{:S(2)}, u32[]{:S(2)}) collective-permute-start(bf16[16,128,128]{2,1,0:T(8,128)(2,1)S(1)} %get-tuple-element.66.refs_0_), channel_id=1, source_target_pairs={{16,0},{17,1},{18,2},{19,3},{20,4},{21,5},{22,6},{23,7},{24,8},{25... | collective-permute-start | bytes 1572872 | tf_op jit(solution)/shard_map/ppermute | solution.py:22
  70.5 24.1 %collective-permute-start.10 = (bf16[16,128,128]{2,1,0:T(8,128)(2,1)S(1)}, bf16[16,128,128]{2,1,0:T(8,128)(2,1)S(1)}, u32[]{:S(2)}, u32[]{:S(2)}) collective-permute-start(bf16[16,128,128]{2,1,0:T(8,128)(2,1)S(1)} %get-tuple-element.65.refs_4_), channel_id=1, source_target_pairs={{16,0},{17,1},{18,2},{19,3},{20,4},{21,5},{22,6},{23,7},{24,8},{25... | collective-permute-start | bytes 1572872 | tf_op jit(solution)/shard_map/ppermute | solution.py:22
  73.9 20.7 %collective-permute-start.9 = (bf16[16,128,128]{2,1,0:T(8,128)(2,1)S(1)}, bf16[16,128,128]{2,1,0:T(8,128)(2,1)S(1)}, u32[]{:S(2)}, u32[]{:S(2)}) collective-permute-start(bf16[16,128,128]{2,1,0:T(8,128)(2,1)S(1)} %get-tuple-element.66.refs_0_), channel_id=1, source_target_pairs={{48,0},{49,1},{50,2},{51,3},{52,4},{53,5},{54,6},{55,7},{56,8},{57... | collective-permute-start | bytes 1572872 | tf_op jit(solution)/shard_map/ppermute | solution.py:22
  78.2 21.3 %collective-permute-start.12 = (bf16[16,128,128]{2,1,0:T(8,128)(2,1)S(1)}, bf16[16,128,128]{2,1,0:T(8,128)(2,1)}, u32[]{:S(2)}, u32[]{:S(2)}) collective-permute-start(bf16[16,128,128]{2,1,0:T(8,128)(2,1)S(1)} %collective-permute-done.11.refs_7_), channel_id=1, source_target_pairs={{48,0},{49,1},{50,2},{51,3},{52,4},{53,5},{54,6},{55,7},{56,8},{57... | collective-permute-start | bytes 1572872 | tf_op jit(solution)/shard_map/ppermute | solution.py:22
  83.4 18.0 %collective-permute-start.8 = (bf16[16,128,128]{2,1,0:T(8,128)(2,1)S(1)}, bf16[16,128,128]{2,1,0:T(8,128)(2,1)}, u32[]{:S(2)}, u32[]{:S(2)}) collective-permute-start(bf16[16,128,128]{2,1,0:T(8,128)(2,1)S(1)} %collective-permute-done.7.refs_1_), channel_id=1, source_target_pairs={{16,0},{17,1},{18,2},{19,3},{20,4},{21,5},{22,6},{23,7},{24,8},{25... | collective-permute-start | bytes 1572872 | tf_op jit(solution)/shard_map/ppermute | solution.py:22
  106.3 27.4 %all-to-all-start = ((bf16[64,8,128]{2,1,0:T(8,128)(2,1)}), bf16[64,8,128]{2,1,0:T(8,128)(2,1)S(1)}, u32[]{:S(2)}, u32[]{:S(2)}) async-start(bf16[64,8,128]{2,1,0:T(8,128)(2,1)} %bitcast.23), calls=%async_computation | async-start | bytes 262144 | tf_op jit(solution)/shard_map/all_to_all | solution.py:289
  165.8 40.3 %all-to-all-start.2 = ((bf16[8,2,8,64,128]{4,3,2,1,0:T(8,128)(2,1)}), bf16[8,2,8,64,128]{4,3,2,1,0:T(8,128)(2,1)S(1)}, u32[]{:S(2)}, u32[]{:S(2)}) async-start(bf16[8,2,8,64,128]{4,3,2,1,0:T(8,128)(2,1)} %get-tuple-element.32), calls=%async_computation.2 | async-start | bytes 4194304 | tf_op jit(solution)/shard_map/all_to_all | solution.py:319
  170.6 61.5 %all-gather.7.cloned.1.call-start = ((), (), s32[]{:S(2)}) async-start(), calls=%async_computation.5 | async-start | bytes 1310720 | tf_op jit(solution)/shard_map/all_gather | solution.py:330
  174.3 17.1 %collective-permute-start.13 = (bf16[16,128,128]{2,1,0:T(8,128)(2,1)S(1)}, bf16[16,128,128]{2,1,0:T(8,128)(2,1)S(1)}, u32[]{:S(2)}, u32[]{:S(2)}) collective-permute-start(bf16[16,128,128]{2,1,0:T(8,128)(2,1)S(1)} %get-tuple-element.30), channel_id=1, source_target_pairs={{48,0},{49,1},{50,2},{51,3},{52,4},{53,5},{54,6},{55,7},{56,8},{57... | collective-permute-start | bytes 1572872 | tf_op jit(solution)/shard_map/ppermute | solution.py:22
  176.9 15.6 %collective-permute-start.15 = (bf16[16,128,128]{2,1,0:T(8,128)(2,1)S(1)}, bf16[16,128,128]{2,1,0:T(8,128)(2,1)S(1)}, u32[]{:S(2)}, u32[]{:S(2)}) collective-permute-start(bf16[16,128,128]{2,1,0:T(8,128)(2,1)S(1)} %get-tuple-element.31), channel_id=1, source_target_pairs={{16,0},{17,1},{18,2},{19,3},{20,4},{21,5},{22,6},{23,7},{24,8},{25... | collective-permute-start | bytes 1572872 | tf_op jit(solution)/shard_map/ppermute | solution.py:22
  192.7 11.1 %collective-permute-start.14 = (bf16[8,128,128]{2,1,0:T(8,128)(2,1)S(1)}, bf16[8,128,128]{2,1,0:T(8,128)(2,1)S(1)}, u32[]{:S(2)}, u32[]{:S(2)}) collective-permute-start(bf16[8,128,128]{2,1,0:T(8,128)(2,1)S(1)} %get-tuple-element.47), channel_id=1, source_target_pairs={{48,0},{49,1},{50,2},{51,3},{52,4},{53,5},{54,6},{55,7},{56,8},{57... | collective-permute-start | bytes 786440 | tf_op jit(solution)/shard_map/ppermute | solution.py:22
  196.0 8.9 %collective-permute-start.16 = (bf16[8,128,128]{2,1,0:T(8,128)(2,1)S(1)}, bf16[8,128,128]{2,1,0:T(8,128)(2,1)S(1)}, u32[]{:S(2)}, u32[]{:S(2)}) collective-permute-start(bf16[8,128,128]{2,1,0:T(8,128)(2,1)S(1)} %get-tuple-element.48), channel_id=1, source_target_pairs={{16,0},{17,1},{18,2},{19,3},{20,4},{21,5},{22,6},{23,7},{24,8},{25... | collective-permute-start | bytes 786440 | tf_op jit(solution)/shard_map/ppermute | solution.py:22
  208.3 30.1 %all-to-all-start.3 = ((bf16[16,128,128]{2,1,0:T(8,128)(2,1)}), bf16[16,128,128]{2,1,0:T(8,128)(2,1)S(1)}, u32[]{:S(2)}, u32[]{:S(2)}) async-start(bf16[16,128,128]{2,1,0:T(8,128)(2,1)} %pad_maximum_fusion), calls=%async_computation.3 | async-start | bytes 1048576 | tf_op jit(solution)/shard_map/all_to_all | solution.py:329
  232.1 6.3 %collective-permute-start.17 = (bf16[4,2,16,4096]{3,2,1,0:T(8,128)(2,1)}, bf16[4,2,16,4096]{3,2,1,0:T(8,128)(2,1)S(1)}, u32[]{:S(2)}, u32[]{:S(2)}) collective-permute-start(bf16[4,2,16,4096]{3,2,1,0:T(8,128)(2,1)} %bitcast.107), channel_id=1, source_target_pairs={{64,0},{0,64},{192,128},{128,192},{320,256},{256,320},{448,384},{3... | collective-permute-start | bytes 3145736 | tf_op jit(solution)/shard_map/ppermute | solution.py:26
  (13 other events, 392.4 us)
Sparse Core Ops, SparseCore 0:
  41.9 24.1 all-gather.4
  208.4 23.6 all-gather.6

commit v3 on v2

--- a/solution.py
+++ b/solution.py
@@ -241,13 +241,14 @@
             jax.ShapeDtypeStruct((128, 256), BF),
         ],
         scratch_shapes=[pltpu.VMEM((64, 256, 128), BF), pltpu.VMEM((64, 256, 128), BF)],
-        compiler_params=pltpu.CompilerParams(vmem_limit_bytes=24 << 20),
+        compiler_params=pltpu.CompilerParams(vmem_limit_bytes=18 << 20),
         cost_estimate=pl.CostEstimate(flops=3 << 29, bytes_accessed=14 << 20, transcendentals=0),
         name="weight_terms",
     )(*tables, *features, back, slope)
 
 
-def pack_kernel(up, down, out):
+def pack_kernel(up, down, first, second, out):
+    del first, second
     for which, ref in ((0, up), (1, down)):
         rows = []
         for at in range(0, BLOCK * BLOCK, 2 * BLOCK):
@@ -263,16 +264,16 @@
             out[which, p] = pair.astype(BF)
 
 
-def pack(up, down):
+def pack(up, down, first, second):
     return pl.pallas_call(
         pack_kernel,
-        in_specs=[VM, VM],
+        in_specs=[VM, VM] + [pl.BlockSpec(memory_space=pl.ANY)] * 2,
         out_specs=VM,
         out_shape=jax.ShapeDtypeStruct((2, 8, BLOCK, 2 * BLOCK), BF),
         compiler_params=pltpu.CompilerParams(vmem_limit_bytes=8 << 20),
         cost_estimate=pl.CostEstimate(flops=0, bytes_accessed=1 << 19, transcendentals=0),
         name="pack",
-    )(up, down)
+    )(up, down, first, second)
 
 
 def unpack(pairs, turned=False):
@@ -306,7 +307,7 @@
         in_specs=[SM, VM, VM, VM],
         out_specs=[VM, VM, VM],
         out_shape=[shape, shape, jax.ShapeDtypeStruct((128, 128), BF)],
-        compiler_params=pltpu.CompilerParams(vmem_limit_bytes=8 << 20),
+        compiler_params=pltpu.CompilerParams(vmem_limit_bytes=48 << 20),
         cost_estimate=pl.CostEstimate(flops=0, bytes_accessed=4 << 20, transcendentals=0),
         name="place_slots",
     )(me, mine, theirs, parts)
@@ -345,8 +346,7 @@
     down_perm,
 ):
     features, first = gather_features(tokens, grad_out)
-    up_own, down_own, *_ = lax.optimization_barrier((up_weight[0], down_weight[0], *first))
-    pairs = lax.all_gather(pack(up_own, down_own), "dp", axis=0)
+    pairs = lax.all_gather(pack(up_weight[0], down_weight[0], *first), "dp", axis=0)
     tables = (block_place(up_col[0]), up_local[0], block_place(down_col[0]), down_local[0])
     up4, down4 = up_perm.reshape(-1, HPD), down_perm.reshape(-1, HPD)
     wanted = jnp.stack([down4, up4 + 256], axis=1).reshape(-1)

time: 251 us -> 251 us (level)
  no operation moved by 1% of the time
where the time goes in v3:
time: 251 us; the launch traced here: 248 us
  starting transfers between devices  89.8 us (36%)
  waiting for transfers between devices  85.7 us (34%)
  Pallas kernels  23.5 us (9%)
  blocking collectives  20.6 us (8%)
  between operations  14.6 us (6%)
  local copies, waits for them, and re-layouts  9.12 us (4%)
  other arithmetic  3.61 us (1%)
    ppermute x17, starting transfers between devices, from_tensor(): return lax.ppermute(value, 'tensor', pairs)  67.7 us
    ppermute x17, waiting for transfers between devices, from_tensor(): return lax.ppermute(value, 'tensor', pairs)  46.6 us
    all_to_all x1, blocking collectives, exchange(): lax.all_to_all(rows.reshape(64, 8, 128), 'tensor', 0, 0, tiled=True)  20.6 us
    all_gather x1, waiting for transfers between devices, reduce_all(): mine = lax.all_gather(own, 'dp', axis=0, axis_index_groups=Y_GROUPS)  20.2 us
    all_to_all x1, waiting for transfers between devices, exchange(): lax.all_to_all(rows.reshape(64, 8, 128), 'tensor', 0, 0, tiled=True)  14.4 us
    all_to_all x1, starting transfers between devices, exchange(): lax.all_to_all(rows.reshape(64, 8, 128), 'tensor', 0, 0, tiled=True)  11.8 us
    pallas_call x1, Pallas kernels, weight_terms(): pl.pallas_call(weight_kernel, in_specs=[SM] * 4 + [VM] * 10, out_specs=[V...  10.4 us
    unnamed x33, local copies, waits for them, and re-layouts  6.98 us
  transfers between devices with their start and end apart: 23, of which 15 were waited for; matrix products, arithmetic and copies ran while one was open for 1% of the time, Pallas kernels for 2%

profile of v3, /device:TPU:24, one launch (start us, length us, event | category | flops | bytes accessed | tf_op | source)
XLA Modules:
  0.0 247.9 jit_solution(11541904561837933285)
XLA Ops:
  8.1 14.4 %collective-permute-start = (bf16[2,1,128,128]{3,2,1,0:T(8,128)(2,1)S(1)}, bf16[2,1,128,128]{3,2,1,0:T(8,128)(2,1)S(1)}, u32[]{:S(2)}, u32[]{:S(2)}) collective-permute-start(bf16[2,1,128,128]{3,2,1,0:T(8,128)(2,1)S(1)} %maximum_bitcast_fusion), channel_id=1, source_target_pairs={{5,0},{6,1},{7,2},{8,3},{9,4},{10,5},{11,6},{12,7},{13,8},{14,9},{... | collective-permute-start | bytes 196616 | tf_op jit(solution)/shard_map/ppermute | solution.py:22
  24.4 4.3 %collective-permute-done.first = bf16[2,1,128,128]{3,2,1,0:T(8,128)(2,1)S(1)} collective-permute-done((bf16[2,1,128,128]{3,2,1,0:T(8,128)(2,1)S(1)}, bf16[2,1,128,128]{3,2,1,0:T(8,128)(2,1)S(1)}, u32[]{:S(2)}, u32[]{:S(2)}) %collective-permute-start) | collective-permute-done | bytes 65568 | tf_op jit(solution)/shard_map/ppermute | solution.py:22
  28.6 10.2 %collective-permute-done.1.second = bf16[2,1,128,128]{3,2,1,0:T(8,128)(2,1)S(1)} collective-permute-done((bf16[2,1,128,128]{3,2,1,0:T(8,128)(2,1)S(1)}, bf16[2,1,128,128]{3,2,1,0:T(8,128)(2,1)S(1)}, u32[]{:S(2)}, u32[]{:S(2)}) %collective-permute-start.1) | collective-permute-done | bytes 65568 | tf_op jit(solution)/shard_map/ppermute | solution.py:22
  44.2 3.4 %collective-permute-start.3 = (bf16[2,3,128,128]{3,2,1,0:T(8,128)(2,1)S(1)}, bf16[2,3,128,128]{3,2,1,0:T(8,128)(2,1)S(1)}, u32[]{:S(2)}, u32[]{:S(2)}) collective-permute-start(bf16[2,3,128,128]{3,2,1,0:T(8,128)(2,1)S(1)} %pad_maximum_fusion.4), channel_id=1, source_target_pairs={{15,0},{0,1},{1,2},{2,3},{3,4},{4,5},{5,6},{6,7},{7,8},{8,9},{9,10... | collective-permute-start | bytes 589832 | tf_op jit(solution)/shard_map/ppermute | solution.py:22
  50.0 4.4 %collective-permute-start.5 = (bf16[2,3,128,128]{3,2,1,0:T(8,128)(2,1)S(1)}, bf16[2,3,128,128]{3,2,1,0:T(8,128)(2,1)S(1)}, u32[]{:S(2)}, u32[]{:S(2)}) collective-permute-start(bf16[2,3,128,128]{3,2,1,0:T(8,128)(2,1)S(1)} %pad_maximum_fusion.4), channel_id=1, source_target_pairs={{14,0},{15,1},{0,2},{1,3},{2,4},{3,5},{4,6},{5,7},{6,8},{7,9},{8,1... | collective-permute-start | bytes 589832 | tf_op jit(solution)/shard_map/ppermute | solution.py:22
  57.6 5.5 %collective-permute-done.5 = bf16[2,3,128,128]{3,2,1,0:T(8,128)(2,1)S(1)} collective-permute-done((bf16[2,3,128,128]{3,2,1,0:T(8,128)(2,1)S(1)}, bf16[2,3,128,128]{3,2,1,0:T(8,128)(2,1)S(1)}, u32[]{:S(2)}, u32[]{:S(2)}) %collective-permute-start.5) | collective-permute-done | bytes 196640 | tf_op jit(solution)/shard_map/ppermute | solution.py:22
  66.6 3.7 %collective-permute-start.7 = (bf16[16,128,128]{2,1,0:T(8,128)(2,1)S(1)}, bf16[16,128,128]{2,1,0:T(8,128)(2,1)S(1)}, u32[]{:S(2)}, u32[]{:S(2)}) collective-permute-start(bf16[16,128,128]{2,1,0:T(8,128)(2,1)S(1)} %get-tuple-element.62.refs_0_), channel_id=1, source_target_pairs={{16,0},{17,1},{18,2},{19,3},{20,4},{21,5},{22,6},{23,7},{24,8},{25... | collective-permute-start | bytes 1572872 | tf_op jit(solution)/shard_map/ppermute | solution.py:22
  70.5 3.5 %collective-permute-start.10 = (bf16[16,128,128]{2,1,0:T(8,128)(2,1)S(1)}, bf16[16,128,128]{2,1,0:T(8,128)(2,1)S(1)}, u32[]{:S(2)}, u32[]{:S(2)}) collective-permute-start(bf16[16,128,128]{2,1,0:T(8,128)(2,1)S(1)} %get-tuple-element.61.refs_4_), channel_id=1, source_target_pairs={{16,0},{17,1},{18,2},{19,3},{20,4},{21,5},{22,6},{23,7},{24,8},{25... | collective-permute-start | bytes 1572872 | tf_op jit(solution)/shard_map/ppermute | solution.py:22
  83.4 4.9 %collective-permute-start.8 = (bf16[16,128,128]{2,1,0:T(8,128)(2,1)S(1)}, bf16[16,128,128]{2,1,0:T(8,128)(2,1)}, u32[]{:S(2)}, u32[]{:S(2)}) collective-permute-start(bf16[16,128,128]{2,1,0:T(8,128)(2,1)S(1)} %collective-permute-done.7.refs_1_), channel_id=1, source_target_pairs={{16,0},{17,1},{18,2},{19,3},{20,4},{21,5},{22,6},{23,7},{24,8},{25... | collective-permute-start | bytes 1572872 | tf_op jit(solution)/shard_map/ppermute | solution.py:22
  90.0 4.2 %spread_weights.1 = (bf16[64,256,128]{2,1,0:T(8,128)(2,1)S(1)}, bf16[64,256,128]{2,1,0:T(8,128)(2,1)S(1)}) custom-call(s32[128]{0:T(128)S(1)} %fusion.17.up_at, s32[128]{0:T(128)S(1)} %bitcast.112, s32[128]{0:T(128)S(1)} %fusion.18.down_at, s32[128]{0:T(128)S(1)} %bitcast.114, bf16[8,2,8,64,128]{4,3,2,1,0:T(8,128)(2,1)S(1)} %bitcast.106), custom_call_target="tpu_custom_call" | custom-call | bytes 12582912 | tf_op jit(solution)/shard_map/spread_weights/pallas_call | solution.py:101
  94.6 4.8 %collective-permute-done.12.refs_6_ = bf16[16,128,128]{2,1,0:T(8,128)(2,1)} collective-permute-done((bf16[16,128,128]{2,1,0:T(8,128)(2,1)S(1)}, bf16[16,128,128]{2,1,0:T(8,128)(2,1)}, u32[]{:S(2)}, u32[]{:S(2)}) %collective-permute-start.12) | collective-permute-done | bytes 524320 | tf_op jit(solution)/shard_map/ppermute | solution.py:22
  101.4 4.9 %forward.1 = (bf16[512,128]{1,0:T(8,128)(2,1)}, f32[128,256]{1,0:T(8,128)S(1)}) custom-call(bf16[16,128,128]{2,1,0:T(8,128)(2,1)S(1)} %get-tuple-element.62.refs_0_, bf16[16,128,128]{2,1,0:T(8,128)(2,1)S(1)} %collective-permute-done.7.refs_1_, bf16[16,128,128]{2,1,0:T(8,128)(2,1)} %collective-permute-done.8.refs_2_, ...), custom_call_target="tpu_custom_call" | custom-call | flops 1073741824 | bytes 12582912 | tf_op jit(solution)/shard_map/forward/pallas_call | solution.py:149
  106.3 11.8 %all-to-all-start = ((bf16[64,8,128]{2,1,0:T(8,128)(2,1)}), bf16[64,8,128]{2,1,0:T(8,128)(2,1)S(1)}, u32[]{:S(2)}, u32[]{:S(2)}) async-start(bf16[64,8,128]{2,1,0:T(8,128)(2,1)} %bitcast.23), calls=%async_computation | async-start | bytes 262144 | tf_op jit(solution)/shard_map/all_to_all | solution.py:290
  119.3 14.4 %all-to-all-done = bf16[64,8,128]{2,1,0:T(8,128)(2,1)S(1)} async-done(((bf16[64,8,128]{2,1,0:T(8,128)(2,1)}), bf16[64,8,128]{2,1,0:T(8,128)(2,1)S(1)}, u32[]{:S(2)}, u32[]{:S(2)}) %all-to-all-start) | async-done | bytes 131104 | tf_op jit(solution)/shard_map/all_to_all | solution.py:290
  134.7 20.6 %all_to_all.20 = bf16[64,8,128]{2,1,0:T(8,128)(2,1)S(1)} all-to-all(bf16[64,8,128]{2,1,0:T(8,128)(2,1)S(1)} %fusion), channel_id=1, replica_groups=mesh['dp'=8,'tensor'=64] {'tensor'}, dimensions={0} | all-to-all | bytes 262144 | tf_op jit(solution)/shard_map/all_to_all | solution.py:290
  155.3 10.4 %weight_terms.1 = (bf16[8,2,8,64,128]{4,3,2,1,0:T(8,128)(2,1)}, bf16[128,256]{1,0:T(8,128)(2,1)S(1)}) custom-call(s32[128]{0:T(128)S(1)} %fusion.17.up_at, s32[128]{0:T(128)S(1)} %bitcast.113, s32[128]{0:T(128)S(1)} %fusion.18.down_at, s32[128]{0:T(128)S(1)} %bitcast.115, bf16[16,128,128]{2,1,0:T(8,128)(2,1)S(1)} %get-tuple-element.62.refs_0_, ...), custom_call_target="tpu_custom_call" | custom-call | flops 1610612736 | bytes 14680064 | tf_op jit(solution)/shard_map/weight_terms/pallas_call | solution.py:235
  165.8 4.8 %all-to-all-start.2 = ((bf16[8,2,8,64,128]{4,3,2,1,0:T(8,128)(2,1)}), bf16[8,2,8,64,128]{4,3,2,1,0:T(8,128)(2,1)S(1)}, u32[]{:S(2)}, u32[]{:S(2)}) async-start(bf16[8,2,8,64,128]{4,3,2,1,0:T(8,128)(2,1)} %get-tuple-element.28), calls=%async_computation.2 | async-start | bytes 4194304 | tf_op jit(solution)/shard_map/all_to_all | solution.py:320
  176.9 4.4 %collective-permute-start.15 = (bf16[16,128,128]{2,1,0:T(8,128)(2,1)S(1)}, bf16[16,128,128]{2,1,0:T(8,128)(2,1)S(1)}, u32[]{:S(2)}, u32[]{:S(2)}) collective-permute-start(bf16[16,128,128]{2,1,0:T(8,128)(2,1)S(1)} %get-tuple-element.27), channel_id=1, source_target_pairs={{16,0},{17,1},{18,2},{19,3},{20,4},{21,5},{22,6},{23,7},{24,8},{25... | collective-permute-start | bytes 1572872 | tf_op jit(solution)/shard_map/ppermute | solution.py:22
  181.4 10.0 %collective-permute-done.13 = bf16[16,128,128]{2,1,0:T(8,128)(2,1)S(1)} collective-permute-done((bf16[16,128,128]{2,1,0:T(8,128)(2,1)S(1)}, bf16[16,128,128]{2,1,0:T(8,128)(2,1)S(1)}, u32[]{:S(2)}, u32[]{:S(2)}) %collective-permute-start.13) | collective-permute-done | bytes 524320 | tf_op jit(solution)/shard_map/ppermute | solution.py:22
  196.0 4.2 %collective-permute-start.16 = (bf16[8,128,128]{2,1,0:T(8,128)(2,1)S(1)}, bf16[8,128,128]{2,1,0:T(8,128)(2,1)S(1)}, u32[]{:S(2)}, u32[]{:S(2)}) collective-permute-start(bf16[8,128,128]{2,1,0:T(8,128)(2,1)S(1)} %get-tuple-element.44), channel_id=1, source_target_pairs={{16,0},{17,1},{18,2},{19,3},{20,4},{21,5},{22,6},{23,7},{24,8},{25... | collective-permute-start | bytes 786440 | tf_op jit(solution)/shard_map/ppermute | solution.py:22
  200.2 3.5 %collective-permute-done.14 = bf16[8,128,128]{2,1,0:T(8,128)(2,1)S(1)} collective-permute-done((bf16[8,128,128]{2,1,0:T(8,128)(2,1)S(1)}, bf16[8,128,128]{2,1,0:T(8,128)(2,1)S(1)}, u32[]{:S(2)}, u32[]{:S(2)}) %collective-permute-start.14) | collective-permute-done | bytes 262176 | tf_op jit(solution)/shard_map/ppermute | solution.py:22
  208.3 3.6 %all-to-all-start.3 = ((bf16[16,128,128]{2,1,0:T(8,128)(2,1)}), bf16[16,128,128]{2,1,0:T(8,128)(2,1)S(1)}, u32[]{:S(2)}, u32[]{:S(2)}) async-start(bf16[16,128,128]{2,1,0:T(8,128)(2,1)} %pad_maximum_fusion), calls=%async_computation.3 | async-start | bytes 1048576 | tf_op jit(solution)/shard_map/all_to_all | solution.py:330
  211.9 20.2 %all-gather.7.cloned.1.call-done = bf16[8,16,4096]{2,1,0:T(8,128)(2,1)} async-done(((bf16[2,16,4096]{2,1,0:T(8,128)(2,1)}), bf16[8,16,4096]{2,1,0:T(8,128)(2,1)}) %all-gather.7.cloned.1.call-update) | async-done | bytes 1048592 | tf_op jit(solution)/shard_map/all_gather | solution.py:331
  234.1 4.4 %all-to-all-done.3.parts = bf16[16,128,128]{2,1,0:T(8,128)(2,1)S(1)} async-done(((bf16[16,128,128]{2,1,0:T(8,128)(2,1)}), bf16[16,128,128]{2,1,0:T(8,128)(2,1)S(1)}, u32[]{:S(2)}, u32[]{:S(2)}) %all-to-all-start.3) | async-done | bytes 524320 | tf_op jit(solution)/shard_map/all_to_all | solution.py:330
  (97 shorter events, 52.7 us)
Async XLA Ops:
  7.2 81.2 %copy-start.6 = (s32[1,128]{1,0:T(1,128)S(1)}, s32[1,128]{1,0:T(1,128)}, u32[]{:S(2)}) copy-start(s32[1,128]{1,0:T(1,128)} %param.17) | copy-start | bytes 1540
  7.2 81.2 %all-gather.5.cloned.1.call-start = ((), (), s32[]{:S(2)}) async-start(), calls=%async_computation.4 | async-start | bytes 2359296 | tf_op jit(solution)/shard_map/all_gather | solution.py:349
  8.1 20.6 %collective-permute-start = (bf16[2,1,128,128]{3,2,1,0:T(8,128)(2,1)S(1)}, bf16[2,1,128,128]{3,2,1,0:T(8,128)(2,1)S(1)}, u32[]{:S(2)}, u32[]{:S(2)}) collective-permute-start(bf16[2,1,128,128]{3,2,1,0:T(8,128)(2,1)S(1)} %maximum_bitcast_fusion), channel_id=1, source_target_pairs={{5,0},{6,1},{7,2},{8,3},{9,4},{10,5},{11,6},{12,7},{13,8},{14,9},{... | collective-permute-start | bytes 196616 | tf_op jit(solution)/shard_map/ppermute | solution.py:22
  22.4 16.4 %collective-permute-start.1 = (bf16[2,1,128,128]{3,2,1,0:T(8,128)(2,1)S(1)}, bf16[2,1,128,128]{3,2,1,0:T(8,128)(2,1)S(1)}, u32[]{:S(2)}, u32[]{:S(2)}) collective-permute-start(bf16[2,1,128,128]{3,2,1,0:T(8,128)(2,1)S(1)} %maximum_bitcast_fusion), channel_id=1, source_target_pairs={{11,0},{12,1},{13,2},{14,3},{15,4},{0,5},{1,6},{2,7},{3,8},{4,9},{... | collective-permute-start | bytes 196616 | tf_op jit(solution)/shard_map/ppermute | solution.py:22
  41.8 15.7 %collective-permute-start.2 = (bf16[2,3,128,128]{3,2,1,0:T(8,128)(2,1)S(1)}, bf16[2,3,128,128]{3,2,1,0:T(8,128)(2,1)S(1)}, u32[]{:S(2)}, u32[]{:S(2)}) collective-permute-start(bf16[2,3,128,128]{3,2,1,0:T(8,128)(2,1)S(1)} %pad_maximum_fusion.4), channel_id=1, source_target_pairs={{1,0},{2,1},{3,2},{4,3},{5,4},{6,5},{7,6},{8,7},{9,8},{10,9},{11,1... | collective-permute-start | bytes 589832 | tf_op jit(solution)/shard_map/ppermute | solution.py:22
  44.2 13.3 %collective-permute-start.3 = (bf16[2,3,128,128]{3,2,1,0:T(8,128)(2,1)S(1)}, bf16[2,3,128,128]{3,2,1,0:T(8,128)(2,1)S(1)}, u32[]{:S(2)}, u32[]{:S(2)}) collective-permute-start(bf16[2,3,128,128]{3,2,1,0:T(8,128)(2,1)S(1)} %pad_maximum_fusion.4), channel_id=1, source_target_pairs={{15,0},{0,1},{1,2},{2,3},{3,4},{4,5},{5,6},{6,7},{7,8},{8,9},{9,10... | collective-permute-start | bytes 589832 | tf_op jit(solution)/shard_map/ppermute | solution.py:22
  47.7 9.9 %collective-permute-start.4 = (bf16[2,3,128,128]{3,2,1,0:T(8,128)(2,1)S(1)}, bf16[2,3,128,128]{3,2,1,0:T(8,128)(2,1)S(1)}, u32[]{:S(2)}, u32[]{:S(2)}) collective-permute-start(bf16[2,3,128,128]{3,2,1,0:T(8,128)(2,1)S(1)} %pad_maximum_fusion.4), channel_id=1, source_target_pairs={{2,0},{3,1},{4,2},{5,3},{6,4},{7,5},{8,6},{9,7},{10,8},{11,9},{12,... | collective-permute-start | bytes 589832 | tf_op jit(solution)/shard_map/ppermute | solution.py:22
  50.0 13.2 %collective-permute-start.5 = (bf16[2,3,128,128]{3,2,1,0:T(8,128)(2,1)S(1)}, bf16[2,3,128,128]{3,2,1,0:T(8,128)(2,1)S(1)}, u32[]{:S(2)}, u32[]{:S(2)}) collective-permute-start(bf16[2,3,128,128]{3,2,1,0:T(8,128)(2,1)S(1)} %pad_maximum_fusion.4), channel_id=1, source_target_pairs={{14,0},{15,1},{0,2},{1,3},{2,4},{3,5},{4,6},{5,7},{6,8},{7,9},{8,1... | collective-permute-start | bytes 589832 | tf_op jit(solution)/shard_map/ppermute | solution.py:22
  54.4 8.8 %collective-permute-start.6 = (bf16[2,1,128,128]{3,2,1,0:T(8,128)(2,1)S(1)}, bf16[2,1,128,128]{3,2,1,0:T(8,128)(2,1)S(1)}, u32[]{:S(2)}, u32[]{:S(2)}) collective-permute-start(bf16[2,1,128,128]{3,2,1,0:T(8,128)(2,1)S(1)} %collective-permute-done.first), channel_id=1, source_target_pairs={{3,0},{4,1},{5,2},{6,3},{7,4},{8,5},{9,6},{10,7},{11,8},{12,9},{13... | collective-permute-start | bytes 196616 | tf_op jit(solution)/shard_map/ppermute | solution.py:22
  63.2 14.9 %collective-permute-start.11 = (bf16[16,128,128]{2,1,0:T(8,128)(2,1)S(1)}, bf16[16,128,128]{2,1,0:T(8,128)(2,1)S(1)}, u32[]{:S(2)}, u32[]{:S(2)}) collective-permute-start(bf16[16,128,128]{2,1,0:T(8,128)(2,1)S(1)} %get-tuple-element.61.refs_4_), channel_id=1, source_target_pairs={{48,0},{49,1},{50,2},{51,3},{52,4},{53,5},{54,6},{55,7},{56,8},{57... | collective-permute-start | bytes 1572872 | tf_op jit(solution)/shard_map/ppermute | solution.py:22
  66.6 16.8 %collective-permute-start.7 = (bf16[16,128,128]{2,1,0:T(8,128)(2,1)S(1)}, bf16[16,128,128]{2,1,0:T(8,128)(2,1)S(1)}, u32[]{:S(2)}, u32[]{:S(2)}) collective-permute-start(bf16[16,128,128]{2,1,0:T(8,128)(2,1)S(1)} %get-tuple-element.62.refs_0_), channel_id=1, source_target_pairs={{16,0},{17,1},{18,2},{19,3},{20,4},{21,5},{22,6},{23,7},{24,8},{25... | collective-permute-start | bytes 1572872 | tf_op jit(solution)/shard_map/ppermute | solution.py:22
  70.5 24.1 %collective-permute-start.10 = (bf16[16,128,128]{2,1,0:T(8,128)(2,1)S(1)}, bf16[16,128,128]{2,1,0:T(8,128)(2,1)S(1)}, u32[]{:S(2)}, u32[]{:S(2)}) collective-permute-start(bf16[16,128,128]{2,1,0:T(8,128)(2,1)S(1)} %get-tuple-element.61.refs_4_), channel_id=1, source_target_pairs={{16,0},{17,1},{18,2},{19,3},{20,4},{21,5},{22,6},{23,7},{24,8},{25... | collective-permute-start | bytes 1572872 | tf_op jit(solution)/shard_map/ppermute | solution.py:22
  73.9 20.7 %collective-permute-start.9 = (bf16[16,128,128]{2,1,0:T(8,128)(2,1)S(1)}, bf16[16,128,128]{2,1,0:T(8,128)(2,1)S(1)}, u32[]{:S(2)}, u32[]{:S(2)}) collective-permute-start(bf16[16,128,128]{2,1,0:T(8,128)(2,1)S(1)} %get-tuple-element.62.refs_0_), channel_id=1, source_target_pairs={{48,0},{49,1},{50,2},{51,3},{52,4},{53,5},{54,6},{55,7},{56,8},{57... | collective-permute-start | bytes 1572872 | tf_op jit(solution)/shard_map/ppermute | solution.py:22
  78.2 21.3 %collective-permute-start.12 = (bf16[16,128,128]{2,1,0:T(8,128)(2,1)S(1)}, bf16[16,128,128]{2,1,0:T(8,128)(2,1)}, u32[]{:S(2)}, u32[]{:S(2)}) collective-permute-start(bf16[16,128,128]{2,1,0:T(8,128)(2,1)S(1)} %collective-permute-done.11.refs_7_), channel_id=1, source_target_pairs={{48,0},{49,1},{50,2},{51,3},{52,4},{53,5},{54,6},{55,7},{56,8},{57... | collective-permute-start | bytes 1572872 | tf_op jit(solution)/shard_map/ppermute | solution.py:22
  83.4 18.0 %collective-permute-start.8 = (bf16[16,128,128]{2,1,0:T(8,128)(2,1)S(1)}, bf16[16,128,128]{2,1,0:T(8,128)(2,1)}, u32[]{:S(2)}, u32[]{:S(2)}) collective-permute-start(bf16[16,128,128]{2,1,0:T(8,128)(2,1)S(1)} %collective-permute-done.7.refs_1_), channel_id=1, source_target_pairs={{16,0},{17,1},{18,2},{19,3},{20,4},{21,5},{22,6},{23,7},{24,8},{25... | collective-permute-start | bytes 1572872 | tf_op jit(solution)/shard_map/ppermute | solution.py:22
  106.3 27.4 %all-to-all-start = ((bf16[64,8,128]{2,1,0:T(8,128)(2,1)}), bf16[64,8,128]{2,1,0:T(8,128)(2,1)S(1)}, u32[]{:S(2)}, u32[]{:S(2)}) async-start(bf16[64,8,128]{2,1,0:T(8,128)(2,1)} %bitcast.23), calls=%async_computation | async-start | bytes 262144 | tf_op jit(solution)/shard_map/all_to_all | solution.py:290
  165.8 40.3 %all-to-all-start.2 = ((bf16[8,2,8,64,128]{4,3,2,1,0:T(8,128)(2,1)}), bf16[8,2,8,64,128]{4,3,2,1,0:T(8,128)(2,1)S(1)}, u32[]{:S(2)}, u32[]{:S(2)}) async-start(bf16[8,2,8,64,128]{4,3,2,1,0:T(8,128)(2,1)} %get-tuple-element.28), calls=%async_computation.2 | async-start | bytes 4194304 | tf_op jit(solution)/shard_map/all_to_all | solution.py:320
  170.6 61.5 %all-gather.7.cloned.1.call-start = ((), (), s32[]{:S(2)}) async-start(), calls=%async_computation.5 | async-start | bytes 1310720 | tf_op jit(solution)/shard_map/all_gather | solution.py:331
  174.3 17.1 %collective-permute-start.13 = (bf16[16,128,128]{2,1,0:T(8,128)(2,1)S(1)}, bf16[16,128,128]{2,1,0:T(8,128)(2,1)S(1)}, u32[]{:S(2)}, u32[]{:S(2)}) collective-permute-start(bf16[16,128,128]{2,1,0:T(8,128)(2,1)S(1)} %get-tuple-element.26), channel_id=1, source_target_pairs={{48,0},{49,1},{50,2},{51,3},{52,4},{53,5},{54,6},{55,7},{56,8},{57... | collective-permute-start | bytes 1572872 | tf_op jit(solution)/shard_map/ppermute | solution.py:22
  176.9 15.6 %collective-permute-start.15 = (bf16[16,128,128]{2,1,0:T(8,128)(2,1)S(1)}, bf16[16,128,128]{2,1,0:T(8,128)(2,1)S(1)}, u32[]{:S(2)}, u32[]{:S(2)}) collective-permute-start(bf16[16,128,128]{2,1,0:T(8,128)(2,1)S(1)} %get-tuple-element.27), channel_id=1, source_target_pairs={{16,0},{17,1},{18,2},{19,3},{20,4},{21,5},{22,6},{23,7},{24,8},{25... | collective-permute-start | bytes 1572872 | tf_op jit(solution)/shard_map/ppermute | solution.py:22
  192.7 11.1 %collective-permute-start.14 = (bf16[8,128,128]{2,1,0:T(8,128)(2,1)S(1)}, bf16[8,128,128]{2,1,0:T(8,128)(2,1)S(1)}, u32[]{:S(2)}, u32[]{:S(2)}) collective-permute-start(bf16[8,128,128]{2,1,0:T(8,128)(2,1)S(1)} %get-tuple-element.43), channel_id=1, source_target_pairs={{48,0},{49,1},{50,2},{51,3},{52,4},{53,5},{54,6},{55,7},{56,8},{57... | collective-permute-start | bytes 786440 | tf_op jit(solution)/shard_map/ppermute | solution.py:22
  196.0 8.9 %collective-permute-start.16 = (bf16[8,128,128]{2,1,0:T(8,128)(2,1)S(1)}, bf16[8,128,128]{2,1,0:T(8,128)(2,1)S(1)}, u32[]{:S(2)}, u32[]{:S(2)}) collective-permute-start(bf16[8,128,128]{2,1,0:T(8,128)(2,1)S(1)} %get-tuple-element.44), channel_id=1, source_target_pairs={{16,0},{17,1},{18,2},{19,3},{20,4},{21,5},{22,6},{23,7},{24,8},{25... | collective-permute-start | bytes 786440 | tf_op jit(solution)/shard_map/ppermute | solution.py:22
  208.3 30.1 %all-to-all-start.3 = ((bf16[16,128,128]{2,1,0:T(8,128)(2,1)}), bf16[16,128,128]{2,1,0:T(8,128)(2,1)S(1)}, u32[]{:S(2)}, u32[]{:S(2)}) async-start(bf16[16,128,128]{2,1,0:T(8,128)(2,1)} %pad_maximum_fusion), calls=%async_computation.3 | async-start | bytes 1048576 | tf_op jit(solution)/shard_map/all_to_all | solution.py:330
  232.1 6.3 %collective-permute-start.17 = (bf16[4,2,16,4096]{3,2,1,0:T(8,128)(2,1)}, bf16[4,2,16,4096]{3,2,1,0:T(8,128)(2,1)S(1)}, u32[]{:S(2)}, u32[]{:S(2)}) collective-permute-start(bf16[4,2,16,4096]{3,2,1,0:T(8,128)(2,1)} %bitcast.107), channel_id=1, source_target_pairs={{64,0},{0,64},{192,128},{128,192},{320,256},{256,320},{448,384},{3... | collective-permute-start | bytes 3145736 | tf_op jit(solution)/shard_map/ppermute | solution.py:26
  (13 other events, 392.4 us)
Sparse Core Ops, SparseCore 0:
  41.9 24.1 all-gather.4
  208.4 23.6 all-gather.6

commit v4 on v3

--- a/solution.py
+++ b/solution.py
@@ -12,6 +12,7 @@
 BF = jnp.bfloat16
 F32 = jnp.float32
 VM = pl.BlockSpec(memory_space=pltpu.VMEM)
+WHOLE = pl.BlockSpec()
 SM = pl.BlockSpec(memory_space=pltpu.SMEM)
 
 
@@ -100,7 +101,7 @@
     shape = jax.ShapeDtypeStruct((64, 256, 128), BF)
     return pl.pallas_call(
         spread_kernel,
-        in_specs=[SM] * 4 + [VM],
+        in_specs=[SM] * 4 + [WHOLE],
         out_specs=[VM, VM],
         out_shape=[shape, shape],
         compiler_params=pltpu.CompilerParams(vmem_limit_bytes=16 << 20),
@@ -181,7 +182,7 @@
     chunk = jax.ShapeDtypeStruct((NZ, 128, 128), BF)
     return pl.pallas_call(
         input_kernel,
-        in_specs=[SM] + [VM] * 2,
+        in_specs=[SM, VM, WHOLE],
         out_specs=[VM] * 4,
         out_shape=[chunk] * 4,
         compiler_params=pltpu.CompilerParams(vmem_limit_bytes=20 << 20),
@@ -267,7 +268,7 @@
 def pack(up, down, first, second):
     return pl.pallas_call(
         pack_kernel,
-        in_specs=[VM, VM] + [pl.BlockSpec(memory_space=pl.ANY)] * 2,
+        in_specs=[WHOLE, WHOLE] + [pl.BlockSpec(memory_space=pl.ANY)] * 2,
         out_specs=VM,
         out_shape=jax.ShapeDtypeStruct((2, 8, BLOCK, 2 * BLOCK), BF),
         compiler_params=pltpu.CompilerParams(vmem_limit_bytes=8 << 20),
@@ -304,10 +305,10 @@
     shape = jax.ShapeDtypeStruct((128, BLOCK * BLOCK), BF)
     return pl.pallas_call(
         place_kernel,
-        in_specs=[SM, VM, VM, VM],
+        in_specs=[SM, WHOLE, VM, VM],
         out_specs=[VM, VM, VM],
         out_shape=[shape, shape, jax.ShapeDtypeStruct((128, 128), BF)],
-        compiler_params=pltpu.CompilerParams(vmem_limit_bytes=48 << 20),
+        compiler_params=pltpu.CompilerParams(vmem_limit_bytes=16 << 20),
         cost_estimate=pl.CostEstimate(flops=0, bytes_accessed=4 << 20, transcendentals=0),
         name="place_slots",
     )(me, mine, theirs, parts)

time: 251 us -> 251 us (level)
  no operation moved by 1% of the time
where the time goes in v4:
time: 251 us; the launch traced here: 248 us
  starting transfers between devices  89.8 us (36%)
  waiting for transfers between devices  85.7 us (34%)
  Pallas kernels  23.5 us (9%)
  blocking collectives  20.6 us (8%)
  between operations  14.6 us (6%)
  local copies, waits for them, and re-layouts  9.12 us (4%)
  other arithmetic  3.61 us (1%)
    ppermute x17, starting transfers between devices, from_tensor(): return lax.ppermute(value, 'tensor', pairs)  67.7 us
    ppermute x17, waiting for transfers between devices, from_tensor(): return lax.ppermute(value, 'tensor', pairs)  46.6 us
    all_to_all x1, blocking collectives, exchange(): lax.all_to_all(rows.reshape(64, 8, 128), 'tensor', 0, 0, tiled=True)  20.6 us
    all_gather x1, waiting for transfers between devices, reduce_all(): mine = lax.all_gather(own, 'dp', axis=0, axis_index_groups=Y_GROUPS)  20.2 us
    all_to_all x1, waiting for transfers between devices, exchange(): lax.all_to_all(rows.reshape(64, 8, 128), 'tensor', 0, 0, tiled=True)  14.4 us
    all_to_all x1, starting transfers between devices, exchange(): lax.all_to_all(rows.reshape(64, 8, 128), 'tensor', 0, 0, tiled=True)  11.8 us
    pallas_call x1, Pallas kernels, weight_terms(): pl.pallas_call(weight_kernel, in_specs=[SM] * 4 + [VM] * 10, out_specs=[V...  10.4 us
    unnamed x33, local copies, waits for them, and re-layouts  6.98 us
  transfers between devices with their start and end apart: 23, of which 15 were waited for; matrix products, arithmetic and copies ran while one was open for 1% of the time, Pallas kernels for 2%

profile of v4, /device:TPU:24, one launch (start us, length us, event | category | flops | bytes accessed | tf_op | source)
XLA Modules:
  0.0 247.9 jit_solution(9061967695364261667)
XLA Ops:
  8.1 14.4 %collective-permute-start = (bf16[2,1,128,128]{3,2,1,0:T(8,128)(2,1)S(1)}, bf16[2,1,128,128]{3,2,1,0:T(8,128)(2,1)S(1)}, u32[]{:S(2)}, u32[]{:S(2)}) collective-permute-start(bf16[2,1,128,128]{3,2,1,0:T(8,128)(2,1)S(1)} %maximum_bitcast_fusion), channel_id=1, source_target_pairs={{5,0},{6,1},{7,2},{8,3},{9,4},{10,5},{11,6},{12,7},{13,8},{14,9},{... | collective-permute-start | bytes 196616 | tf_op jit(solution)/shard_map/ppermute | solution.py:23
  24.4 4.3 %collective-permute-done.first = bf16[2,1,128,128]{3,2,1,0:T(8,128)(2,1)S(1)} collective-permute-done((bf16[2,1,128,128]{3,2,1,0:T(8,128)(2,1)S(1)}, bf16[2,1,128,128]{3,2,1,0:T(8,128)(2,1)S(1)}, u32[]{:S(2)}, u32[]{:S(2)}) %collective-permute-start) | collective-permute-done | bytes 65568 | tf_op jit(solution)/shard_map/ppermute | solution.py:23
  28.6 10.2 %collective-permute-done.1.second = bf16[2,1,128,128]{3,2,1,0:T(8,128)(2,1)S(1)} collective-permute-done((bf16[2,1,128,128]{3,2,1,0:T(8,128)(2,1)S(1)}, bf16[2,1,128,128]{3,2,1,0:T(8,128)(2,1)S(1)}, u32[]{:S(2)}, u32[]{:S(2)}) %collective-permute-start.1) | collective-permute-done | bytes 65568 | tf_op jit(solution)/shard_map/ppermute | solution.py:23
  44.2 3.4 %collective-permute-start.3 = (bf16[2,3,128,128]{3,2,1,0:T(8,128)(2,1)S(1)}, bf16[2,3,128,128]{3,2,1,0:T(8,128)(2,1)S(1)}, u32[]{:S(2)}, u32[]{:S(2)}) collective-permute-start(bf16[2,3,128,128]{3,2,1,0:T(8,128)(2,1)S(1)} %pad_maximum_fusion.4), channel_id=1, source_target_pairs={{15,0},{0,1},{1,2},{2,3},{3,4},{4,5},{5,6},{6,7},{7,8},{8,9},{9,10... | collective-permute-start | bytes 589832 | tf_op jit(solution)/shard_map/ppermute | solution.py:23
  50.0 4.4 %collective-permute-start.5 = (bf16[2,3,128,128]{3,2,1,0:T(8,128)(2,1)S(1)}, bf16[2,3,128,128]{3,2,1,0:T(8,128)(2,1)S(1)}, u32[]{:S(2)}, u32[]{:S(2)}) collective-permute-start(bf16[2,3,128,128]{3,2,1,0:T(8,128)(2,1)S(1)} %pad_maximum_fusion.4), channel_id=1, source_target_pairs={{14,0},{15,1},{0,2},{1,3},{2,4},{3,5},{4,6},{5,7},{6,8},{7,9},{8,1... | collective-permute-start | bytes 589832 | tf_op jit(solution)/shard_map/ppermute | solution.py:23
  57.6 5.5 %collective-permute-done.5 = bf16[2,3,128,128]{3,2,1,0:T(8,128)(2,1)S(1)} collective-permute-done((bf16[2,3,128,128]{3,2,1,0:T(8,128)(2,1)S(1)}, bf16[2,3,128,128]{3,2,1,0:T(8,128)(2,1)S(1)}, u32[]{:S(2)}, u32[]{:S(2)}) %collective-permute-start.5) | collective-permute-done | bytes 196640 | tf_op jit(solution)/shard_map/ppermute | solution.py:23
  66.6 3.7 %collective-permute-start.7 = (bf16[16,128,128]{2,1,0:T(8,128)(2,1)S(1)}, bf16[16,128,128]{2,1,0:T(8,128)(2,1)S(1)}, u32[]{:S(2)}, u32[]{:S(2)}) collective-permute-start(bf16[16,128,128]{2,1,0:T(8,128)(2,1)S(1)} %get-tuple-element.62.refs_0_), channel_id=1, source_target_pairs={{16,0},{17,1},{18,2},{19,3},{20,4},{21,5},{22,6},{23,7},{24,8},{25... | collective-permute-start | bytes 1572872 | tf_op jit(solution)/shard_map/ppermute | solution.py:23
  70.5 3.5 %collective-permute-start.10 = (bf16[16,128,128]{2,1,0:T(8,128)(2,1)S(1)}, bf16[16,128,128]{2,1,0:T(8,128)(2,1)S(1)}, u32[]{:S(2)}, u32[]{:S(2)}) collective-permute-start(bf16[16,128,128]{2,1,0:T(8,128)(2,1)S(1)} %get-tuple-element.61.refs_4_), channel_id=1, source_target_pairs={{16,0},{17,1},{18,2},{19,3},{20,4},{21,5},{22,6},{23,7},{24,8},{25... | collective-permute-start | bytes 1572872 | tf_op jit(solution)/shard_map/ppermute | solution.py:23
  83.4 4.9 %collective-permute-start.8 = (bf16[16,128,128]{2,1,0:T(8,128)(2,1)S(1)}, bf16[16,128,128]{2,1,0:T(8,128)(2,1)}, u32[]{:S(2)}, u32[]{:S(2)}) collective-permute-start(bf16[16,128,128]{2,1,0:T(8,128)(2,1)S(1)} %collective-permute-done.7.refs_1_), channel_id=1, source_target_pairs={{16,0},{17,1},{18,2},{19,3},{20,4},{21,5},{22,6},{23,7},{24,8},{25... | collective-permute-start | bytes 1572872 | tf_op jit(solution)/shard_map/ppermute | solution.py:23
  90.0 4.2 %spread_weights.1 = (bf16[64,256,128]{2,1,0:T(8,128)(2,1)S(1)}, bf16[64,256,128]{2,1,0:T(8,128)(2,1)S(1)}) custom-call(s32[128]{0:T(128)S(1)} %fusion.17.up_at, s32[128]{0:T(128)S(1)} %bitcast.112, s32[128]{0:T(128)S(1)} %fusion.18.down_at, s32[128]{0:T(128)S(1)} %bitcast.114, bf16[8,2,8,64,128]{4,3,2,1,0:T(8,128)(2,1)S(1)} %bitcast.106), custom_call_target="tpu_custom_call" | custom-call | bytes 12582912 | tf_op jit(solution)/shard_map/spread_weights/pallas_call | solution.py:102
  94.6 4.8 %collective-permute-done.12.refs_6_ = bf16[16,128,128]{2,1,0:T(8,128)(2,1)} collective-permute-done((bf16[16,128,128]{2,1,0:T(8,128)(2,1)S(1)}, bf16[16,128,128]{2,1,0:T(8,128)(2,1)}, u32[]{:S(2)}, u32[]{:S(2)}) %collective-permute-start.12) | collective-permute-done | bytes 524320 | tf_op jit(solution)/shard_map/ppermute | solution.py:23
  101.4 4.9 %forward.1 = (bf16[512,128]{1,0:T(8,128)(2,1)}, f32[128,256]{1,0:T(8,128)S(1)}) custom-call(bf16[16,128,128]{2,1,0:T(8,128)(2,1)S(1)} %get-tuple-element.62.refs_0_, bf16[16,128,128]{2,1,0:T(8,128)(2,1)S(1)} %collective-permute-done.7.refs_1_, bf16[16,128,128]{2,1,0:T(8,128)(2,1)} %collective-permute-done.8.refs_2_, ...), custom_call_target="tpu_custom_call" | custom-call | flops 1073741824 | bytes 12582912 | tf_op jit(solution)/shard_map/forward/pallas_call | solution.py:150
  106.3 11.8 %all-to-all-start = ((bf16[64,8,128]{2,1,0:T(8,128)(2,1)}), bf16[64,8,128]{2,1,0:T(8,128)(2,1)S(1)}, u32[]{:S(2)}, u32[]{:S(2)}) async-start(bf16[64,8,128]{2,1,0:T(8,128)(2,1)} %bitcast.23), calls=%async_computation | async-start | bytes 262144 | tf_op jit(solution)/shard_map/all_to_all | solution.py:291
  119.3 14.4 %all-to-all-done = bf16[64,8,128]{2,1,0:T(8,128)(2,1)S(1)} async-done(((bf16[64,8,128]{2,1,0:T(8,128)(2,1)}), bf16[64,8,128]{2,1,0:T(8,128)(2,1)S(1)}, u32[]{:S(2)}, u32[]{:S(2)}) %all-to-all-start) | async-done | bytes 131104 | tf_op jit(solution)/shard_map/all_to_all | solution.py:291
  134.7 20.6 %all_to_all.20 = bf16[64,8,128]{2,1,0:T(8,128)(2,1)S(1)} all-to-all(bf16[64,8,128]{2,1,0:T(8,128)(2,1)S(1)} %fusion), channel_id=1, replica_groups=mesh['dp'=8,'tensor'=64] {'tensor'}, dimensions={0} | all-to-all | bytes 262144 | tf_op jit(solution)/shard_map/all_to_all | solution.py:291
  155.3 10.4 %weight_terms.1 = (bf16[8,2,8,64,128]{4,3,2,1,0:T(8,128)(2,1)}, bf16[128,256]{1,0:T(8,128)(2,1)S(1)}) custom-call(s32[128]{0:T(128)S(1)} %fusion.17.up_at, s32[128]{0:T(128)S(1)} %bitcast.113, s32[128]{0:T(128)S(1)} %fusion.18.down_at, s32[128]{0:T(128)S(1)} %bitcast.115, bf16[16,128,128]{2,1,0:T(8,128)(2,1)S(1)} %get-tuple-element.62.refs_0_, ...), custom_call_target="tpu_custom_call" | custom-call | flops 1610612736 | bytes 14680064 | tf_op jit(solution)/shard_map/weight_terms/pallas_call | solution.py:236
  165.8 4.8 %all-to-all-start.2 = ((bf16[8,2,8,64,128]{4,3,2,1,0:T(8,128)(2,1)}), bf16[8,2,8,64,128]{4,3,2,1,0:T(8,128)(2,1)S(1)}, u32[]{:S(2)}, u32[]{:S(2)}) async-start(bf16[8,2,8,64,128]{4,3,2,1,0:T(8,128)(2,1)} %get-tuple-element.28), calls=%async_computation.2 | async-start | bytes 4194304 | tf_op jit(solution)/shard_map/all_to_all | solution.py:321
  176.9 4.4 %collective-permute-start.15 = (bf16[16,128,128]{2,1,0:T(8,128)(2,1)S(1)}, bf16[16,128,128]{2,1,0:T(8,128)(2,1)S(1)}, u32[]{:S(2)}, u32[]{:S(2)}) collective-permute-start(bf16[16,128,128]{2,1,0:T(8,128)(2,1)S(1)} %get-tuple-element.27), channel_id=1, source_target_pairs={{16,0},{17,1},{18,2},{19,3},{20,4},{21,5},{22,6},{23,7},{24,8},{25... | collective-permute-start | bytes 1572872 | tf_op jit(solution)/shard_map/ppermute | solution.py:23
  181.4 10.0 %collective-permute-done.13 = bf16[16,128,128]{2,1,0:T(8,128)(2,1)S(1)} collective-permute-done((bf16[16,128,128]{2,1,0:T(8,128)(2,1)S(1)}, bf16[16,128,128]{2,1,0:T(8,128)(2,1)S(1)}, u32[]{:S(2)}, u32[]{:S(2)}) %collective-permute-start.13) | collective-permute-done | bytes 524320 | tf_op jit(solution)/shard_map/ppermute | solution.py:23
  196.0 4.2 %collective-permute-start.16 = (bf16[8,128,128]{2,1,0:T(8,128)(2,1)S(1)}, bf16[8,128,128]{2,1,0:T(8,128)(2,1)S(1)}, u32[]{:S(2)}, u32[]{:S(2)}) collective-permute-start(bf16[8,128,128]{2,1,0:T(8,128)(2,1)S(1)} %get-tuple-element.44), channel_id=1, source_target_pairs={{16,0},{17,1},{18,2},{19,3},{20,4},{21,5},{22,6},{23,7},{24,8},{25... | collective-permute-start | bytes 786440 | tf_op jit(solution)/shard_map/ppermute | solution.py:23
  200.2 3.5 %collective-permute-done.14 = bf16[8,128,128]{2,1,0:T(8,128)(2,1)S(1)} collective-permute-done((bf16[8,128,128]{2,1,0:T(8,128)(2,1)S(1)}, bf16[8,128,128]{2,1,0:T(8,128)(2,1)S(1)}, u32[]{:S(2)}, u32[]{:S(2)}) %collective-permute-start.14) | collective-permute-done | bytes 262176 | tf_op jit(solution)/shard_map/ppermute | solution.py:23
  208.3 3.6 %all-to-all-start.3 = ((bf16[16,128,128]{2,1,0:T(8,128)(2,1)}), bf16[16,128,128]{2,1,0:T(8,128)(2,1)S(1)}, u32[]{:S(2)}, u32[]{:S(2)}) async-start(bf16[16,128,128]{2,1,0:T(8,128)(2,1)} %pad_maximum_fusion), calls=%async_computation.3 | async-start | bytes 1048576 | tf_op jit(solution)/shard_map/all_to_all | solution.py:331
  211.9 20.2 %all-gather.7.cloned.1.call-done = bf16[8,16,4096]{2,1,0:T(8,128)(2,1)} async-done(((bf16[2,16,4096]{2,1,0:T(8,128)(2,1)}), bf16[8,16,4096]{2,1,0:T(8,128)(2,1)}) %all-gather.7.cloned.1.call-update) | async-done | bytes 1048592 | tf_op jit(solution)/shard_map/all_gather | solution.py:332
  234.1 4.4 %all-to-all-done.3.parts = bf16[16,128,128]{2,1,0:T(8,128)(2,1)S(1)} async-done(((bf16[16,128,128]{2,1,0:T(8,128)(2,1)}), bf16[16,128,128]{2,1,0:T(8,128)(2,1)S(1)}, u32[]{:S(2)}, u32[]{:S(2)}) %all-to-all-start.3) | async-done | bytes 524320 | tf_op jit(solution)/shard_map/all_to_all | solution.py:331
  (97 shorter events, 52.7 us)
Async XLA Ops:
  7.2 81.2 %copy-start.6 = (s32[1,128]{1,0:T(1,128)S(1)}, s32[1,128]{1,0:T(1,128)}, u32[]{:S(2)}) copy-start(s32[1,128]{1,0:T(1,128)} %param.17) | copy-start | bytes 1540
  7.2 81.2 %all-gather.5.cloned.1.call-start = ((), (), s32[]{:S(2)}) async-start(), calls=%async_computation.4 | async-start | bytes 2359296 | tf_op jit(solution)/shard_map/all_gather | solution.py:350
  8.1 20.6 %collective-permute-start = (bf16[2,1,128,128]{3,2,1,0:T(8,128)(2,1)S(1)}, bf16[2,1,128,128]{3,2,1,0:T(8,128)(2,1)S(1)}, u32[]{:S(2)}, u32[]{:S(2)}) collective-permute-start(bf16[2,1,128,128]{3,2,1,0:T(8,128)(2,1)S(1)} %maximum_bitcast_fusion), channel_id=1, source_target_pairs={{5,0},{6,1},{7,2},{8,3},{9,4},{10,5},{11,6},{12,7},{13,8},{14,9},{... | collective-permute-start | bytes 196616 | tf_op jit(solution)/shard_map/ppermute | solution.py:23
  22.4 16.4 %collective-permute-start.1 = (bf16[2,1,128,128]{3,2,1,0:T(8,128)(2,1)S(1)}, bf16[2,1,128,128]{3,2,1,0:T(8,128)(2,1)S(1)}, u32[]{:S(2)}, u32[]{:S(2)}) collective-permute-start(bf16[2,1,128,128]{3,2,1,0:T(8,128)(2,1)S(1)} %maximum_bitcast_fusion), channel_id=1, source_target_pairs={{11,0},{12,1},{13,2},{14,3},{15,4},{0,5},{1,6},{2,7},{3,8},{4,9},{... | collective-permute-start | bytes 196616 | tf_op jit(solution)/shard_map/ppermute | solution.py:23
  41.8 15.7 %collective-permute-start.2 = (bf16[2,3,128,128]{3,2,1,0:T(8,128)(2,1)S(1)}, bf16[2,3,128,128]{3,2,1,0:T(8,128)(2,1)S(1)}, u32[]{:S(2)}, u32[]{:S(2)}) collective-permute-start(bf16[2,3,128,128]{3,2,1,0:T(8,128)(2,1)S(1)} %pad_maximum_fusion.4), channel_id=1, source_target_pairs={{1,0},{2,1},{3,2},{4,3},{5,4},{6,5},{7,6},{8,7},{9,8},{10,9},{11,1... | collective-permute-start | bytes 589832 | tf_op jit(solution)/shard_map/ppermute | solution.py:23
  44.2 13.3 %collective-permute-start.3 = (bf16[2,3,128,128]{3,2,1,0:T(8,128)(2,1)S(1)}, bf16[2,3,128,128]{3,2,1,0:T(8,128)(2,1)S(1)}, u32[]{:S(2)}, u32[]{:S(2)}) collective-permute-start(bf16[2,3,128,128]{3,2,1,0:T(8,128)(2,1)S(1)} %pad_maximum_fusion.4), channel_id=1, source_target_pairs={{15,0},{0,1},{1,2},{2,3},{3,4},{4,5},{5,6},{6,7},{7,8},{8,9},{9,10... | collective-permute-start | bytes 589832 | tf_op jit(solution)/shard_map/ppermute | solution.py:23
  47.7 9.9 %collective-permute-start.4 = (bf16[2,3,128,128]{3,2,1,0:T(8,128)(2,1)S(1)}, bf16[2,3,128,128]{3,2,1,0:T(8,128)(2,1)S(1)}, u32[]{:S(2)}, u32[]{:S(2)}) collective-permute-start(bf16[2,3,128,128]{3,2,1,0:T(8,128)(2,1)S(1)} %pad_maximum_fusion.4), channel_id=1, source_target_pairs={{2,0},{3,1},{4,2},{5,3},{6,4},{7,5},{8,6},{9,7},{10,8},{11,9},{12,... | collective-permute-start | bytes 589832 | tf_op jit(solution)/shard_map/ppermute | solution.py:23
  50.0 13.2 %collective-permute-start.5 = (bf16[2,3,128,128]{3,2,1,0:T(8,128)(2,1)S(1)}, bf16[2,3,128,128]{3,2,1,0:T(8,128)(2,1)S(1)}, u32[]{:S(2)}, u32[]{:S(2)}) collective-permute-start(bf16[2,3,128,128]{3,2,1,0:T(8,128)(2,1)S(1)} %pad_maximum_fusion.4), channel_id=1, source_target_pairs={{14,0},{15,1},{0,2},{1,3},{2,4},{3,5},{4,6},{5,7},{6,8},{7,9},{8,1... | collective-permute-start | bytes 589832 | tf_op jit(solution)/shard_map/ppermute | solution.py:23
  54.4 8.8 %collective-permute-start.6 = (bf16[2,1,128,128]{3,2,1,0:T(8,128)(2,1)S(1)}, bf16[2,1,128,128]{3,2,1,0:T(8,128)(2,1)S(1)}, u32[]{:S(2)}, u32[]{:S(2)}) collective-permute-start(bf16[2,1,128,128]{3,2,1,0:T(8,128)(2,1)S(1)} %collective-permute-done.first), channel_id=1, source_target_pairs={{3,0},{4,1},{5,2},{6,3},{7,4},{8,5},{9,6},{10,7},{11,8},{12,9},{13... | collective-permute-start | bytes 196616 | tf_op jit(solution)/shard_map/ppermute | solution.py:23
  63.2 14.9 %collective-permute-start.11 = (bf16[16,128,128]{2,1,0:T(8,128)(2,1)S(1)}, bf16[16,128,128]{2,1,0:T(8,128)(2,1)S(1)}, u32[]{:S(2)}, u32[]{:S(2)}) collective-permute-start(bf16[16,128,128]{2,1,0:T(8,128)(2,1)S(1)} %get-tuple-element.61.refs_4_), channel_id=1, source_target_pairs={{48,0},{49,1},{50,2},{51,3},{52,4},{53,5},{54,6},{55,7},{56,8},{57... | collective-permute-start | bytes 1572872 | tf_op jit(solution)/shard_map/ppermute | solution.py:23
  66.6 16.8 %collective-permute-start.7 = (bf16[16,128,128]{2,1,0:T(8,128)(2,1)S(1)}, bf16[16,128,128]{2,1,0:T(8,128)(2,1)S(1)}, u32[]{:S(2)}, u32[]{:S(2)}) collective-permute-start(bf16[16,128,128]{2,1,0:T(8,128)(2,1)S(1)} %get-tuple-element.62.refs_0_), channel_id=1, source_target_pairs={{16,0},{17,1},{18,2},{19,3},{20,4},{21,5},{22,6},{23,7},{24,8},{25... | collective-permute-start | bytes 1572872 | tf_op jit(solution)/shard_map/ppermute | solution.py:23
  70.5 24.1 %collective-permute-start.10 = (bf16[16,128,128]{2,1,0:T(8,128)(2,1)S(1)}, bf16[16,128,128]{2,1,0:T(8,128)(2,1)S(1)}, u32[]{:S(2)}, u32[]{:S(2)}) collective-permute-start(bf16[16,128,128]{2,1,0:T(8,128)(2,1)S(1)} %get-tuple-element.61.refs_4_), channel_id=1, source_target_pairs={{16,0},{17,1},{18,2},{19,3},{20,4},{21,5},{22,6},{23,7},{24,8},{25... | collective-permute-start | bytes 1572872 | tf_op jit(solution)/shard_map/ppermute | solution.py:23
  73.9 20.7 %collective-permute-start.9 = (bf16[16,128,128]{2,1,0:T(8,128)(2,1)S(1)}, bf16[16,128,128]{2,1,0:T(8,128)(2,1)S(1)}, u32[]{:S(2)}, u32[]{:S(2)}) collective-permute-start(bf16[16,128,128]{2,1,0:T(8,128)(2,1)S(1)} %get-tuple-element.62.refs_0_), channel_id=1, source_target_pairs={{48,0},{49,1},{50,2},{51,3},{52,4},{53,5},{54,6},{55,7},{56,8},{57... | collective-permute-start | bytes 1572872 | tf_op jit(solution)/shard_map/ppermute | solution.py:23
  78.2 21.3 %collective-permute-start.12 = (bf16[16,128,128]{2,1,0:T(8,128)(2,1)S(1)}, bf16[16,128,128]{2,1,0:T(8,128)(2,1)}, u32[]{:S(2)}, u32[]{:S(2)}) collective-permute-start(bf16[16,128,128]{2,1,0:T(8,128)(2,1)S(1)} %collective-permute-done.11.refs_7_), channel_id=1, source_target_pairs={{48,0},{49,1},{50,2},{51,3},{52,4},{53,5},{54,6},{55,7},{56,8},{57... | collective-permute-start | bytes 1572872 | tf_op jit(solution)/shard_map/ppermute | solution.py:23
  83.4 18.0 %collective-permute-start.8 = (bf16[16,128,128]{2,1,0:T(8,128)(2,1)S(1)}, bf16[16,128,128]{2,1,0:T(8,128)(2,1)}, u32[]{:S(2)}, u32[]{:S(2)}) collective-permute-start(bf16[16,128,128]{2,1,0:T(8,128)(2,1)S(1)} %collective-permute-done.7.refs_1_), channel_id=1, source_target_pairs={{16,0},{17,1},{18,2},{19,3},{20,4},{21,5},{22,6},{23,7},{24,8},{25... | collective-permute-start | bytes 1572872 | tf_op jit(solution)/shard_map/ppermute | solution.py:23
  106.3 27.4 %all-to-all-start = ((bf16[64,8,128]{2,1,0:T(8,128)(2,1)}), bf16[64,8,128]{2,1,0:T(8,128)(2,1)S(1)}, u32[]{:S(2)}, u32[]{:S(2)}) async-start(bf16[64,8,128]{2,1,0:T(8,128)(2,1)} %bitcast.23), calls=%async_computation | async-start | bytes 262144 | tf_op jit(solution)/shard_map/all_to_all | solution.py:291
  165.8 40.3 %all-to-all-start.2 = ((bf16[8,2,8,64,128]{4,3,2,1,0:T(8,128)(2,1)}), bf16[8,2,8,64,128]{4,3,2,1,0:T(8,128)(2,1)S(1)}, u32[]{:S(2)}, u32[]{:S(2)}) async-start(bf16[8,2,8,64,128]{4,3,2,1,0:T(8,128)(2,1)} %get-tuple-element.28), calls=%async_computation.2 | async-start | bytes 4194304 | tf_op jit(solution)/shard_map/all_to_all | solution.py:321
  170.6 61.5 %all-gather.7.cloned.1.call-start = ((), (), s32[]{:S(2)}) async-start(), calls=%async_computation.5 | async-start | bytes 1310720 | tf_op jit(solution)/shard_map/all_gather | solution.py:332
  174.3 17.1 %collective-permute-start.13 = (bf16[16,128,128]{2,1,0:T(8,128)(2,1)S(1)}, bf16[16,128,128]{2,1,0:T(8,128)(2,1)S(1)}, u32[]{:S(2)}, u32[]{:S(2)}) collective-permute-start(bf16[16,128,128]{2,1,0:T(8,128)(2,1)S(1)} %get-tuple-element.26), channel_id=1, source_target_pairs={{48,0},{49,1},{50,2},{51,3},{52,4},{53,5},{54,6},{55,7},{56,8},{57... | collective-permute-start | bytes 1572872 | tf_op jit(solution)/shard_map/ppermute | solution.py:23
  176.9 15.6 %collective-permute-start.15 = (bf16[16,128,128]{2,1,0:T(8,128)(2,1)S(1)}, bf16[16,128,128]{2,1,0:T(8,128)(2,1)S(1)}, u32[]{:S(2)}, u32[]{:S(2)}) collective-permute-start(bf16[16,128,128]{2,1,0:T(8,128)(2,1)S(1)} %get-tuple-element.27), channel_id=1, source_target_pairs={{16,0},{17,1},{18,2},{19,3},{20,4},{21,5},{22,6},{23,7},{24,8},{25... | collective-permute-start | bytes 1572872 | tf_op jit(solution)/shard_map/ppermute | solution.py:23
  192.7 11.1 %collective-permute-start.14 = (bf16[8,128,128]{2,1,0:T(8,128)(2,1)S(1)}, bf16[8,128,128]{2,1,0:T(8,128)(2,1)S(1)}, u32[]{:S(2)}, u32[]{:S(2)}) collective-permute-start(bf16[8,128,128]{2,1,0:T(8,128)(2,1)S(1)} %get-tuple-element.43), channel_id=1, source_target_pairs={{48,0},{49,1},{50,2},{51,3},{52,4},{53,5},{54,6},{55,7},{56,8},{57... | collective-permute-start | bytes 786440 | tf_op jit(solution)/shard_map/ppermute | solution.py:23
  196.0 8.9 %collective-permute-start.16 = (bf16[8,128,128]{2,1,0:T(8,128)(2,1)S(1)}, bf16[8,128,128]{2,1,0:T(8,128)(2,1)S(1)}, u32[]{:S(2)}, u32[]{:S(2)}) collective-permute-start(bf16[8,128,128]{2,1,0:T(8,128)(2,1)S(1)} %get-tuple-element.44), channel_id=1, source_target_pairs={{16,0},{17,1},{18,2},{19,3},{20,4},{21,5},{22,6},{23,7},{24,8},{25... | collective-permute-start | bytes 786440 | tf_op jit(solution)/shard_map/ppermute | solution.py:23
  208.3 30.1 %all-to-all-start.3 = ((bf16[16,128,128]{2,1,0:T(8,128)(2,1)}), bf16[16,128,128]{2,1,0:T(8,128)(2,1)S(1)}, u32[]{:S(2)}, u32[]{:S(2)}) async-start(bf16[16,128,128]{2,1,0:T(8,128)(2,1)} %pad_maximum_fusion), calls=%async_computation.3 | async-start | bytes 1048576 | tf_op jit(solution)/shard_map/all_to_all | solution.py:331
  232.1 6.3 %collective-permute-start.17 = (bf16[4,2,16,4096]{3,2,1,0:T(8,128)(2,1)}, bf16[4,2,16,4096]{3,2,1,0:T(8,128)(2,1)S(1)}, u32[]{:S(2)}, u32[]{:S(2)}) collective-permute-start(bf16[4,2,16,4096]{3,2,1,0:T(8,128)(2,1)} %bitcast.107), channel_id=1, source_target_pairs={{64,0},{0,64},{192,128},{128,192},{320,256},{256,320},{448,384},{3... | collective-permute-start | bytes 3145736 | tf_op jit(solution)/shard_map/ppermute | solution.py:27
  (13 other events, 392.4 us)
Sparse Core Ops, SparseCore 0:
  41.9 24.1 all-gather.4
  208.4 23.6 all-gather.6

commit v5 on v4

--- a/solution.py
+++ b/solution.py
@@ -324,7 +324,7 @@
     low = add(near[:half], low, got_minus[:half])
     high = add(near[half:], got_plus[half:], high)
     column = jnp.concatenate([low, high])
-    slots, _ = order((slots, column))
+    slots, *_ = order((slots, on_plus, on_minus))
     own = jnp.sum(slots.astype(F32), axis=0).astype(BF)
     own = jnp.stack([unpack(jnp.swapaxes(own[0], 1, 2), True), unpack(own[1])])
     column, own = order((column, own))

time: 251 us -> 251 us (level)
  no operation moved by 1% of the time
where the time goes in v5:
time: 251 us; the launch traced here: 248 us
  starting transfers between devices  89.8 us (36%)
  waiting for transfers between devices  85.7 us (34%)
  Pallas kernels  23.5 us (9%)
  blocking collectives  20.6 us (8%)
  between operations  14.6 us (6%)
  local copies, waits for them, and re-layouts  9.12 us (4%)
  other arithmetic  3.61 us (1%)
    ppermute x17, starting transfers between devices, from_tensor(): return lax.ppermute(value, 'tensor', pairs)  67.7 us
    ppermute x17, waiting for transfers between devices, from_tensor(): return lax.ppermute(value, 'tensor', pairs)  46.6 us
    all_to_all x1, blocking collectives, exchange(): lax.all_to_all(rows.reshape(64, 8, 128), 'tensor', 0, 0, tiled=True)  20.6 us
    all_gather x1, waiting for transfers between devices, reduce_all(): mine = lax.all_gather(own, 'dp', axis=0, axis_index_groups=Y_GROUPS)  20.2 us
    all_to_all x1, waiting for transfers between devices, exchange(): lax.all_to_all(rows.reshape(64, 8, 128), 'tensor', 0, 0, tiled=True)  14.4 us
    all_to_all x1, starting transfers between devices, exchange(): lax.all_to_all(rows.reshape(64, 8, 128), 'tensor', 0, 0, tiled=True)  11.8 us
    pallas_call x1, Pallas kernels, weight_terms(): pl.pallas_call(weight_kernel, in_specs=[SM] * 4 + [VM] * 10, out_specs=[V...  10.4 us
    unnamed x33, local copies, waits for them, and re-layouts  6.98 us
  transfers between devices with their start and end apart: 23, of which 15 were waited for; matrix products, arithmetic and copies ran while one was open for 1% of the time, Pallas kernels for 2%

profile of v5, /device:TPU:24, one launch (start us, length us, event | category | flops | bytes accessed | tf_op | source)
XLA Modules:
  0.0 247.9 jit_solution(9061967695364261667)
XLA Ops:
  8.1 14.4 %collective-permute-start = (bf16[2,1,128,128]{3,2,1,0:T(8,128)(2,1)S(1)}, bf16[2,1,128,128]{3,2,1,0:T(8,128)(2,1)S(1)}, u32[]{:S(2)}, u32[]{:S(2)}) collective-permute-start(bf16[2,1,128,128]{3,2,1,0:T(8,128)(2,1)S(1)} %maximum_bitcast_fusion), channel_id=1, source_target_pairs={{5,0},{6,1},{7,2},{8,3},{9,4},{10,5},{11,6},{12,7},{13,8},{14,9},{... | collective-permute-start | bytes 196616 | tf_op jit(solution)/shard_map/ppermute | solution.py:23
  24.4 4.3 %collective-permute-done.first = bf16[2,1,128,128]{3,2,1,0:T(8,128)(2,1)S(1)} collective-permute-done((bf16[2,1,128,128]{3,2,1,0:T(8,128)(2,1)S(1)}, bf16[2,1,128,128]{3,2,1,0:T(8,128)(2,1)S(1)}, u32[]{:S(2)}, u32[]{:S(2)}) %collective-permute-start) | collective-permute-done | bytes 65568 | tf_op jit(solution)/shard_map/ppermute | solution.py:23
  28.6 10.2 %collective-permute-done.1.second = bf16[2,1,128,128]{3,2,1,0:T(8,128)(2,1)S(1)} collective-permute-done((bf16[2,1,128,128]{3,2,1,0:T(8,128)(2,1)S(1)}, bf16[2,1,128,128]{3,2,1,0:T(8,128)(2,1)S(1)}, u32[]{:S(2)}, u32[]{:S(2)}) %collective-permute-start.1) | collective-permute-done | bytes 65568 | tf_op jit(solution)/shard_map/ppermute | solution.py:23
  44.2 3.4 %collective-permute-start.3 = (bf16[2,3,128,128]{3,2,1,0:T(8,128)(2,1)S(1)}, bf16[2,3,128,128]{3,2,1,0:T(8,128)(2,1)S(1)}, u32[]{:S(2)}, u32[]{:S(2)}) collective-permute-start(bf16[2,3,128,128]{3,2,1,0:T(8,128)(2,1)S(1)} %pad_maximum_fusion.4), channel_id=1, source_target_pairs={{15,0},{0,1},{1,2},{2,3},{3,4},{4,5},{5,6},{6,7},{7,8},{8,9},{9,10... | collective-permute-start | bytes 589832 | tf_op jit(solution)/shard_map/ppermute | solution.py:23
  50.0 4.4 %collective-permute-start.5 = (bf16[2,3,128,128]{3,2,1,0:T(8,128)(2,1)S(1)}, bf16[2,3,128,128]{3,2,1,0:T(8,128)(2,1)S(1)}, u32[]{:S(2)}, u32[]{:S(2)}) collective-permute-start(bf16[2,3,128,128]{3,2,1,0:T(8,128)(2,1)S(1)} %pad_maximum_fusion.4), channel_id=1, source_target_pairs={{14,0},{15,1},{0,2},{1,3},{2,4},{3,5},{4,6},{5,7},{6,8},{7,9},{8,1... | collective-permute-start | bytes 589832 | tf_op jit(solution)/shard_map/ppermute | solution.py:23
  57.6 5.5 %collective-permute-done.5 = bf16[2,3,128,128]{3,2,1,0:T(8,128)(2,1)S(1)} collective-permute-done((bf16[2,3,128,128]{3,2,1,0:T(8,128)(2,1)S(1)}, bf16[2,3,128,128]{3,2,1,0:T(8,128)(2,1)S(1)}, u32[]{:S(2)}, u32[]{:S(2)}) %collective-permute-start.5) | collective-permute-done | bytes 196640 | tf_op jit(solution)/shard_map/ppermute | solution.py:23
  66.6 3.7 %collective-permute-start.7 = (bf16[16,128,128]{2,1,0:T(8,128)(2,1)S(1)}, bf16[16,128,128]{2,1,0:T(8,128)(2,1)S(1)}, u32[]{:S(2)}, u32[]{:S(2)}) collective-permute-start(bf16[16,128,128]{2,1,0:T(8,128)(2,1)S(1)} %get-tuple-element.62.refs_0_), channel_id=1, source_target_pairs={{16,0},{17,1},{18,2},{19,3},{20,4},{21,5},{22,6},{23,7},{24,8},{25... | collective-permute-start | bytes 1572872 | tf_op jit(solution)/shard_map/ppermute | solution.py:23
  70.5 3.5 %collective-permute-start.10 = (bf16[16,128,128]{2,1,0:T(8,128)(2,1)S(1)}, bf16[16,128,128]{2,1,0:T(8,128)(2,1)S(1)}, u32[]{:S(2)}, u32[]{:S(2)}) collective-permute-start(bf16[16,128,128]{2,1,0:T(8,128)(2,1)S(1)} %get-tuple-element.61.refs_4_), channel_id=1, source_target_pairs={{16,0},{17,1},{18,2},{19,3},{20,4},{21,5},{22,6},{23,7},{24,8},{25... | collective-permute-start | bytes 1572872 | tf_op jit(solution)/shard_map/ppermute | solution.py:23
  83.4 4.9 %collective-permute-start.8 = (bf16[16,128,128]{2,1,0:T(8,128)(2,1)S(1)}, bf16[16,128,128]{2,1,0:T(8,128)(2,1)}, u32[]{:S(2)}, u32[]{:S(2)}) collective-permute-start(bf16[16,128,128]{2,1,0:T(8,128)(2,1)S(1)} %collective-permute-done.7.refs_1_), channel_id=1, source_target_pairs={{16,0},{17,1},{18,2},{19,3},{20,4},{21,5},{22,6},{23,7},{24,8},{25... | collective-permute-start | bytes 1572872 | tf_op jit(solution)/shard_map/ppermute | solution.py:23
  90.0 4.2 %spread_weights.1 = (bf16[64,256,128]{2,1,0:T(8,128)(2,1)S(1)}, bf16[64,256,128]{2,1,0:T(8,128)(2,1)S(1)}) custom-call(s32[128]{0:T(128)S(1)} %fusion.17.up_at, s32[128]{0:T(128)S(1)} %bitcast.112, s32[128]{0:T(128)S(1)} %fusion.18.down_at, s32[128]{0:T(128)S(1)} %bitcast.114, bf16[8,2,8,64,128]{4,3,2,1,0:T(8,128)(2,1)S(1)} %bitcast.106), custom_call_target="tpu_custom_call" | custom-call | bytes 12582912 | tf_op jit(solution)/shard_map/spread_weights/pallas_call | solution.py:102
  94.6 4.8 %collective-permute-done.12.refs_6_ = bf16[16,128,128]{2,1,0:T(8,128)(2,1)} collective-permute-done((bf16[16,128,128]{2,1,0:T(8,128)(2,1)S(1)}, bf16[16,128,128]{2,1,0:T(8,128)(2,1)}, u32[]{:S(2)}, u32[]{:S(2)}) %collective-permute-start.12) | collective-permute-done | bytes 524320 | tf_op jit(solution)/shard_map/ppermute | solution.py:23
  101.4 4.9 %forward.1 = (bf16[512,128]{1,0:T(8,128)(2,1)}, f32[128,256]{1,0:T(8,128)S(1)}) custom-call(bf16[16,128,128]{2,1,0:T(8,128)(2,1)S(1)} %get-tuple-element.62.refs_0_, bf16[16,128,128]{2,1,0:T(8,128)(2,1)S(1)} %collective-permute-done.7.refs_1_, bf16[16,128,128]{2,1,0:T(8,128)(2,1)} %collective-permute-done.8.refs_2_, ...), custom_call_target="tpu_custom_call" | custom-call | flops 1073741824 | bytes 12582912 | tf_op jit(solution)/shard_map/forward/pallas_call | solution.py:150
  106.3 11.8 %all-to-all-start = ((bf16[64,8,128]{2,1,0:T(8,128)(2,1)}), bf16[64,8,128]{2,1,0:T(8,128)(2,1)S(1)}, u32[]{:S(2)}, u32[]{:S(2)}) async-start(bf16[64,8,128]{2,1,0:T(8,128)(2,1)} %bitcast.23), calls=%async_computation | async-start | bytes 262144 | tf_op jit(solution)/shard_map/all_to_all | solution.py:291
  119.3 14.4 %all-to-all-done = bf16[64,8,128]{2,1,0:T(8,128)(2,1)S(1)} async-done(((bf16[64,8,128]{2,1,0:T(8,128)(2,1)}), bf16[64,8,128]{2,1,0:T(8,128)(2,1)S(1)}, u32[]{:S(2)}, u32[]{:S(2)}) %all-to-all-start) | async-done | bytes 131104 | tf_op jit(solution)/shard_map/all_to_all | solution.py:291
  134.7 20.6 %all_to_all.20 = bf16[64,8,128]{2,1,0:T(8,128)(2,1)S(1)} all-to-all(bf16[64,8,128]{2,1,0:T(8,128)(2,1)S(1)} %fusion), channel_id=1, replica_groups=mesh['dp'=8,'tensor'=64] {'tensor'}, dimensions={0} | all-to-all | bytes 262144 | tf_op jit(solution)/shard_map/all_to_all | solution.py:291
  155.3 10.4 %weight_terms.1 = (bf16[8,2,8,64,128]{4,3,2,1,0:T(8,128)(2,1)}, bf16[128,256]{1,0:T(8,128)(2,1)S(1)}) custom-call(s32[128]{0:T(128)S(1)} %fusion.17.up_at, s32[128]{0:T(128)S(1)} %bitcast.113, s32[128]{0:T(128)S(1)} %fusion.18.down_at, s32[128]{0:T(128)S(1)} %bitcast.115, bf16[16,128,128]{2,1,0:T(8,128)(2,1)S(1)} %get-tuple-element.62.refs_0_, ...), custom_call_target="tpu_custom_call" | custom-call | flops 1610612736 | bytes 14680064 | tf_op jit(solution)/shard_map/weight_terms/pallas_call | solution.py:236
  165.8 4.8 %all-to-all-start.2 = ((bf16[8,2,8,64,128]{4,3,2,1,0:T(8,128)(2,1)}), bf16[8,2,8,64,128]{4,3,2,1,0:T(8,128)(2,1)S(1)}, u32[]{:S(2)}, u32[]{:S(2)}) async-start(bf16[8,2,8,64,128]{4,3,2,1,0:T(8,128)(2,1)} %get-tuple-element.28), calls=%async_computation.2 | async-start | bytes 4194304 | tf_op jit(solution)/shard_map/all_to_all | solution.py:321
  176.9 4.4 %collective-permute-start.15 = (bf16[16,128,128]{2,1,0:T(8,128)(2,1)S(1)}, bf16[16,128,128]{2,1,0:T(8,128)(2,1)S(1)}, u32[]{:S(2)}, u32[]{:S(2)}) collective-permute-start(bf16[16,128,128]{2,1,0:T(8,128)(2,1)S(1)} %get-tuple-element.27), channel_id=1, source_target_pairs={{16,0},{17,1},{18,2},{19,3},{20,4},{21,5},{22,6},{23,7},{24,8},{25... | collective-permute-start | bytes 1572872 | tf_op jit(solution)/shard_map/ppermute | solution.py:23
  181.4 10.0 %collective-permute-done.13 = bf16[16,128,128]{2,1,0:T(8,128)(2,1)S(1)} collective-permute-done((bf16[16,128,128]{2,1,0:T(8,128)(2,1)S(1)}, bf16[16,128,128]{2,1,0:T(8,128)(2,1)S(1)}, u32[]{:S(2)}, u32[]{:S(2)}) %collective-permute-start.13) | collective-permute-done | bytes 524320 | tf_op jit(solution)/shard_map/ppermute | solution.py:23
  196.0 4.2 %collective-permute-start.16 = (bf16[8,128,128]{2,1,0:T(8,128)(2,1)S(1)}, bf16[8,128,128]{2,1,0:T(8,128)(2,1)S(1)}, u32[]{:S(2)}, u32[]{:S(2)}) collective-permute-start(bf16[8,128,128]{2,1,0:T(8,128)(2,1)S(1)} %get-tuple-element.44), channel_id=1, source_target_pairs={{16,0},{17,1},{18,2},{19,3},{20,4},{21,5},{22,6},{23,7},{24,8},{25... | collective-permute-start | bytes 786440 | tf_op jit(solution)/shard_map/ppermute | solution.py:23
  200.2 3.5 %collective-permute-done.14 = bf16[8,128,128]{2,1,0:T(8,128)(2,1)S(1)} collective-permute-done((bf16[8,128,128]{2,1,0:T(8,128)(2,1)S(1)}, bf16[8,128,128]{2,1,0:T(8,128)(2,1)S(1)}, u32[]{:S(2)}, u32[]{:S(2)}) %collective-permute-start.14) | collective-permute-done | bytes 262176 | tf_op jit(solution)/shard_map/ppermute | solution.py:23
  208.3 3.6 %all-to-all-start.3 = ((bf16[16,128,128]{2,1,0:T(8,128)(2,1)}), bf16[16,128,128]{2,1,0:T(8,128)(2,1)S(1)}, u32[]{:S(2)}, u32[]{:S(2)}) async-start(bf16[16,128,128]{2,1,0:T(8,128)(2,1)} %pad_maximum_fusion), calls=%async_computation.3 | async-start | bytes 1048576 | tf_op jit(solution)/shard_map/all_to_all | solution.py:331
  211.9 20.2 %all-gather.7.cloned.1.call-done = bf16[8,16,4096]{2,1,0:T(8,128)(2,1)} async-done(((bf16[2,16,4096]{2,1,0:T(8,128)(2,1)}), bf16[8,16,4096]{2,1,0:T(8,128)(2,1)}) %all-gather.7.cloned.1.call-update) | async-done | bytes 1048592 | tf_op jit(solution)/shard_map/all_gather | solution.py:332
  234.1 4.4 %all-to-all-done.3.parts = bf16[16,128,128]{2,1,0:T(8,128)(2,1)S(1)} async-done(((bf16[16,128,128]{2,1,0:T(8,128)(2,1)}), bf16[16,128,128]{2,1,0:T(8,128)(2,1)S(1)}, u32[]{:S(2)}, u32[]{:S(2)}) %all-to-all-start.3) | async-done | bytes 524320 | tf_op jit(solution)/shard_map/all_to_all | solution.py:331
  (97 shorter events, 52.7 us)
Async XLA Ops:
  7.2 81.2 %copy-start.6 = (s32[1,128]{1,0:T(1,128)S(1)}, s32[1,128]{1,0:T(1,128)}, u32[]{:S(2)}) copy-start(s32[1,128]{1,0:T(1,128)} %param.17) | copy-start | bytes 1540
  7.2 81.2 %all-gather.5.cloned.1.call-start = ((), (), s32[]{:S(2)}) async-start(), calls=%async_computation.4 | async-start | bytes 2359296 | tf_op jit(solution)/shard_map/all_gather | solution.py:350
  8.1 20.6 %collective-permute-start = (bf16[2,1,128,128]{3,2,1,0:T(8,128)(2,1)S(1)}, bf16[2,1,128,128]{3,2,1,0:T(8,128)(2,1)S(1)}, u32[]{:S(2)}, u32[]{:S(2)}) collective-permute-start(bf16[2,1,128,128]{3,2,1,0:T(8,128)(2,1)S(1)} %maximum_bitcast_fusion), channel_id=1, source_target_pairs={{5,0},{6,1},{7,2},{8,3},{9,4},{10,5},{11,6},{12,7},{13,8},{14,9},{... | collective-permute-start | bytes 196616 | tf_op jit(solution)/shard_map/ppermute | solution.py:23
  22.4 16.4 %collective-permute-start.1 = (bf16[2,1,128,128]{3,2,1,0:T(8,128)(2,1)S(1)}, bf16[2,1,128,128]{3,2,1,0:T(8,128)(2,1)S(1)}, u32[]{:S(2)}, u32[]{:S(2)}) collective-permute-start(bf16[2,1,128,128]{3,2,1,0:T(8,128)(2,1)S(1)} %maximum_bitcast_fusion), channel_id=1, source_target_pairs={{11,0},{12,1},{13,2},{14,3},{15,4},{0,5},{1,6},{2,7},{3,8},{4,9},{... | collective-permute-start | bytes 196616 | tf_op jit(solution)/shard_map/ppermute | solution.py:23
  41.8 15.7 %collective-permute-start.2 = (bf16[2,3,128,128]{3,2,1,0:T(8,128)(2,1)S(1)}, bf16[2,3,128,128]{3,2,1,0:T(8,128)(2,1)S(1)}, u32[]{:S(2)}, u32[]{:S(2)}) collective-permute-start(bf16[2,3,128,128]{3,2,1,0:T(8,128)(2,1)S(1)} %pad_maximum_fusion.4), channel_id=1, source_target_pairs={{1,0},{2,1},{3,2},{4,3},{5,4},{6,5},{7,6},{8,7},{9,8},{10,9},{11,1... | collective-permute-start | bytes 589832 | tf_op jit(solution)/shard_map/ppermute | solution.py:23
  44.2 13.3 %collective-permute-start.3 = (bf16[2,3,128,128]{3,2,1,0:T(8,128)(2,1)S(1)}, bf16[2,3,128,128]{3,2,1,0:T(8,128)(2,1)S(1)}, u32[]{:S(2)}, u32[]{:S(2)}) collective-permute-start(bf16[2,3,128,128]{3,2,1,0:T(8,128)(2,1)S(1)} %pad_maximum_fusion.4), channel_id=1, source_target_pairs={{15,0},{0,1},{1,2},{2,3},{3,4},{4,5},{5,6},{6,7},{7,8},{8,9},{9,10... | collective-permute-start | bytes 589832 | tf_op jit(solution)/shard_map/ppermute | solution.py:23
  47.7 9.9 %collective-permute-start.4 = (bf16[2,3,128,128]{3,2,1,0:T(8,128)(2,1)S(1)}, bf16[2,3,128,128]{3,2,1,0:T(8,128)(2,1)S(1)}, u32[]{:S(2)}, u32[]{:S(2)}) collective-permute-start(bf16[2,3,128,128]{3,2,1,0:T(8,128)(2,1)S(1)} %pad_maximum_fusion.4), channel_id=1, source_target_pairs={{2,0},{3,1},{4,2},{5,3},{6,4},{7,5},{8,6},{9,7},{10,8},{11,9},{12,... | collective-permute-start | bytes 589832 | tf_op jit(solution)/shard_map/ppermute | solution.py:23
  50.0 13.2 %collective-permute-start.5 = (bf16[2,3,128,128]{3,2,1,0:T(8,128)(2,1)S(1)}, bf16[2,3,128,128]{3,2,1,0:T(8,128)(2,1)S(1)}, u32[]{:S(2)}, u32[]{:S(2)}) collective-permute-start(bf16[2,3,128,128]{3,2,1,0:T(8,128)(2,1)S(1)} %pad_maximum_fusion.4), channel_id=1, source_target_pairs={{14,0},{15,1},{0,2},{1,3},{2,4},{3,5},{4,6},{5,7},{6,8},{7,9},{8,1... | collective-permute-start | bytes 589832 | tf_op jit(solution)/shard_map/ppermute | solution.py:23
  54.4 8.8 %collective-permute-start.6 = (bf16[2,1,128,128]{3,2,1,0:T(8,128)(2,1)S(1)}, bf16[2,1,128,128]{3,2,1,0:T(8,128)(2,1)S(1)}, u32[]{:S(2)}, u32[]{:S(2)}) collective-permute-start(bf16[2,1,128,128]{3,2,1,0:T(8,128)(2,1)S(1)} %collective-permute-done.first), channel_id=1, source_target_pairs={{3,0},{4,1},{5,2},{6,3},{7,4},{8,5},{9,6},{10,7},{11,8},{12,9},{13... | collective-permute-start | bytes 196616 | tf_op jit(solution)/shard_map/ppermute | solution.py:23
  63.2 14.9 %collective-permute-start.11 = (bf16[16,128,128]{2,1,0:T(8,128)(2,1)S(1)}, bf16[16,128,128]{2,1,0:T(8,128)(2,1)S(1)}, u32[]{:S(2)}, u32[]{:S(2)}) collective-permute-start(bf16[16,128,128]{2,1,0:T(8,128)(2,1)S(1)} %get-tuple-element.61.refs_4_), channel_id=1, source_target_pairs={{48,0},{49,1},{50,2},{51,3},{52,4},{53,5},{54,6},{55,7},{56,8},{57... | collective-permute-start | bytes 1572872 | tf_op jit(solution)/shard_map/ppermute | solution.py:23
  66.6 16.8 %collective-permute-start.7 = (bf16[16,128,128]{2,1,0:T(8,128)(2,1)S(1)}, bf16[16,128,128]{2,1,0:T(8,128)(2,1)S(1)}, u32[]{:S(2)}, u32[]{:S(2)}) collective-permute-start(bf16[16,128,128]{2,1,0:T(8,128)(2,1)S(1)} %get-tuple-element.62.refs_0_), channel_id=1, source_target_pairs={{16,0},{17,1},{18,2},{19,3},{20,4},{21,5},{22,6},{23,7},{24,8},{25... | collective-permute-start | bytes 1572872 | tf_op jit(solution)/shard_map/ppermute | solution.py:23
  70.5 24.1 %collective-permute-start.10 = (bf16[16,128,128]{2,1,0:T(8,128)(2,1)S(1)}, bf16[16,128,128]{2,1,0:T(8,128)(2,1)S(1)}, u32[]{:S(2)}, u32[]{:S(2)}) collective-permute-start(bf16[16,128,128]{2,1,0:T(8,128)(2,1)S(1)} %get-tuple-element.61.refs_4_), channel_id=1, source_target_pairs={{16,0},{17,1},{18,2},{19,3},{20,4},{21,5},{22,6},{23,7},{24,8},{25... | collective-permute-start | bytes 1572872 | tf_op jit(solution)/shard_map/ppermute | solution.py:23
  73.9 20.7 %collective-permute-start.9 = (bf16[16,128,128]{2,1,0:T(8,128)(2,1)S(1)}, bf16[16,128,128]{2,1,0:T(8,128)(2,1)S(1)}, u32[]{:S(2)}, u32[]{:S(2)}) collective-permute-start(bf16[16,128,128]{2,1,0:T(8,128)(2,1)S(1)} %get-tuple-element.62.refs_0_), channel_id=1, source_target_pairs={{48,0},{49,1},{50,2},{51,3},{52,4},{53,5},{54,6},{55,7},{56,8},{57... | collective-permute-start | bytes 1572872 | tf_op jit(solution)/shard_map/ppermute | solution.py:23
  78.2 21.3 %collective-permute-start.12 = (bf16[16,128,128]{2,1,0:T(8,128)(2,1)S(1)}, bf16[16,128,128]{2,1,0:T(8,128)(2,1)}, u32[]{:S(2)}, u32[]{:S(2)}) collective-permute-start(bf16[16,128,128]{2,1,0:T(8,128)(2,1)S(1)} %collective-permute-done.11.refs_7_), channel_id=1, source_target_pairs={{48,0},{49,1},{50,2},{51,3},{52,4},{53,5},{54,6},{55,7},{56,8},{57... | collective-permute-start | bytes 1572872 | tf_op jit(solution)/shard_map/ppermute | solution.py:23
  83.4 18.0 %collective-permute-start.8 = (bf16[16,128,128]{2,1,0:T(8,128)(2,1)S(1)}, bf16[16,128,128]{2,1,0:T(8,128)(2,1)}, u32[]{:S(2)}, u32[]{:S(2)}) collective-permute-start(bf16[16,128,128]{2,1,0:T(8,128)(2,1)S(1)} %collective-permute-done.7.refs_1_), channel_id=1, source_target_pairs={{16,0},{17,1},{18,2},{19,3},{20,4},{21,5},{22,6},{23,7},{24,8},{25... | collective-permute-start | bytes 1572872 | tf_op jit(solution)/shard_map/ppermute | solution.py:23
  106.3 27.4 %all-to-all-start = ((bf16[64,8,128]{2,1,0:T(8,128)(2,1)}), bf16[64,8,128]{2,1,0:T(8,128)(2,1)S(1)}, u32[]{:S(2)}, u32[]{:S(2)}) async-start(bf16[64,8,128]{2,1,0:T(8,128)(2,1)} %bitcast.23), calls=%async_computation | async-start | bytes 262144 | tf_op jit(solution)/shard_map/all_to_all | solution.py:291
  165.8 40.3 %all-to-all-start.2 = ((bf16[8,2,8,64,128]{4,3,2,1,0:T(8,128)(2,1)}), bf16[8,2,8,64,128]{4,3,2,1,0:T(8,128)(2,1)S(1)}, u32[]{:S(2)}, u32[]{:S(2)}) async-start(bf16[8,2,8,64,128]{4,3,2,1,0:T(8,128)(2,1)} %get-tuple-element.28), calls=%async_computation.2 | async-start | bytes 4194304 | tf_op jit(solution)/shard_map/all_to_all | solution.py:321
  170.6 61.5 %all-gather.7.cloned.1.call-start = ((), (), s32[]{:S(2)}) async-start(), calls=%async_computation.5 | async-start | bytes 1310720 | tf_op jit(solution)/shard_map/all_gather | solution.py:332
  174.3 17.1 %collective-permute-start.13 = (bf16[16,128,128]{2,1,0:T(8,128)(2,1)S(1)}, bf16[16,128,128]{2,1,0:T(8,128)(2,1)S(1)}, u32[]{:S(2)}, u32[]{:S(2)}) collective-permute-start(bf16[16,128,128]{2,1,0:T(8,128)(2,1)S(1)} %get-tuple-element.26), channel_id=1, source_target_pairs={{48,0},{49,1},{50,2},{51,3},{52,4},{53,5},{54,6},{55,7},{56,8},{57... | collective-permute-start | bytes 1572872 | tf_op jit(solution)/shard_map/ppermute | solution.py:23
  176.9 15.6 %collective-permute-start.15 = (bf16[16,128,128]{2,1,0:T(8,128)(2,1)S(1)}, bf16[16,128,128]{2,1,0:T(8,128)(2,1)S(1)}, u32[]{:S(2)}, u32[]{:S(2)}) collective-permute-start(bf16[16,128,128]{2,1,0:T(8,128)(2,1)S(1)} %get-tuple-element.27), channel_id=1, source_target_pairs={{16,0},{17,1},{18,2},{19,3},{20,4},{21,5},{22,6},{23,7},{24,8},{25... | collective-permute-start | bytes 1572872 | tf_op jit(solution)/shard_map/ppermute | solution.py:23
  192.7 11.1 %collective-permute-start.14 = (bf16[8,128,128]{2,1,0:T(8,128)(2,1)S(1)}, bf16[8,128,128]{2,1,0:T(8,128)(2,1)S(1)}, u32[]{:S(2)}, u32[]{:S(2)}) collective-permute-start(bf16[8,128,128]{2,1,0:T(8,128)(2,1)S(1)} %get-tuple-element.43), channel_id=1, source_target_pairs={{48,0},{49,1},{50,2},{51,3},{52,4},{53,5},{54,6},{55,7},{56,8},{57... | collective-permute-start | bytes 786440 | tf_op jit(solution)/shard_map/ppermute | solution.py:23
  196.0 8.9 %collective-permute-start.16 = (bf16[8,128,128]{2,1,0:T(8,128)(2,1)S(1)}, bf16[8,128,128]{2,1,0:T(8,128)(2,1)S(1)}, u32[]{:S(2)}, u32[]{:S(2)}) collective-permute-start(bf16[8,128,128]{2,1,0:T(8,128)(2,1)S(1)} %get-tuple-element.44), channel_id=1, source_target_pairs={{16,0},{17,1},{18,2},{19,3},{20,4},{21,5},{22,6},{23,7},{24,8},{25... | collective-permute-start | bytes 786440 | tf_op jit(solution)/shard_map/ppermute | solution.py:23
  208.3 30.1 %all-to-all-start.3 = ((bf16[16,128,128]{2,1,0:T(8,128)(2,1)}), bf16[16,128,128]{2,1,0:T(8,128)(2,1)S(1)}, u32[]{:S(2)}, u32[]{:S(2)}) async-start(bf16[16,128,128]{2,1,0:T(8,128)(2,1)} %pad_maximum_fusion), calls=%async_computation.3 | async-start | bytes 1048576 | tf_op jit(solution)/shard_map/all_to_all | solution.py:331
  232.1 6.3 %collective-permute-start.17 = (bf16[4,2,16,4096]{3,2,1,0:T(8,128)(2,1)}, bf16[4,2,16,4096]{3,2,1,0:T(8,128)(2,1)S(1)}, u32[]{:S(2)}, u32[]{:S(2)}) collective-permute-start(bf16[4,2,16,4096]{3,2,1,0:T(8,128)(2,1)} %bitcast.107), channel_id=1, source_target_pairs={{64,0},{0,64},{192,128},{128,192},{320,256},{256,320},{448,384},{3... | collective-permute-start | bytes 3145736 | tf_op jit(solution)/shard_map/ppermute | solution.py:27
  (13 other events, 392.4 us)
Sparse Core Ops, SparseCore 0:
  41.9 24.1 all-gather.4
  208.4 23.6 all-gather.6

commit v6 on v5

--- a/solution.py
+++ b/solution.py
@@ -321,12 +321,13 @@
     slots = lax.all_to_all(slots, "dp", 0, 0, tiled=True)
     on_plus, on_minus = add(later[:half], got_plus[:half]), add(later[half:], got_minus[half:])
     low, high = from_tensor(on_plus, -1, 0), from_tensor(on_minus, 1, 0)
+    slots, *_ = order((slots, on_plus, on_minus))
+    own = jnp.sum(slots.astype(F32), axis=0).astype(BF)
+    own = jnp.stack([unpack(jnp.swapaxes(own[0], 1, 2), True), unpack(own[1])])
+    low, high, own = order((low, high, own))
     low = add(near[:half], low, got_minus[:half])
     high = add(near[half:], got_plus[half:], high)
     column = jnp.concatenate([low, high])
-    slots, *_ = order((slots, on_plus, on_minus))
-    own = jnp.sum(slots.astype(F32), axis=0).astype(BF)
-    own = jnp.stack([unpack(jnp.swapaxes(own[0], 1, 2), True), unpack(own[1])])
     column, own = order((column, own))
     parts = lax.all_to_all(column, "tensor", 0, 0, tiled=True, axis_index_groups=Z_GROUPS)
     mine = lax.all_gather(own, "dp", axis=0, axis_index_groups=Y_GROUPS)

time: 251 us -> 251 us (level)
    unnamed x33 -> x37, local copies, waits for them, and re-layouts: 6.98 us -> 6.99 us
  transfers between devices with their start and end apart: 23 -> 23, of which waited for: 15 -> 15; matrix products, arithmetic and copies ran while one was open for 1% -> 2% of each run, Pallas kernels for 2% -> 2%
where the time goes in v6:
time: 251 us; the launch traced here: 248 us
  starting transfers between devices  89.8 us (36%)
  waiting for transfers between devices  83.7 us (33%)
  Pallas kernels  23.5 us (9%)
  blocking collectives  20.6 us (8%)
  between operations  14.6 us (6%)
  local copies, waits for them, and re-layouts  9.13 us (4%)
  other arithmetic  5.49 us (2%)
    ppermute x17, starting transfers between devices, from_tensor(): return lax.ppermute(value, 'tensor', pairs)  67.7 us
    ppermute x17, waiting for transfers between devices, from_tensor(): return lax.ppermute(value, 'tensor', pairs)  44.6 us
    all_to_all x1, blocking collectives, exchange(): lax.all_to_all(rows.reshape(64, 8, 128), 'tensor', 0, 0, tiled=True)  20.6 us
    all_gather x1, waiting for transfers between devices, reduce_all(): mine = lax.all_gather(own, 'dp', axis=0, axis_index_groups=Y_GROUPS)  20.2 us
    all_to_all x1, waiting for transfers between devices, exchange(): lax.all_to_all(rows.reshape(64, 8, 128), 'tensor', 0, 0, tiled=True)  14.4 us
    all_to_all x1, starting transfers between devices, exchange(): lax.all_to_all(rows.reshape(64, 8, 128), 'tensor', 0, 0, tiled=True)  11.8 us
    pallas_call x1, Pallas kernels, weight_terms(): pl.pallas_call(weight_kernel, in_specs=[SM] * 4 + [VM] * 10, out_specs=[V...  10.4 us
    unnamed x37, local copies, waits for them, and re-layouts  6.99 us
  transfers between devices with their start and end apart: 23, of which 15 were waited for; matrix products, arithmetic and copies ran while one was open for 2% of the time, Pallas kernels for 2%

profile of v6, /device:TPU:24, one launch (start us, length us, event | category | flops | bytes accessed | tf_op | source)
XLA Modules:
  0.0 247.9 jit_solution(8378962908879072722)
XLA Ops:
  8.1 14.4 %collective-permute-start = (bf16[2,1,128,128]{3,2,1,0:T(8,128)(2,1)S(1)}, bf16[2,1,128,128]{3,2,1,0:T(8,128)(2,1)S(1)}, u32[]{:S(2)}, u32[]{:S(2)}) collective-permute-start(bf16[2,1,128,128]{3,2,1,0:T(8,128)(2,1)S(1)} %maximum_bitcast_fusion), channel_id=1, source_target_pairs={{5,0},{6,1},{7,2},{8,3},{9,4},{10,5},{11,6},{12,7},{13,8},{14,9},{... | collective-permute-start | bytes 196616 | tf_op jit(solution)/shard_map/ppermute | solution.py:23
  24.4 4.3 %collective-permute-done.first = bf16[2,1,128,128]{3,2,1,0:T(8,128)(2,1)S(1)} collective-permute-done((bf16[2,1,128,128]{3,2,1,0:T(8,128)(2,1)S(1)}, bf16[2,1,128,128]{3,2,1,0:T(8,128)(2,1)S(1)}, u32[]{:S(2)}, u32[]{:S(2)}) %collective-permute-start) | collective-permute-done | bytes 65568 | tf_op jit(solution)/shard_map/ppermute | solution.py:23
  28.6 10.2 %collective-permute-done.1.second = bf16[2,1,128,128]{3,2,1,0:T(8,128)(2,1)S(1)} collective-permute-done((bf16[2,1,128,128]{3,2,1,0:T(8,128)(2,1)S(1)}, bf16[2,1,128,128]{3,2,1,0:T(8,128)(2,1)S(1)}, u32[]{:S(2)}, u32[]{:S(2)}) %collective-permute-start.1) | collective-permute-done | bytes 65568 | tf_op jit(solution)/shard_map/ppermute | solution.py:23
  44.2 3.4 %collective-permute-start.3 = (bf16[2,3,128,128]{3,2,1,0:T(8,128)(2,1)S(1)}, bf16[2,3,128,128]{3,2,1,0:T(8,128)(2,1)S(1)}, u32[]{:S(2)}, u32[]{:S(2)}) collective-permute-start(bf16[2,3,128,128]{3,2,1,0:T(8,128)(2,1)S(1)} %pad_maximum_fusion.4), channel_id=1, source_target_pairs={{15,0},{0,1},{1,2},{2,3},{3,4},{4,5},{5,6},{6,7},{7,8},{8,9},{9,10... | collective-permute-start | bytes 589832 | tf_op jit(solution)/shard_map/ppermute | solution.py:23
  50.0 4.4 %collective-permute-start.5 = (bf16[2,3,128,128]{3,2,1,0:T(8,128)(2,1)S(1)}, bf16[2,3,128,128]{3,2,1,0:T(8,128)(2,1)S(1)}, u32[]{:S(2)}, u32[]{:S(2)}) collective-permute-start(bf16[2,3,128,128]{3,2,1,0:T(8,128)(2,1)S(1)} %pad_maximum_fusion.4), channel_id=1, source_target_pairs={{14,0},{15,1},{0,2},{1,3},{2,4},{3,5},{4,6},{5,7},{6,8},{7,9},{8,1... | collective-permute-start | bytes 589832 | tf_op jit(solution)/shard_map/ppermute | solution.py:23
  57.6 5.5 %collective-permute-done.5 = bf16[2,3,128,128]{3,2,1,0:T(8,128)(2,1)S(1)} collective-permute-done((bf16[2,3,128,128]{3,2,1,0:T(8,128)(2,1)S(1)}, bf16[2,3,128,128]{3,2,1,0:T(8,128)(2,1)S(1)}, u32[]{:S(2)}, u32[]{:S(2)}) %collective-permute-start.5) | collective-permute-done | bytes 196640 | tf_op jit(solution)/shard_map/ppermute | solution.py:23
  63.2 3.4 %collective-permute-start.11 = (bf16[16,128,128]{2,1,0:T(8,128)(2,1)S(1)}, bf16[16,128,128]{2,1,0:T(8,128)(2,1)S(1)}, u32[]{:S(2)}, u32[]{:S(2)}) collective-permute-start(bf16[16,128,128]{2,1,0:T(8,128)(2,1)S(1)} %get-tuple-element.67.refs_4_), channel_id=1, source_target_pairs={{48,0},{49,1},{50,2},{51,3},{52,4},{53,5},{54,6},{55,7},{56,8},{57... | collective-permute-start | bytes 1572872 | tf_op jit(solution)/shard_map/ppermute | solution.py:23
  66.6 3.7 %collective-permute-start.7 = (bf16[16,128,128]{2,1,0:T(8,128)(2,1)S(1)}, bf16[16,128,128]{2,1,0:T(8,128)(2,1)S(1)}, u32[]{:S(2)}, u32[]{:S(2)}) collective-permute-start(bf16[16,128,128]{2,1,0:T(8,128)(2,1)S(1)} %get-tuple-element.68.refs_0_), channel_id=1, source_target_pairs={{16,0},{17,1},{18,2},{19,3},{20,4},{21,5},{22,6},{23,7},{24,8},{25... | collective-permute-start | bytes 1572872 | tf_op jit(solution)/shard_map/ppermute | solution.py:23
  70.5 3.5 %collective-permute-start.10 = (bf16[16,128,128]{2,1,0:T(8,128)(2,1)S(1)}, bf16[16,128,128]{2,1,0:T(8,128)(2,1)S(1)}, u32[]{:S(2)}, u32[]{:S(2)}) collective-permute-start(bf16[16,128,128]{2,1,0:T(8,128)(2,1)S(1)} %get-tuple-element.67.refs_4_), channel_id=1, source_target_pairs={{16,0},{17,1},{18,2},{19,3},{20,4},{21,5},{22,6},{23,7},{24,8},{25... | collective-permute-start | bytes 1572872 | tf_op jit(solution)/shard_map/ppermute | solution.py:23
  83.4 4.9 %collective-permute-start.8 = (bf16[16,128,128]{2,1,0:T(8,128)(2,1)S(1)}, bf16[16,128,128]{2,1,0:T(8,128)(2,1)}, u32[]{:S(2)}, u32[]{:S(2)}) collective-permute-start(bf16[16,128,128]{2,1,0:T(8,128)(2,1)S(1)} %collective-permute-done.7.refs_1_), channel_id=1, source_target_pairs={{16,0},{17,1},{18,2},{19,3},{20,4},{21,5},{22,6},{23,7},{24,8},{25... | collective-permute-start | bytes 1572872 | tf_op jit(solution)/shard_map/ppermute | solution.py:23
  90.0 4.2 %spread_weights.1 = (bf16[64,256,128]{2,1,0:T(8,128)(2,1)S(1)}, bf16[64,256,128]{2,1,0:T(8,128)(2,1)S(1)}) custom-call(s32[128]{0:T(128)S(1)} %fusion.17.up_at, s32[128]{0:T(128)S(1)} %bitcast.112, s32[128]{0:T(128)S(1)} %fusion.18.down_at, s32[128]{0:T(128)S(1)} %bitcast.114, bf16[8,2,8,64,128]{4,3,2,1,0:T(8,128)(2,1)S(1)} %bitcast.106), custom_call_target="tpu_custom_call" | custom-call | bytes 12582912 | tf_op jit(solution)/shard_map/spread_weights/pallas_call | solution.py:102
  94.6 4.8 %collective-permute-done.12.refs_6_ = bf16[16,128,128]{2,1,0:T(8,128)(2,1)} collective-permute-done((bf16[16,128,128]{2,1,0:T(8,128)(2,1)S(1)}, bf16[16,128,128]{2,1,0:T(8,128)(2,1)}, u32[]{:S(2)}, u32[]{:S(2)}) %collective-permute-start.12) | collective-permute-done | bytes 524320 | tf_op jit(solution)/shard_map/ppermute | solution.py:23
  101.4 4.9 %forward.1 = (bf16[512,128]{1,0:T(8,128)(2,1)}, f32[128,256]{1,0:T(8,128)S(1)}) custom-call(bf16[16,128,128]{2,1,0:T(8,128)(2,1)S(1)} %get-tuple-element.68.refs_0_, bf16[16,128,128]{2,1,0:T(8,128)(2,1)S(1)} %collective-permute-done.7.refs_1_, bf16[16,128,128]{2,1,0:T(8,128)(2,1)} %collective-permute-done.8.refs_2_, ...), custom_call_target="tpu_custom_call" | custom-call | flops 1073741824 | bytes 12582912 | tf_op jit(solution)/shard_map/forward/pallas_call | solution.py:150
  106.3 11.8 %all-to-all-start = ((bf16[64,8,128]{2,1,0:T(8,128)(2,1)}), bf16[64,8,128]{2,1,0:T(8,128)(2,1)S(1)}, u32[]{:S(2)}, u32[]{:S(2)}) async-start(bf16[64,8,128]{2,1,0:T(8,128)(2,1)} %bitcast.23), calls=%async_computation | async-start | bytes 262144 | tf_op jit(solution)/shard_map/all_to_all | solution.py:291
  119.3 14.4 %all-to-all-done = bf16[64,8,128]{2,1,0:T(8,128)(2,1)S(1)} async-done(((bf16[64,8,128]{2,1,0:T(8,128)(2,1)}), bf16[64,8,128]{2,1,0:T(8,128)(2,1)S(1)}, u32[]{:S(2)}, u32[]{:S(2)}) %all-to-all-start) | async-done | bytes 131104 | tf_op jit(solution)/shard_map/all_to_all | solution.py:291
  134.7 20.6 %all_to_all.20 = bf16[64,8,128]{2,1,0:T(8,128)(2,1)S(1)} all-to-all(bf16[64,8,128]{2,1,0:T(8,128)(2,1)S(1)} %fusion), channel_id=1, replica_groups=mesh['dp'=8,'tensor'=64] {'tensor'}, dimensions={0} | all-to-all | bytes 262144 | tf_op jit(solution)/shard_map/all_to_all | solution.py:291
  155.3 10.4 %weight_terms.1 = (bf16[8,2,8,64,128]{4,3,2,1,0:T(8,128)(2,1)}, bf16[128,256]{1,0:T(8,128)(2,1)S(1)}) custom-call(s32[128]{0:T(128)S(1)} %fusion.17.up_at, s32[128]{0:T(128)S(1)} %bitcast.113, s32[128]{0:T(128)S(1)} %fusion.18.down_at, s32[128]{0:T(128)S(1)} %bitcast.115, bf16[16,128,128]{2,1,0:T(8,128)(2,1)S(1)} %get-tuple-element.68.refs_0_, ...), custom_call_target="tpu_custom_call" | custom-call | flops 1610612736 | bytes 14680064 | tf_op jit(solution)/shard_map/weight_terms/pallas_call | solution.py:236
  165.8 4.8 %all-to-all-start.2 = ((bf16[8,2,8,64,128]{4,3,2,1,0:T(8,128)(2,1)}), bf16[8,2,8,64,128]{4,3,2,1,0:T(8,128)(2,1)S(1)}, u32[]{:S(2)}, u32[]{:S(2)}) async-start(bf16[8,2,8,64,128]{4,3,2,1,0:T(8,128)(2,1)} %get-tuple-element.31), calls=%async_computation.2 | async-start | bytes 4194304 | tf_op jit(solution)/shard_map/all_to_all | solution.py:321
  176.9 4.4 %collective-permute-start.15 = (bf16[16,128,128]{2,1,0:T(8,128)(2,1)S(1)}, bf16[16,128,128]{2,1,0:T(8,128)(2,1)S(1)}, u32[]{:S(2)}, u32[]{:S(2)}) collective-permute-start(bf16[16,128,128]{2,1,0:T(8,128)(2,1)S(1)} %get-tuple-element.30), channel_id=1, source_target_pairs={{16,0},{17,1},{18,2},{19,3},{20,4},{21,5},{22,6},{23,7},{24,8},{25... | collective-permute-start | bytes 1572872 | tf_op jit(solution)/shard_map/ppermute | solution.py:23
  181.4 10.0 %collective-permute-done.13 = bf16[16,128,128]{2,1,0:T(8,128)(2,1)S(1)} collective-permute-done((bf16[16,128,128]{2,1,0:T(8,128)(2,1)S(1)}, bf16[16,128,128]{2,1,0:T(8,128)(2,1)S(1)}, u32[]{:S(2)}, u32[]{:S(2)}) %collective-permute-start.13) | collective-permute-done | bytes 524320 | tf_op jit(solution)/shard_map/ppermute | solution.py:23
  196.8 4.2 %collective-permute-start.16 = (bf16[8,128,128]{2,1,0:T(8,128)(2,1)}, bf16[8,128,128]{2,1,0:T(8,128)(2,1)}, u32[]{:S(2)}, u32[]{:S(2)}) collective-permute-start(bf16[8,128,128]{2,1,0:T(8,128)(2,1)} %get-tuple-element.49), channel_id=1, source_target_pairs={{16,0},{17,1},{18,2},{19,3},{20,4},{21,5},{22,6},{23,7},{24,8},{25... | collective-permute-start | bytes 786440 | tf_op jit(solution)/shard_map/ppermute | solution.py:23
  208.2 3.6 %all-to-all-start.3 = ((bf16[16,128,128]{2,1,0:T(8,128)(2,1)}), bf16[16,128,128]{2,1,0:T(8,128)(2,1)S(1)}, u32[]{:S(2)}, u32[]{:S(2)}) async-start(bf16[16,128,128]{2,1,0:T(8,128)(2,1)} %pad_maximum_fusion), calls=%async_computation.3 | async-start | bytes 1048576 | tf_op jit(solution)/shard_map/all_to_all | solution.py:332
  211.8 20.2 %all-gather.7.cloned.1.call-done = bf16[8,16,4096]{2,1,0:T(8,128)(2,1)} async-done(((bf16[2,16,4096]{2,1,0:T(8,128)(2,1)}), bf16[8,16,4096]{2,1,0:T(8,128)(2,1)}) %all-gather.7.cloned.1.call-update) | async-done | bytes 1048592 | tf_op jit(solution)/shard_map/all_gather | solution.py:333
  234.0 4.4 %all-to-all-done.3.parts = bf16[16,128,128]{2,1,0:T(8,128)(2,1)S(1)} async-done(((bf16[16,128,128]{2,1,0:T(8,128)(2,1)}), bf16[16,128,128]{2,1,0:T(8,128)(2,1)S(1)}, u32[]{:S(2)}, u32[]{:S(2)}) %all-to-all-start.3) | async-done | bytes 524320 | tf_op jit(solution)/shard_map/all_to_all | solution.py:332
  (101 shorter events, 52.8 us)
Async XLA Ops:
  7.2 81.2 %copy-start.6 = (s32[1,128]{1,0:T(1,128)S(1)}, s32[1,128]{1,0:T(1,128)}, u32[]{:S(2)}) copy-start(s32[1,128]{1,0:T(1,128)} %param.17) | copy-start | bytes 1540
  7.2 81.2 %all-gather.5.cloned.1.call-start = ((), (), s32[]{:S(2)}) async-start(), calls=%async_computation.4 | async-start | bytes 2359296 | tf_op jit(solution)/shard_map/all_gather | solution.py:351
  8.1 20.6 %collective-permute-start = (bf16[2,1,128,128]{3,2,1,0:T(8,128)(2,1)S(1)}, bf16[2,1,128,128]{3,2,1,0:T(8,128)(2,1)S(1)}, u32[]{:S(2)}, u32[]{:S(2)}) collective-permute-start(bf16[2,1,128,128]{3,2,1,0:T(8,128)(2,1)S(1)} %maximum_bitcast_fusion), channel_id=1, source_target_pairs={{5,0},{6,1},{7,2},{8,3},{9,4},{10,5},{11,6},{12,7},{13,8},{14,9},{... | collective-permute-start | bytes 196616 | tf_op jit(solution)/shard_map/ppermute | solution.py:23
  22.4 16.4 %collective-permute-start.1 = (bf16[2,1,128,128]{3,2,1,0:T(8,128)(2,1)S(1)}, bf16[2,1,128,128]{3,2,1,0:T(8,128)(2,1)S(1)}, u32[]{:S(2)}, u32[]{:S(2)}) collective-permute-start(bf16[2,1,128,128]{3,2,1,0:T(8,128)(2,1)S(1)} %maximum_bitcast_fusion), channel_id=1, source_target_pairs={{11,0},{12,1},{13,2},{14,3},{15,4},{0,5},{1,6},{2,7},{3,8},{4,9},{... | collective-permute-start | bytes 196616 | tf_op jit(solution)/shard_map/ppermute | solution.py:23
  41.8 15.7 %collective-permute-start.2 = (bf16[2,3,128,128]{3,2,1,0:T(8,128)(2,1)S(1)}, bf16[2,3,128,128]{3,2,1,0:T(8,128)(2,1)S(1)}, u32[]{:S(2)}, u32[]{:S(2)}) collective-permute-start(bf16[2,3,128,128]{3,2,1,0:T(8,128)(2,1)S(1)} %pad_maximum_fusion.4), channel_id=1, source_target_pairs={{1,0},{2,1},{3,2},{4,3},{5,4},{6,5},{7,6},{8,7},{9,8},{10,9},{11,1... | collective-permute-start | bytes 589832 | tf_op jit(solution)/shard_map/ppermute | solution.py:23
  44.2 13.3 %collective-permute-start.3 = (bf16[2,3,128,128]{3,2,1,0:T(8,128)(2,1)S(1)}, bf16[2,3,128,128]{3,2,1,0:T(8,128)(2,1)S(1)}, u32[]{:S(2)}, u32[]{:S(2)}) collective-permute-start(bf16[2,3,128,128]{3,2,1,0:T(8,128)(2,1)S(1)} %pad_maximum_fusion.4), channel_id=1, source_target_pairs={{15,0},{0,1},{1,2},{2,3},{3,4},{4,5},{5,6},{6,7},{7,8},{8,9},{9,10... | collective-permute-start | bytes 589832 | tf_op jit(solution)/shard_map/ppermute | solution.py:23
  47.7 9.9 %collective-permute-start.4 = (bf16[2,3,128,128]{3,2,1,0:T(8,128)(2,1)S(1)}, bf16[2,3,128,128]{3,2,1,0:T(8,128)(2,1)S(1)}, u32[]{:S(2)}, u32[]{:S(2)}) collective-permute-start(bf16[2,3,128,128]{3,2,1,0:T(8,128)(2,1)S(1)} %pad_maximum_fusion.4), channel_id=1, source_target_pairs={{2,0},{3,1},{4,2},{5,3},{6,4},{7,5},{8,6},{9,7},{10,8},{11,9},{12,... | collective-permute-start | bytes 589832 | tf_op jit(solution)/shard_map/ppermute | solution.py:23
  50.0 13.2 %collective-permute-start.5 = (bf16[2,3,128,128]{3,2,1,0:T(8,128)(2,1)S(1)}, bf16[2,3,128,128]{3,2,1,0:T(8,128)(2,1)S(1)}, u32[]{:S(2)}, u32[]{:S(2)}) collective-permute-start(bf16[2,3,128,128]{3,2,1,0:T(8,128)(2,1)S(1)} %pad_maximum_fusion.4), channel_id=1, source_target_pairs={{14,0},{15,1},{0,2},{1,3},{2,4},{3,5},{4,6},{5,7},{6,8},{7,9},{8,1... | collective-permute-start | bytes 589832 | tf_op jit(solution)/shard_map/ppermute | solution.py:23
  54.4 8.8 %collective-permute-start.6 = (bf16[2,1,128,128]{3,2,1,0:T(8,128)(2,1)S(1)}, bf16[2,1,128,128]{3,2,1,0:T(8,128)(2,1)S(1)}, u32[]{:S(2)}, u32[]{:S(2)}) collective-permute-start(bf16[2,1,128,128]{3,2,1,0:T(8,128)(2,1)S(1)} %collective-permute-done.first), channel_id=1, source_target_pairs={{3,0},{4,1},{5,2},{6,3},{7,4},{8,5},{9,6},{10,7},{11,8},{12,9},{13... | collective-permute-start | bytes 196616 | tf_op jit(solution)/shard_map/ppermute | solution.py:23
  63.2 14.9 %collective-permute-start.11 = (bf16[16,128,128]{2,1,0:T(8,128)(2,1)S(1)}, bf16[16,128,128]{2,1,0:T(8,128)(2,1)S(1)}, u32[]{:S(2)}, u32[]{:S(2)}) collective-permute-start(bf16[16,128,128]{2,1,0:T(8,128)(2,1)S(1)} %get-tuple-element.67.refs_4_), channel_id=1, source_target_pairs={{48,0},{49,1},{50,2},{51,3},{52,4},{53,5},{54,6},{55,7},{56,8},{57... | collective-permute-start | bytes 1572872 | tf_op jit(solution)/shard_map/ppermute | solution.py:23
  66.6 16.8 %collective-permute-start.7 = (bf16[16,128,128]{2,1,0:T(8,128)(2,1)S(1)}, bf16[16,128,128]{2,1,0:T(8,128)(2,1)S(1)}, u32[]{:S(2)}, u32[]{:S(2)}) collective-permute-start(bf16[16,128,128]{2,1,0:T(8,128)(2,1)S(1)} %get-tuple-element.68.refs_0_), channel_id=1, source_target_pairs={{16,0},{17,1},{18,2},{19,3},{20,4},{21,5},{22,6},{23,7},{24,8},{25... | collective-permute-start | bytes 1572872 | tf_op jit(solution)/shard_map/ppermute | solution.py:23
  70.5 24.1 %collective-permute-start.10 = (bf16[16,128,128]{2,1,0:T(8,128)(2,1)S(1)}, bf16[16,128,128]{2,1,0:T(8,128)(2,1)S(1)}, u32[]{:S(2)}, u32[]{:S(2)}) collective-permute-start(bf16[16,128,128]{2,1,0:T(8,128)(2,1)S(1)} %get-tuple-element.67.refs_4_), channel_id=1, source_target_pairs={{16,0},{17,1},{18,2},{19,3},{20,4},{21,5},{22,6},{23,7},{24,8},{25... | collective-permute-start | bytes 1572872 | tf_op jit(solution)/shard_map/ppermute | solution.py:23
  73.9 20.7 %collective-permute-start.9 = (bf16[16,128,128]{2,1,0:T(8,128)(2,1)S(1)}, bf16[16,128,128]{2,1,0:T(8,128)(2,1)S(1)}, u32[]{:S(2)}, u32[]{:S(2)}) collective-permute-start(bf16[16,128,128]{2,1,0:T(8,128)(2,1)S(1)} %get-tuple-element.68.refs_0_), channel_id=1, source_target_pairs={{48,0},{49,1},{50,2},{51,3},{52,4},{53,5},{54,6},{55,7},{56,8},{57... | collective-permute-start | bytes 1572872 | tf_op jit(solution)/shard_map/ppermute | solution.py:23
  78.2 21.3 %collective-permute-start.12 = (bf16[16,128,128]{2,1,0:T(8,128)(2,1)S(1)}, bf16[16,128,128]{2,1,0:T(8,128)(2,1)}, u32[]{:S(2)}, u32[]{:S(2)}) collective-permute-start(bf16[16,128,128]{2,1,0:T(8,128)(2,1)S(1)} %collective-permute-done.11.refs_7_), channel_id=1, source_target_pairs={{48,0},{49,1},{50,2},{51,3},{52,4},{53,5},{54,6},{55,7},{56,8},{57... | collective-permute-start | bytes 1572872 | tf_op jit(solution)/shard_map/ppermute | solution.py:23
  83.4 18.0 %collective-permute-start.8 = (bf16[16,128,128]{2,1,0:T(8,128)(2,1)S(1)}, bf16[16,128,128]{2,1,0:T(8,128)(2,1)}, u32[]{:S(2)}, u32[]{:S(2)}) collective-permute-start(bf16[16,128,128]{2,1,0:T(8,128)(2,1)S(1)} %collective-permute-done.7.refs_1_), channel_id=1, source_target_pairs={{16,0},{17,1},{18,2},{19,3},{20,4},{21,5},{22,6},{23,7},{24,8},{25... | collective-permute-start | bytes 1572872 | tf_op jit(solution)/shard_map/ppermute | solution.py:23
  106.3 27.4 %all-to-all-start = ((bf16[64,8,128]{2,1,0:T(8,128)(2,1)}), bf16[64,8,128]{2,1,0:T(8,128)(2,1)S(1)}, u32[]{:S(2)}, u32[]{:S(2)}) async-start(bf16[64,8,128]{2,1,0:T(8,128)(2,1)} %bitcast.23), calls=%async_computation | async-start | bytes 262144 | tf_op jit(solution)/shard_map/all_to_all | solution.py:291
  165.8 35.3 %all-to-all-start.2 = ((bf16[8,2,8,64,128]{4,3,2,1,0:T(8,128)(2,1)}), bf16[8,2,8,64,128]{4,3,2,1,0:T(8,128)(2,1)S(1)}, u32[]{:S(2)}, u32[]{:S(2)}) async-start(bf16[8,2,8,64,128]{4,3,2,1,0:T(8,128)(2,1)} %get-tuple-element.31), calls=%async_computation.2 | async-start | bytes 4194304 | tf_op jit(solution)/shard_map/all_to_all | solution.py:321
  170.6 61.5 %all-gather.7.cloned.1.call-start = ((), (), s32[]{:S(2)}) async-start(), calls=%async_computation.5 | async-start | bytes 1310720 | tf_op jit(solution)/shard_map/all_gather | solution.py:333
  174.3 17.1 %collective-permute-start.13 = (bf16[16,128,128]{2,1,0:T(8,128)(2,1)S(1)}, bf16[16,128,128]{2,1,0:T(8,128)(2,1)S(1)}, u32[]{:S(2)}, u32[]{:S(2)}) collective-permute-start(bf16[16,128,128]{2,1,0:T(8,128)(2,1)S(1)} %get-tuple-element.29), channel_id=1, source_target_pairs={{48,0},{49,1},{50,2},{51,3},{52,4},{53,5},{54,6},{55,7},{56,8},{57... | collective-permute-start | bytes 1572872 | tf_op jit(solution)/shard_map/ppermute | solution.py:23
  176.9 15.6 %collective-permute-start.15 = (bf16[16,128,128]{2,1,0:T(8,128)(2,1)S(1)}, bf16[16,128,128]{2,1,0:T(8,128)(2,1)S(1)}, u32[]{:S(2)}, u32[]{:S(2)}) collective-permute-start(bf16[16,128,128]{2,1,0:T(8,128)(2,1)S(1)} %get-tuple-element.30), channel_id=1, source_target_pairs={{16,0},{17,1},{18,2},{19,3},{20,4},{21,5},{22,6},{23,7},{24,8},{25... | collective-permute-start | bytes 1572872 | tf_op jit(solution)/shard_map/ppermute | solution.py:23
  193.5 11.4 %collective-permute-start.14 = (bf16[8,128,128]{2,1,0:T(8,128)(2,1)}, bf16[8,128,128]{2,1,0:T(8,128)(2,1)}, u32[]{:S(2)}, u32[]{:S(2)}) collective-permute-start(bf16[8,128,128]{2,1,0:T(8,128)(2,1)} %get-tuple-element.50), channel_id=1, source_target_pairs={{48,0},{49,1},{50,2},{51,3},{52,4},{53,5},{54,6},{55,7},{56,8},{57... | collective-permute-start | bytes 786440 | tf_op jit(solution)/shard_map/ppermute | solution.py:23
  196.8 9.2 %collective-permute-start.16 = (bf16[8,128,128]{2,1,0:T(8,128)(2,1)}, bf16[8,128,128]{2,1,0:T(8,128)(2,1)}, u32[]{:S(2)}, u32[]{:S(2)}) collective-permute-start(bf16[8,128,128]{2,1,0:T(8,128)(2,1)} %get-tuple-element.49), channel_id=1, source_target_pairs={{16,0},{17,1},{18,2},{19,3},{20,4},{21,5},{22,6},{23,7},{24,8},{25... | collective-permute-start | bytes 786440 | tf_op jit(solution)/shard_map/ppermute | solution.py:23
  208.2 30.1 %all-to-all-start.3 = ((bf16[16,128,128]{2,1,0:T(8,128)(2,1)}), bf16[16,128,128]{2,1,0:T(8,128)(2,1)S(1)}, u32[]{:S(2)}, u32[]{:S(2)}) async-start(bf16[16,128,128]{2,1,0:T(8,128)(2,1)} %pad_maximum_fusion), calls=%async_computation.3 | async-start | bytes 1048576 | tf_op jit(solution)/shard_map/all_to_all | solution.py:332
  232.1 6.3 %collective-permute-start.17 = (bf16[4,2,16,4096]{3,2,1,0:T(8,128)(2,1)}, bf16[4,2,16,4096]{3,2,1,0:T(8,128)(2,1)S(1)}, u32[]{:S(2)}, u32[]{:S(2)}) collective-permute-start(bf16[4,2,16,4096]{3,2,1,0:T(8,128)(2,1)} %bitcast.107), channel_id=1, source_target_pairs={{64,0},{0,64},{192,128},{128,192},{320,256},{256,320},{448,384},{3... | collective-permute-start | bytes 3145736 | tf_op jit(solution)/shard_map/ppermute | solution.py:27
  (15 other events, 401.2 us)
Sparse Core Ops, SparseCore 0:
  41.9 24.1 all-gather.4
  208.4 23.6 all-gather.6
